TPU v7x, 32 devices: a whole 2x2x4 slice. The times are simulated.
32 devices in a mesh: clip: 8 (over z, x), band: 4 (over y, core).
Axes of the slice: x: 2, y: 2, z: 4, core: 2. Of those that a mesh axis runs over, the one named last changes fastest.
Arguments:
- pixels: bfloat16 [98304, 256], P(('clip', 'band')), may hold values from -6 to 6
- lengths: int32 [32, 6], P(('clip', 'band')), may hold values from 0 to 1536, as said below
- shifts: int32 [32, 6, 2], P(('clip', 'band')), may hold values from 0 to 3
- visible: int32 [18432], P(('clip', 'band')), may hold values from 0 to 3071, as said below
- patch_embed: float32 [256, 768], P('clip'), may hold values from -0.375 to 0.375
- encoder_in: float32 [768, 6656], P('clip'), may hold values from -0.21875 to 0.21875
- encoder_down: float32 [3072, 768], P('clip'), may hold values from -0.109375 to 0.109375
- decoder_in: float32 [512, 4352], P('clip'), may hold values from -0.25 to 0.25
- decoder_down: float32 [2048, 512], P('clip'), may hold values from -0.125 to 0.125
- norm_vectors: float32 [8192], P('clip')
- first_embed: float32 [256, 768], P('clip'), may hold values from -4.7683716e-07 to 4.7683716e-07
- first_encoder_in: float32 [768, 6656], P('clip'), may hold values from -4.7683716e-07 to 4.7683716e-07
- first_encoder_down: float32 [3072, 768], P('clip'), may hold values from -4.7683716e-07 to 4.7683716e-07
- first_decoder_in: float32 [512, 4352], P('clip'), may hold values from -4.7683716e-07 to 4.7683716e-07
- first_decoder_down: float32 [2048, 512], P('clip'), may hold values from -4.7683716e-07 to 4.7683716e-07
- first_vectors: float32 [8192], P('clip'), may hold values from -2.3841858e-06 to 2.3841858e-06
- second_embed: float32 [256, 768], P('clip'), may hold values from 4.802467e-15 to 1.9173348e-14
- second_encoder_in: float32 [768, 6656], P('clip'), may hold values from 4.802467e-15 to 1.9173348e-14
- second_encoder_down: float32 [3072, 768], P('clip'), may hold values from 4.802467e-15 to 1.9173348e-14
- second_decoder_in: float32 [512, 4352], P('clip'), may hold values from 4.802467e-15 to 1.9173348e-14
- second_decoder_down: float32 [2048, 512], P('clip'), may hold values from 4.802467e-15 to 1.9173348e-14
- second_vectors: float32 [8192], P('clip'), may hold values from 1.1869215e-13 to 4.747686e-13
Outputs:
- loss_sum: float32 [], replicated
- grad_norm: float32 [], replicated
- updated_embed: float32 [256, 768], P('clip')
- updated_encoder_in: float32 [768, 6656], P('clip')
- updated_encoder_down: float32 [3072, 768], P('clip')
- updated_decoder_in: float32 [512, 4352], P('clip')
- updated_decoder_down: float32 [2048, 512], P('clip')
- updated_vectors: float32 [8192], P('clip')
- moment_embed: float32 [256, 768], P('clip')
- moment_encoder_in: float32 [768, 6656], P('clip')
- moment_encoder_down: float32 [3072, 768], P('clip')
- moment_decoder_in: float32 [512, 4352], P('clip')
- moment_decoder_down: float32 [2048, 512], P('clip')
- moment_vectors: float32 [8192], P('clip')
- square_embed: float32 [256, 768], P('clip')
- square_encoder_in: float32 [768, 6656], P('clip')
- square_encoder_down: float32 [3072, 768], P('clip')
- square_decoder_in: float32 [512, 4352], P('clip')
- square_decoder_down: float32 [2048, 512], P('clip')
- square_vectors: float32 [8192], P('clip')
Inputs may be any that keep to these rules, and one draw needn't show every extreme that they name: `lengths`: each row lists its clips first, each 512 or 1536 patches, then zero slots; every row sums to 3072; some row holds 2 clips of 1536 patches. Each pack's 576 entries rise; exactly three patches are visible in each aligned block of 16 patches (two time columns).
All inputs are finite; a program needn't handle non-finite values.
Results may differ from a plain program's by a relative error of at most 0.0003.
The roundings to bfloat16 on the way count: a program that leaves them out, or rounds other values in their place, can miss the bound.
Values may be sent and summed in bfloat16 or wider, within the bound.
A program may use at most 448 MiB of HBM per device.

v0:
```python
import jax
import jax.numpy as jnp
from jax import lax
from jax.sharding import PartitionSpec as P

HEADS_ENC = 12
HEADS_DEC = 16
STEP = 10


LEARN_RATE = 0.02
BETA_ONE = 0.9
BETA_TWO = 0.95
EPSILON = 1e-08
DECAY_RATE = 0.05
CLIP_LIMIT = 0.001


def layer_norm(stream, gain, offset):
    centre = stream - jnp.mean(stream, axis=-1, keepdims=True)
    spread = jnp.mean(centre * centre, axis=-1, keepdims=True)
    return centre * lax.rsqrt(spread + 1e-06) * gain + offset


def sincos(time_pos, frequency, width):
    quarter = width // 4
    omega = 1.0 / 10000.0 ** (jnp.arange(quarter, dtype=jnp.float32) / quarter)
    time_angle = time_pos.astype(jnp.float32)[:, None] * omega[None, :]
    band_angle = frequency.astype(jnp.float32)[:, None] * omega[None, :]
    return jnp.concatenate(
        [jnp.sin(time_angle), jnp.cos(time_angle), jnp.sin(band_angle), jnp.cos(band_angle)], axis=1
    )


def layout(clip_lengths, clip_shifts, patch_dev):
    columns = clip_lengths // 8
    clip_ends = jnp.cumsum(columns)
    starts = clip_ends - columns
    windows = columns // 8
    offsets = jnp.cumsum(windows) - windows
    patches = jnp.arange(patch_dev, dtype=jnp.int32)
    column = patches // 8
    frequency = patches % 8
    clip_id = jnp.sum((column[:, None] >= clip_ends[None, :]).astype(jnp.int32), axis=1)
    onehot = (
        clip_id[:, None] == jnp.arange(clip_lengths.shape[0], dtype=jnp.int32)[None, :]
    ).astype(jnp.int32)

    def select(values):
        return jnp.sum(onehot * values[None, :], axis=1)

    time_pos = column - select(starts)
    turned_time = (time_pos + select(clip_shifts[:, 0])) % select(columns)
    turned_band = (frequency + select(clip_shifts[:, 1])) % 8
    target_band = turned_band // 4 * 2 + turned_time // 4 % 2
    dest_row = (
        target_band * (patch_dev // 4)
        + (select(offsets) + turned_time // 8) * 16
        + turned_time % 4 * 4
        + turned_band % 4
    )
    return (time_pos, frequency, clip_id, dest_row)


def product(values_in, weights_in):
    return jnp.dot(values_in, weights_in, preferred_element_type=jnp.float32)


def input_grad(grad_low, weights_in):
    return lax.dot_general(
        grad_low, weights_in, (((1,), (1,)), ((), ())), preferred_element_type=jnp.float32
    )


def weight_grad(values_in, grad_low):
    return lax.dot_general(
        values_in, grad_low, (((0,), (0,)), ((), ())), preferred_element_type=jnp.float32
    )


def split_heads(projections, heads, group):
    rows = projections.shape[0]
    head_size = projections.shape[1] // (3 * heads)
    split_parts = projections.reshape(rows // group, group, 3, heads, head_size)
    return (split_parts[:, :, 0], split_parts[:, :, 1], split_parts[:, :, 2], head_size)


def softmax_probs(query, key_rows, head_size, score_bias):
    scores = jnp.einsum("bqhd,bkhd->bhqk", query, key_rows, preferred_element_type=jnp.float32)
    return jax.nn.softmax(scores * head_size ** (-0.5) + score_bias, axis=-1)


def attend(projections, heads, group, score_bias):
    query, key_rows, value_rows, head_size = split_heads(projections, heads, group)
    probs = softmax_probs(query, key_rows, head_size, score_bias)
    mixed = jnp.einsum(
        "bhqk,bkhd->bqhd",
        probs.astype(jnp.bfloat16),
        value_rows,
        preferred_element_type=jnp.float32,
    )
    return mixed.reshape(projections.shape[0], -1)


def attend_back(grad_mixed, projections, heads, group, score_bias):
    query, key_rows, value_rows, head_size = split_heads(projections, heads, group)
    probs = softmax_probs(query, key_rows, head_size, score_bias)
    grad_heads = grad_mixed.reshape(query.shape)
    grad_probs = jnp.einsum(
        "bqhd,bkhd->bhqk", grad_heads, value_rows, preferred_element_type=jnp.float32
    )
    grad_values = jnp.einsum(
        "bhqk,bqhd->bkhd",
        probs.astype(jnp.bfloat16),
        grad_heads,
        preferred_element_type=jnp.float32,
    )
    grad_scores = probs * (grad_probs - jnp.sum(grad_probs * probs, axis=-1, keepdims=True))
    scaled = (grad_scores * head_size ** (-0.5)).astype(jnp.bfloat16)
    grad_query = jnp.einsum("bhqk,bkhd->bqhd", scaled, key_rows, preferred_element_type=jnp.float32)
    grad_keys = jnp.einsum("bhqk,bqhd->bkhd", scaled, query, preferred_element_type=jnp.float32)
    return jnp.stack([grad_query, grad_keys, grad_values], axis=2).reshape(projections.shape[0], -1)


def block_forward(stream, weights, gains, heads, group, score_bias):
    w_qkv, w_out, w_up, w_down = weights
    normed = layer_norm(stream, gains[0], gains[1]).astype(jnp.bfloat16)
    projections = product(normed, w_qkv).astype(jnp.bfloat16)
    attended = attend(projections, heads, group, score_bias).astype(jnp.bfloat16)
    middle = stream + product(attended, w_out)
    second_normed = layer_norm(middle, gains[2], gains[3]).astype(jnp.bfloat16)
    up_values = product(second_normed, w_up)
    activated = jax.nn.gelu(up_values).astype(jnp.bfloat16)
    return (
        middle + product(activated, w_down),
        (stream, normed, projections, attended, middle, second_normed, up_values, activated),
    )


def block_backward(grad_out, cache, weights, gains, heads, group, score_bias):
    w_qkv, w_out, w_up, w_down = weights
    stream, normed, projections, attended, middle, second_normed, up_values, activated = cache
    grad_down = grad_out.astype(jnp.bfloat16)
    g_down = weight_grad(activated, grad_down)
    _, gelu_back = jax.vjp(jax.nn.gelu, up_values)
    grad_up = gelu_back(input_grad(grad_down, w_down))[0].astype(jnp.bfloat16)
    g_up = weight_grad(second_normed, grad_up)
    _, norm_back = jax.vjp(layer_norm, middle, gains[2], gains[3])
    grad_middle, g_gain_two, g_offset_two = norm_back(input_grad(grad_up, w_up))
    grad_middle = grad_middle + grad_out
    grad_branch = grad_middle.astype(jnp.bfloat16)
    g_out = weight_grad(attended, grad_branch)
    grad_attended = input_grad(grad_branch, w_out).astype(jnp.bfloat16)
    grad_projections = attend_back(grad_attended, projections, heads, group, score_bias).astype(
        jnp.bfloat16
    )
    g_qkv = weight_grad(normed, grad_projections)
    _, first_back = jax.vjp(layer_norm, stream, gains[0], gains[1])
    grad_stream, g_gain_one, g_offset_one = first_back(input_grad(grad_projections, w_qkv))
    norm_grads = jnp.stack([g_gain_one, g_offset_one, g_gain_two, g_offset_two])
    return (grad_stream + grad_middle, (g_qkv, g_out, g_up, g_down), norm_grads)


def adam_update(weight, first, second, grad, decay):
    first = BETA_ONE * first + (1.0 - BETA_ONE) * grad
    second = BETA_TWO * second + (1.0 - BETA_TWO) * grad * grad
    first_hat = first / (1.0 - BETA_ONE**STEP)
    second_hat = second / (1.0 - BETA_TWO**STEP)
    weight = weight - LEARN_RATE * (first_hat / (jnp.sqrt(second_hat) + EPSILON) + decay * weight)
    return (weight, first, second)


def shards(
    pixels,
    lengths,
    shifts,
    visible,
    patch_embed,
    encoder_in,
    encoder_down,
    decoder_in,
    decoder_down,
    norm_vectors,
    first_embed,
    first_encoder_in,
    first_encoder_down,
    first_decoder_in,
    first_decoder_down,
    first_vectors,
    second_embed,
    second_encoder_in,
    second_encoder_down,
    second_decoder_in,
    second_decoder_down,
    second_vectors,
):
    masters = (patch_embed, encoder_in, encoder_down, decoder_in, decoder_down, norm_vectors)
    firsts = (
        first_embed,
        first_encoder_in,
        first_encoder_down,
        first_decoder_in,
        first_decoder_down,
        first_vectors,
    )
    seconds = (
        second_embed,
        second_encoder_in,
        second_encoder_down,
        second_decoder_in,
        second_decoder_down,
        second_vectors,
    )
    w_embed, w_enc, w_enc_down, w_dec, w_dec_down, gathered_vectors = (
        lax.all_gather(patch_embed.astype(jnp.bfloat16), "clip", axis=0, tiled=True),
        lax.all_gather(encoder_in.astype(jnp.bfloat16), "clip", axis=0, tiled=True),
        lax.all_gather(encoder_down.astype(jnp.bfloat16), "clip", axis=0, tiled=True),
        lax.all_gather(decoder_in.astype(jnp.bfloat16), "clip", axis=0, tiled=True),
        lax.all_gather(decoder_down.astype(jnp.bfloat16), "clip", axis=0, tiled=True),
        lax.all_gather(norm_vectors.astype(jnp.bfloat16), "clip", axis=0, tiled=True),
    )
    enc_width, dec_width = (w_enc.shape[0], w_dec.shape[0])
    enc_hidden, dec_hidden = (w_enc_down.shape[0], w_dec_down.shape[0])
    vectors = gathered_vectors.astype(jnp.float32)
    enc_gains = vectors[: 6 * enc_width].reshape(6, enc_width)
    dec_gains = vectors[6 * enc_width :].reshape(7, dec_width)
    enc_weights = (
        w_enc[:, : 3 * enc_width],
        w_enc[:, 3 * enc_width : 4 * enc_width],
        w_enc[:, 4 * enc_width : 4 * enc_width + enc_hidden],
        w_enc_down,
    )
    w_proj = w_enc[:, 4 * enc_width + enc_hidden :]
    dec_weights = (
        w_dec[:, : 3 * dec_width],
        w_dec[:, 3 * dec_width : 4 * dec_width],
        w_dec[:, 4 * dec_width : 4 * dec_width + dec_hidden],
        w_dec_down,
    )
    w_head = w_dec[:, 4 * dec_width + dec_hidden :]
    patch_dev = pixels.shape[0]
    time_pos, frequency, clip_id, dest_row = layout(lengths[0], shifts[0], patch_dev)
    source = (
        jnp.zeros((patch_dev,), jnp.int32).at[dest_row].set(jnp.arange(patch_dev, dtype=jnp.int32))
    )
    seen = pixels[visible]
    segment = clip_id[visible]
    score_bias = jnp.where(segment[:, None] == segment[None, :], 0.0, -1e30)
    embedded = product(seen, w_embed) + sincos(time_pos[visible], frequency[visible], enc_width)
    encoded, enc_cache = block_forward(
        embedded, enc_weights, enc_gains, HEADS_ENC, seen.shape[0], score_bias
    )
    final_enc = layer_norm(encoded, enc_gains[4], enc_gains[5]).astype(jnp.bfloat16)
    projected = product(final_enc, w_proj)
    kept_mask = jnp.zeros((patch_dev,), jnp.float32).at[visible].set(1.0)
    placed = jnp.zeros((patch_dev, dec_width), jnp.float32).at[visible].set(projected)
    grid = jnp.where(kept_mask[:, None] > 0.5, placed, dec_gains[6][None, :]) + sincos(
        time_pos, frequency, dec_width
    )
    pixel_float = pixels.astype(jnp.float32)
    centre = pixel_float - jnp.mean(pixel_float, axis=1, keepdims=True)
    target = (centre * lax.rsqrt(jnp.mean(centre * centre, axis=1, keepdims=True) + 1e-06)).astype(
        jnp.bfloat16
    )
    grid_rows = grid.astype(jnp.bfloat16)[source]
    target_rows = target[source]
    masked_rows = (1.0 - kept_mask).astype(jnp.bfloat16)[source]
    grid_rows, target_rows, masked_rows = (
        lax.all_to_all(grid_rows, "band", split_axis=0, concat_axis=0, tiled=True),
        lax.all_to_all(target_rows, "band", split_axis=0, concat_axis=0, tiled=True),
        lax.all_to_all(masked_rows, "band", split_axis=0, concat_axis=0, tiled=True),
    )
    decoded, dec_cache = block_forward(
        grid_rows.astype(jnp.float32), dec_weights, dec_gains, HEADS_DEC, 16, 0.0
    )
    final_dec = layer_norm(decoded, dec_gains[4], dec_gains[5]).astype(jnp.bfloat16)
    predicted = product(final_dec, w_head)
    error = predicted - target_rows.astype(jnp.float32)
    row_weight = masked_rows.astype(jnp.float32)
    local_loss = jnp.sum(row_weight * jnp.mean(error * error, axis=1))
    masked_count = 13.0 * (patch_dev // 16) * lax.axis_size("clip") * lax.axis_size("band")
    grad_pred = (row_weight[:, None] * error * (2.0 / (error.shape[1] * masked_count))).astype(
        jnp.bfloat16
    )
    g_head = weight_grad(final_dec, grad_pred)
    _, dec_final_back = jax.vjp(layer_norm, decoded, dec_gains[4], dec_gains[5])
    grad_decoded, g_dec_gain, g_dec_offset = dec_final_back(input_grad(grad_pred, w_head))
    grad_grid, g_dec_mats, g_dec_norms = block_backward(
        grad_decoded, dec_cache, dec_weights, dec_gains, HEADS_DEC, 16, 0.0
    )
    grad_grid = grad_grid.astype(jnp.bfloat16)
    grad_grid = lax.all_to_all(grad_grid, "band", split_axis=0, concat_axis=0, tiled=True)
    grad_patch = grad_grid[dest_row]
    g_token = jnp.sum((1.0 - kept_mask)[:, None] * grad_patch.astype(jnp.float32), axis=0)
    grad_proj = grad_patch[visible]
    g_proj = weight_grad(final_enc, grad_proj)
    _, enc_final_back = jax.vjp(layer_norm, encoded, enc_gains[4], enc_gains[5])
    grad_encoded, g_enc_gain, g_enc_offset = enc_final_back(input_grad(grad_proj, w_proj))
    grad_embedded, g_enc_mats, g_enc_norms = block_backward(
        grad_encoded, enc_cache, enc_weights, enc_gains, HEADS_ENC, seen.shape[0], score_bias
    )
    g_embed = weight_grad(seen, grad_embedded.astype(jnp.bfloat16))
    g_enc_in = jnp.concatenate([g_enc_mats[0], g_enc_mats[1], g_enc_mats[2], g_proj], axis=1)
    g_dec_in = jnp.concatenate([g_dec_mats[0], g_dec_mats[1], g_dec_mats[2], g_head], axis=1)
    g_vectors = jnp.concatenate(
        [
            g_enc_norms.reshape(-1),
            g_enc_gain,
            g_enc_offset,
            g_dec_norms.reshape(-1),
            g_dec_gain,
            g_dec_offset,
            g_token,
        ]
    )
    shard_grads = (
        lax.psum_scatter(g_embed, "clip", scatter_dimension=0, tiled=True),
        lax.psum_scatter(g_enc_in, "clip", scatter_dimension=0, tiled=True),
        lax.psum_scatter(g_enc_mats[3], "clip", scatter_dimension=0, tiled=True),
        lax.psum_scatter(g_dec_in, "clip", scatter_dimension=0, tiled=True),
        lax.psum_scatter(g_dec_mats[3], "clip", scatter_dimension=0, tiled=True),
        lax.psum_scatter(g_vectors, "clip", scatter_dimension=0, tiled=True),
    )
    reduced = lax.psum(
        (
            shard_grads[0],
            shard_grads[1],
            shard_grads[2],
            shard_grads[3],
            shard_grads[4],
            shard_grads[5],
        ),
        "band",
    )
    squares = jnp.zeros((), jnp.float32)
    for grad in reduced:
        squares = squares + jnp.sum(grad * grad)
    loss_sum = lax.psum(local_loss, ("clip", "band"))
    norm_squared = lax.psum(squares, "clip")
    grad_norm = jnp.sqrt(norm_squared)
    factor = jnp.minimum(1.0, CLIP_LIMIT / (grad_norm + 1e-06))
    results = []
    for index in range(6):
        decay = DECAY_RATE if index < 5 else 0.0
        results.append(
            adam_update(
                masters[index], firsts[index], seconds[index], reduced[index] * factor, decay
            )
        )
    return (
        loss_sum,
        grad_norm,
        results[0][0],
        results[1][0],
        results[2][0],
        results[3][0],
        results[4][0],
        results[5][0],
        results[0][1],
        results[1][1],
        results[2][1],
        results[3][1],
        results[4][1],
        results[5][1],
        results[0][2],
        results[1][2],
        results[2][2],
        results[3][2],
        results[4][2],
        results[5][2],
    )


def solution(mesh):
    in_specs = (
        P(("clip", "band"), None),
        P(("clip", "band"), None),
        P(("clip", "band"), None, None),
        P(("clip", "band")),
        P("clip", None),
        P("clip", None),
        P("clip", None),
        P("clip", None),
        P("clip", None),
        P("clip"),
        P("clip", None),
        P("clip", None),
        P("clip", None),
        P("clip", None),
        P("clip", None),
        P("clip"),
        P("clip", None),
        P("clip", None),
        P("clip", None),
        P("clip", None),
        P("clip", None),
        P("clip"),
    )
    out_specs = (
        P(),
        P(),
        P("clip", None),
        P("clip", None),
        P("clip", None),
        P("clip", None),
        P("clip", None),
        P("clip"),
        P("clip", None),
        P("clip", None),
        P("clip", None),
        P("clip", None),
        P("clip", None),
        P("clip"),
        P("clip", None),
        P("clip", None),
        P("clip", None),
        P("clip", None),
        P("clip", None),
        P("clip"),
    )
    return jax.shard_map(shards, mesh=mesh, in_specs=in_specs, out_specs=out_specs, check_vma=False)
```

profile of v0, /device:TPU:0, one launch (start us, length us, event | category | flops | bytes accessed | tf_op | source)
XLA Modules:
  0.0 2116.6 jit_solution(4484206498462612302)
XLA Ops:
  58.7 27.7 %all_gather.19 = bf16[8192]{0:T(1024)(128)(2,1)S(1)} all-gather(bf16[1024]{0:T(1024)(128)(2,1)S(1)} %convert_element_type.228), channel_id=1, replica_groups=mesh['clip'=8,'band'=4] {'clip'}, dimensions={0}, use_global_device_ids=true | all-gather | bytes 18432 | tf_op jit(solution)/shard_map/all_gather | solution.py:220
  103.7 34.7 %all_gather.18 = bf16[256,768]{1,0:T(8,128)(2,1)} all-gather(bf16[32,768]{1,0:T(8,128)(2,1)S(1)} %convert_element_type.225), channel_id=1, replica_groups=mesh['clip'=8,'band'=4] {'clip'}, dimensions={0}, use_global_device_ids=true | all-gather | bytes 442368 | tf_op jit(solution)/shard_map/all_gather | solution.py:215
  214.6 35.0 %all-gather.7.cloned.1.call-done = bf16[3072,768]{1,0:T(8,128)(2,1)} async-done(((bf16[384,768]{1,0:T(8,128)(2,1)}), bf16[3072,768]{1,0:T(8,128)(2,1)}) %all-gather.7.cloned.1.call-update) | async-done | bytes 4718608 | tf_op jit(solution)/shard_map/all_gather | solution.py:217
  304.3 29.9 %all-to-all-done.1 = bf16[4,768,512]{2,1,0:T(8,128)(2,1)S(1)} async-done(((bf16[4,768,512]{2,1,0:T(8,128)(2,1)}), bf16[4,768,512]{2,1,0:T(8,128)(2,1)S(1)}, u32[]{:S(2)}, u32[]{:S(2)}) %all-to-all-start.1) | async-done | bytes 3145760 | tf_op jit(solution)/shard_map/all_to_all | solution.py:269
  349.7 41.1 %reshape.987 = bf16[192,16,3,16,32]{4,3,2,1,0:T(8,128)(2,1)} reshape(bf16[3072,1536]{1,0:T(8,128)(2,1)} %convolution_convert_fusion) | data formatting | bytes 18874368 | tf_op jit(solution)/shard_map/reshape | solution.py:84
  390.8 26.3 %fusion.214 = (bf16[192,16,1,16,32]{4,3,2,1,0:T(8,128)(2,1)}, bf16[192,16,1,16,32]{4,3,2,1,0:T(8,128)(2,1)}, bf16[192,16,1,16,32]{4,3,2,1,0:T(8,128)(2,1)}) fusion(bf16[192,16,3,16,32]{4,3,2,1,0:T(8,128)(2,1)} %reshape.987), kind=kLoop, calls=%fused_computation.398 | loop fusion | bytes 18874368 | tf_op jit(solution)/shard_map/slice | solution.py:85
  417.1 23.1 %fusion.23 = f32[192,16,16,16]{2,3,1,0:T(8,128)} fusion(bf16[192,16,1,16,32]{4,3,2,1,0:T(8,128)(2,1)} %get-tuple-element.79, bf16[192,16,1,16,32]{4,3,2,1,0:T(8,128)(2,1)} %get-tuple-element.78), kind=kOutput, calls=%fused_computation.50 | convolution fusion | flops 50331648 | bytes 9437184 | tf_op jit(solution)/shard_map/bqhd,bkhd->bhqk/dot_general | solution.py:89
  440.3 33.1 %fusion.221 = (f32[192,16,16]{2,1,0:T(8,128)}, f32[192,16,16,16]{2,3,1,0:T(8,128)}) fusion(f32[192,16,16,16]{2,3,1,0:T(8,128)} %fusion.23), kind=kOutput, calls=%fused_computation.405 | output fusion | flops 3145743 | bytes 6488064 | tf_op jit(solution)/shard_map/sub | solution.py:90
  575.6 26.5 %fusion.10 = bf16[3072,2048]{1,0:T(8,128)(2,1)} fusion(f32[3072,2048]{1,0:T(8,128)} %get-tuple-element.127, bf16[2048,512]{1,0:T(8,128)(2,1)} %all-gather.11.cloned.1.call-done, f32[3072,512]{1,0:T(8,128)} %get-tuple-element.75, f32[3072]{0:T(1024)S(1)} %negate_multiply_fusion.2), kind=kOutput, calls=%fused_computation.24 | convolution fusion | flops 6571425792 | bytes 46149632 | tf_op jit(solution)/shard_map/dot_general | solution.py:70
  633.9 24.1 %fusion.20 = f32[192,16,16,16]{2,3,1,0:T(8,128)} fusion(bf16[192,16,1,16,32]{4,3,2,1,0:T(8,128)(2,1)} %get-tuple-element.80, bf16[192,16,16,32]{3,2,1,0:T(8,128)(2,1)} %reshape.988), kind=kOutput, calls=%fused_computation.47 | convolution fusion | flops 50331648 | bytes 9437184 | tf_op jit(solution)/shard_map/bqhd,bkhd->bhqk/dot_general | solution.py:109
  677.3 46.2 %fusion.38 = bf16[192,16,1,16,32]{4,1,3,0,2:T(8,128)(2,1)} fusion(f32[192,16,16,16]{2,3,1,0:T(8,128)} %fusion.20, bf16[192,16,1,16,32]{4,3,2,1,0:T(8,128)(2,1)} %get-tuple-element.78, f32[192,16,16,16]{2,3,1,0:T(8,128)} %get-tuple-element.123, f32[192,16,16]{2,1,0:T(8,128)S(1)} %copy-done.46), kind=kOutput, calls=%fused_computation.65 | convolution fusion | flops 55885840 | bytes 12779520 | tf_op jit(solution)/shard_map/bhqk,bkhd->bqhd/dot_general | solution.py:120
  723.5 43.5 %fusion.41 = bf16[192,16,1,16,32]{4,1,3,0,2:T(8,128)(2,1)} fusion(bf16[192,16,1,16,32]{4,3,2,1,0:T(8,128)(2,1)} %get-tuple-element.79, f32[192,16,16,16]{2,3,1,0:T(8,128)} %fusion.20, f32[192,16,16,16]{2,3,1,0:T(8,128)} %get-tuple-element.123, f32[192,16,16]{2,1,0:T(8,128)S(1)} %copy-done.46), kind=kOutput, calls=%fused_computation.66 | convolution fusion | flops 55885840 | bytes 12779520 | tf_op jit(solution)/shard_map/bhqk,bqhd->bkhd/dot_general | solution.py:121
  819.6 32.2 %copy.126 = bf16[192,16,3,16,32]{4,3,2,1,0:T(8,128)(2,1)} copy(bf16[192,16,3,16,32]{0,4,3,2,1:T(8,128)(2,1)} %maximum_convert_fusion) | data formatting | bytes 18874368 | tf_op jit(solution)/shard_map/convert_element_type | solution.py:154
  851.8 48.3 %convert_element_type.272 = bf16[3072,1536]{1,0:T(8,128)(2,1)} reshape(bf16[192,16,3,16,32]{4,3,2,1,0:T(8,128)(2,1)} %copy.126) | data formatting | bytes 18874368 | tf_op jit(solution)/shard_map/convert_element_type | solution.py:154
  924.2 36.8 %all-to-all-done.3 = bf16[4,768,512]{2,1,0:T(8,128)(2,1)S(1)} async-done(((bf16[4,768,512]{2,1,0:T(8,128)(2,1)}), bf16[4,768,512]{2,1,0:T(8,128)(2,1)S(1)}, u32[]{:S(2)}, u32[]{:S(2)}) %all-to-all-start.3) | async-done | bytes 3145760 | tf_op jit(solution)/shard_map/all_to_all | solution.py:292
  1022.9 27.2 %fusion.121 = bf16[1,576,1,12,64]{1,4,3,2,0:T(8,128)(2,1)} fusion(f32[12,576,576]{1,2,0:T(8,128)} %fusion.133, bf16[1,576,3,12,64]{1,4,3,2,0:T(8,128)(2,1)} %bitcast.216, f32[12,576,576]{1,2,0:T(8,128)} %get-tuple-element.117, f32[12,576]{1,0:T(8,128)S(1)} %copy-done.151), kind=kOutput, calls=%fused_computation.189 | convolution fusion | flops 537926976 | bytes 72728576 | tf_op jit(solution)/shard_map/bhqk,bkhd->bqhd/dot_general | solution.py:120
  1050.1 27.8 %fusion.118 = bf16[1,576,1,12,64]{1,4,3,2,0:T(8,128)(2,1)} fusion(f32[12,576,576]{1,2,0:T(8,128)} %fusion.133, bf16[1,576,3,12,64]{1,4,3,2,0:T(8,128)(2,1)} %bitcast.217, f32[12,576,576]{1,2,0:T(8,128)} %get-tuple-element.117, f32[12,576]{1,0:T(8,128)S(1)} %copy-done.151), kind=kOutput, calls=%fused_computation.188 | convolution fusion | flops 537926976 | bytes 72728576 | tf_op jit(solution)/shard_map/bhqk,bqhd->bkhd/dot_general | solution.py:121
  1173.0 68.0 %reduce-scatter.14.cloned.1.call-done = f32[256,512]{1,0:T(8,128)} async-done(((f32[2048,512]{1,0:T(8,128)}), f32[256,512]{1,0:T(8,128)}) %reduce-scatter.14.cloned.1.call-update) | async-done | bytes 524304 | tf_op jit(solution)/shard_map/reduce_scatter | solution.py:321
  1241.0 159.6 %reduce-scatter.12.cloned.1.call-done = f32[64,4352]{1,0:T(8,128)} async-done(((f32[512,4352]{1,0:T(8,128)}), f32[64,4352]{1,0:T(8,128)}) %reduce-scatter.12.cloned.1.call-update) | async-done | bytes 1114128 | tf_op jit(solution)/shard_map/reduce_scatter | solution.py:320
  1400.6 166.2 %reduce-scatter.10.cloned.1.call-done = f32[384,768]{1,0:T(8,128)} async-done(((f32[3072,768]{1,0:T(8,128)}), f32[384,768]{1,0:T(8,128)}) %reduce-scatter.10.cloned.1.call-update) | async-done | bytes 1179664 | tf_op jit(solution)/shard_map/reduce_scatter | solution.py:319
  1566.7 338.4 %reduce-scatter.8.cloned.1.call-done = f32[96,6656]{1,0:T(8,128)} async-done(((f32[768,6656]{1,0:T(8,128)}), f32[96,6656]{1,0:T(8,128)}) %reduce-scatter.8.cloned.1.call-update) | async-done | bytes 2555920 | tf_op jit(solution)/shard_map/reduce_scatter | solution.py:318
  1908.8 35.4 %all-reduce = f32[8192]{0:T(1024)S(1)} all-reduce(f32[8192]{0:T(1024)S(1)} %constant_dynamic-update-slice_fusion), channel_id=7, replica_groups=mesh['clip'=8,'band'=4] {'clip'}, use_global_device_ids=true, to_apply=%region_74.75.clone | all-reduce | flops 8192 | bytes 65536
  1951.3 62.9 %all-reduce.4.cloned.1.call-done = (f32[32,768]{1,0:T(8,128)}, f32[96,6656]{1,0:T(8,128)}, f32[384,768]{1,0:T(8,128)}, f32[64,4352]{1,0:T(8,128)}, f32[256,512]{1,0:T(8,128)}) async-done(((f32[32,768]{1,0:T(8,128)}, f32[96,6656]{1,0:T(8,128)}, f32[384,768]{1,0:T(8,128)}, f32[64,4352]{1,0:T(8,128)}, f32[256,512]{1,0:T(8,128)}), (f32[32,768]{1,0:T(8,128)}, f32[96,6656]{1,0:T(8,128)}, f32[384,768]{1,0:T(8,128)}, ...) | async-done | bytes 5472272 | tf_op jit(solution)/shard_map/psum | solution.py:324
  2028.0 40.0 %psum.56 = f32[]{:T(128)} all-reduce(f32[]{:T(128)} %multiply_reduce_fusion.25), channel_id=1, replica_groups=mesh['clip'=8,'band'=4] {'clip','band'}, use_global_device_ids=true, to_apply=%region_31.32 | all-reduce | flops 1 | bytes 8 | tf_op jit(solution)/shard_map/psum | solution.py:338
  (551 shorter events, 659.1 us)
Async XLA Ops:
  7.2 166.9 %all-gather.5.cloned.1.call-start = ((), (), s32[]{:S(2)}) async-start(), calls=%async_computation.9 | async-start | bytes 11501568 | tf_op jit(solution)/shard_map/all_gather | solution.py:216
  10.3 239.3 %all-gather.7.cloned.1.call-start = ((), (), s32[]{:S(2)}) async-start(), calls=%async_computation.10 | async-start | bytes 5308416 | tf_op jit(solution)/shard_map/all_gather | solution.py:217
  51.2 208.7 %all-to-all-start = ((bf16[4,2,384]{2,1,0:T(2,128)(2,1)}), bf16[4,2,384]{2,1,0:T(2,128)(2,1)}, u32[]{:S(2)}, u32[]{:S(2)}) async-start(bf16[4,2,384]{2,1,0:T(2,128)(2,1)} %reshape.1116), calls=%async_computation | async-start | bytes 12288 | tf_op jit(solution)/shard_map/all_to_all | solution.py:271
  55.4 285.0 %all-gather.9.cloned.1.call-start = ((), (), s32[]{:S(2)}) async-start(), calls=%async_computation.11 | async-start | bytes 5013504 | tf_op jit(solution)/shard_map/all_gather | solution.py:218
  259.8 33.8 %all-to-all-start.2 = ((bf16[4,768,256]{1,2,0:T(8,128)(2,1)}), bf16[4,768,256]{1,2,0:T(8,128)(2,1)}, u32[]{:S(2)}, u32[]{:S(2)}) async-start(bf16[4,768,256]{1,2,0:T(8,128)(2,1)} %copy.118), calls=%async_computation.2 | async-start | bytes 3145728 | tf_op jit(solution)/shard_map/all_to_all | solution.py:270
  293.6 40.6 %all-to-all-start.1 = ((bf16[4,768,512]{2,1,0:T(8,128)(2,1)}), bf16[4,768,512]{2,1,0:T(8,128)(2,1)S(1)}, u32[]{:S(2)}, u32[]{:S(2)}) async-start(bf16[4,768,512]{2,1,0:T(8,128)(2,1)} %bitcast.210), calls=%async_computation.1 | async-start | bytes 6291456 | tf_op jit(solution)/shard_map/all_to_all | solution.py:269
  297.3 250.0 %all-gather.11.cloned.1.call-start = ((), (), s32[]{:S(2)}) async-start(), calls=%async_computation.12 | async-start | bytes 2359296 | tf_op jit(solution)/shard_map/all_gather | solution.py:219
  920.3 40.7 %all-to-all-start.3 = ((bf16[4,768,512]{2,1,0:T(8,128)(2,1)}), bf16[4,768,512]{2,1,0:T(8,128)(2,1)S(1)}, u32[]{:S(2)}, u32[]{:S(2)}) async-start(bf16[4,768,512]{2,1,0:T(8,128)(2,1)} %bitcast.211), calls=%async_computation.3 | async-start | bytes 6291456 | tf_op jit(solution)/shard_map/all_to_all | solution.py:292
  924.1 248.9 %reduce-scatter.6.cloned.1.call-start = ((), (), s32[]{:S(2)}) async-start(), calls=%async_computation.13 | async-start | bytes 884736 | tf_op jit(solution)/shard_map/reduce_scatter | solution.py:317
  1089.4 151.6 %reduce-scatter.14.cloned.1.call-start = ((), (), s32[]{:S(2)}) async-start(), calls=%async_computation.17 | async-start | bytes 4718592 | tf_op jit(solution)/shard_map/reduce_scatter | solution.py:321
  1104.8 295.8 %reduce-scatter.12.cloned.1.call-start = ((), (), s32[]{:S(2)}) async-start(), calls=%async_computation.16 | async-start | bytes 10027008 | tf_op jit(solution)/shard_map/reduce_scatter | solution.py:320
  1139.6 427.1 %reduce-scatter.10.cloned.1.call-start = ((), (), s32[]{:S(2)}) async-start(), calls=%async_computation.15 | async-start | bytes 10616832 | tf_op jit(solution)/shard_map/reduce_scatter | solution.py:319
  1152.7 752.4 %reduce-scatter.8.cloned.1.call-start = ((), (), s32[]{:S(2)}) async-start(), calls=%async_computation.14 | async-start | bytes 23003136 | tf_op jit(solution)/shard_map/reduce_scatter | solution.py:318
  1172.8 734.4 %copy-start.136 = (f32[768]{0:T(1024)S(1)}, f32[768]{0:T(1024)}, u32[]{:S(2)}) copy-start(f32[768]{0:T(1024)} %get-tuple-element.33) | copy-start | bytes 9220
  1172.8 734.4 %copy-start.135 = (f32[768]{0:T(1024)S(1)}, f32[768]{0:T(1024)}, u32[]{:S(2)}) copy-start(f32[768]{0:T(1024)} %get-tuple-element.37) | copy-start | bytes 9220
  1172.8 734.4 %copy-start.138 = (f32[768]{0:T(1024)S(1)}, f32[768]{0:T(1024)}, u32[]{:S(2)}) copy-start(f32[768]{0:T(1024)} %get-tuple-element.31) | copy-start | bytes 9220
  1172.9 734.4 %copy-start.137 = (f32[768]{0:T(1024)S(1)}, f32[768]{0:T(1024)}, u32[]{:S(2)}) copy-start(f32[768]{0:T(1024)} %get-tuple-element.36) | copy-start | bytes 9220
  1172.9 734.4 %copy-start.141 = (f32[768]{0:T(1024)S(1)}, f32[768]{0:T(1024)}, u32[]{:S(2)}) copy-start(f32[768]{0:T(1024)} %get-tuple-element.29) | copy-start | bytes 9220
  1172.9 734.4 %copy-start.140 = (f32[768]{0:T(1024)S(1)}, f32[768]{0:T(1024)}, u32[]{:S(2)}) copy-start(f32[768]{0:T(1024)} %get-tuple-element.35) | copy-start | bytes 9220
  1172.9 734.5 %copy-start.128 = (f32[512]{0:T(512)S(1)}, f32[512]{0:T(512)}, u32[]{:S(2)}) copy-start(f32[512]{0:T(512)} %get-tuple-element.20) | copy-start | bytes 6148
  1172.9 734.5 %copy-start.127 = (f32[512]{0:T(512)S(1)}, f32[512]{0:T(512)}, u32[]{:S(2)}) copy-start(f32[512]{0:T(512)} %get-tuple-element.26) | copy-start | bytes 6148
  1172.9 734.5 %copy-start.6 = (bf16[3072,512]{1,0:T(8,128)(2,1)S(1)}, bf16[3072,512]{1,0:T(8,128)(2,1)}, u32[]{:S(2)}) copy-start(bf16[3072,512]{1,0:T(8,128)(2,1)} %gather_fusion.7) | copy-start | bytes 9437188
  1172.9 734.5 %copy-start.91 = (f32[3072]{0:T(1024)S(1)}, f32[3072]{0:T(1024)}, u32[]{:S(2)}) copy-start(f32[3072]{0:T(1024)} %get-tuple-element.98) | copy-start | bytes 36868
  1172.9 841.3 %all-reduce.4.cloned.1.call-start = ((), (), s32[]{:S(2)}) async-start(), calls=%async_computation.18 | async-start | bytes 10944512 | tf_op jit(solution)/shard_map/psum | solution.py:324
  (151 other events, 8955.0 us)
Sparse Core Ops, SparseCore 0:
  10.8 157.9 all-gather.4
  171.5 78.0 all-gather.6
  252.4 74.7 all-gather.8
  329.7 47.4 all-gather.10
  1089.5 60.6 reduce-scatter.5
  1154.1 86.8 reduce-scatter.13
  1244.6 155.8 reduce-scatter.11
  1404.2 162.5 reduce-scatter.9
  1570.7 334.3 reduce-scatter.7
  1907.9 106.2 all-reduce.3
where the time goes:
time: 2130 us; the launch traced here: 2120 us
  waiting for transfers between devices  897 us (42%)
  matrix products  491 us (23%)
  local copies, waits for them, and re-layouts  360 us (17%)
  blocking collectives  166 us (8%)
  other arithmetic  162 us (8%)
  between operations  23.5 us (1%)
    reduce_scatter x1, waiting for transfers between devices, shards(): lax.psum_scatter(g_enc_in, 'clip', scatter_dimension=0, tiled=True)  338 us
    reduce_scatter x1, waiting for transfers between devices, shards(): lax.psum_scatter(g_enc_mats[3], 'clip', scatter_dimension=0, tiled=True)  166 us
    reduce_scatter x1, waiting for transfers between devices, shards(): lax.psum_scatter(g_dec_in, 'clip', scatter_dimension=0, tiled=True)  160 us
    dot_general x10, matrix products, input_grad(): lax.dot_general(grad_low, weights_in, (((1,), (1,)), ((), ())), preferred...  80.7 us
    convert_element_type x2, local copies, waits for them, and re-layouts, block_backward(): attend_back(grad_attended, projections, heads, group, score_bias)  80.4 us
    dot_general x11, matrix products, product(): return jnp.dot(values_in, weights_in, preferred_element_type=jnp.float32)  76 us
    dot_general x2, matrix products, attend_back(): jnp.einsum('bhqk,bkhd->bqhd', scaled, key_rows, preferred_element_type=jn...  73.4 us
    dot_general x2, matrix products, attend_back(): jnp.einsum('bhqk,bqhd->bkhd', scaled, query, preferred_element_type=jnp.f...  71.3 us
  transfers between devices with their start and end apart: 14, of which 8 were waited for; matrix products, arithmetic and copies ran while one was open for 22% of the time, Pallas kernels for 0%

commit v1 on v0

--- a/solution.py
+++ b/solution.py
@@ -1,6 +1,10 @@
+import functools
+
 import jax
 import jax.numpy as jnp
 from jax import lax
+from jax.experimental import pallas as pl
+from jax.experimental.pallas import tpu as pltpu
 from jax.sharding import PartitionSpec as P
 
 HEADS_ENC = 12
@@ -14,6 +18,258 @@
 EPSILON = 1e-08
 DECAY_RATE = 0.05
 CLIP_LIMIT = 0.001
+
+
+F32, BF16 = jnp.float32, jnp.bfloat16
+GELU_C = 0.7978845608028654
+
+
+def mm(a, b, ca=1, cb=0):
+    return lax.dot_general(a, b, (((ca,), (cb,)), ((), ())), preferred_element_type=F32)
+
+
+def wide(v, n):
+    return jnp.concatenate([v] * (n // 128), axis=1)
+
+
+def loop(n, body, unroll=1):
+    def step(i, carry):
+        for k in range(unroll):
+            body(i * unroll + k)
+        return carry
+    lax.fori_loop(0, n // unroll, step, 0)
+
+
+def fold(v):
+    total = v[:, :128]
+    for i in range(1, v.shape[1] // 128):
+        total = total + v[:, 128 * i : 128 * (i + 1)]
+    return total
+
+
+def decoder_kernel(
+    coef, heads, shift_ref, rvis_ref, gvt_ref, pix_ref, et_ref, ef_ref, vec_ref, w_ref, wt_ref, wd_ref, wdt_ref,
+    gin_ref, gdown_ref, gvec_ref, gp_ref, loss_ref,
+    res, xh1, xh2, xh3, tmp, n1, n2, fin, rs, qkv, att, act, dgel, probs, dqkv, dup, low, oh, mrow, hb, hm, wm,
+):
+    width = w_ref.shape[0]
+    hidden = wd_ref.shape[0]
+    rows = res.shape[1]
+    size = width // heads
+    per = 128 // size
+    scale = size ** -0.5
+    groups = width // 128
+    c_out, c_up, c_head = 3 * width, 4 * width, 4 * width + hidden
+    pixels = w_ref.shape[1] - c_head
+    cols = rows // 8
+    nblk = pix_ref.shape[0] // rows
+    chunk = 512
+
+    gin_ref[...] = jnp.zeros_like(gin_ref)
+    gdown_ref[...] = jnp.zeros_like(gdown_ref)
+    gvec_ref[...] = jnp.zeros_like(gvec_ref)
+    gp_ref[...] = jnp.zeros_like(gp_ref)
+    loss_ref[...] = jnp.zeros_like(loss_ref)
+    f_id = lax.broadcasted_iota(jnp.int32, (128, 128 * per), 0)
+    q_id = lax.broadcasted_iota(jnp.int32, (128, 128 * per), 1)
+    hm[...] = jnp.where(f_id // size == q_id // 128, 1.0, 0.0).astype(BF16)
+    wm[...] = jnp.where(f_id // 32 == (q_id % 128) // 32, 1.0, 0.0).astype(BF16)
+
+    def lane(i):
+        return pl.ds(pl.multiple_of(i * 128, 128), 128)
+
+    def ln_forward(k, xh, out):
+        def body(i):
+            x = res[:, lane(i)]
+            centre = x - jnp.mean(x, axis=0, keepdims=True)
+            r = lax.rsqrt(jnp.mean(centre * centre, axis=0, keepdims=True) + 1e-06)
+            xhat = centre * r
+            xh[:, lane(i)] = xhat
+            rs[8 * k : 8 * k + 8, lane(i)] = jnp.broadcast_to(r, (8, 128))
+            out[:, lane(i)] = (xhat * vec_ref[2 * k] + vec_ref[2 * k + 1]).astype(BF16)
+        loop(rows // 128, body, 4)
+
+    def ln_backward(k, xh, add):
+        def body(i):
+            d = tmp[:, lane(i)]
+            xhat = xh[:, lane(i)]
+            gvec_ref[2 * k] += d * xhat
+            gvec_ref[2 * k + 1] += d
+            dx = d * vec_ref[2 * k]
+            m1 = jnp.mean(dx, axis=0, keepdims=True)
+            m2 = jnp.mean(dx * xhat, axis=0, keepdims=True)
+            g = rs[8 * k : 8 * k + 1, lane(i)] * (dx - m1 - xhat * m2)
+            if add:
+                g = g + res[:, lane(i)]
+            res[:, lane(i)] = g
+            low[:, lane(i)] = g.astype(BF16)
+        loop(rows // 128, body, 4)
+
+    def block(j):
+        first = pl.multiple_of(j * rows, rows)
+        turn = shift_ref[j]
+        spot = lax.broadcasted_iota(jnp.int32, (rvis_ref.shape[0], rows), 1) + first
+        hot = jnp.where(wide(rvis_ref[...], rows) == spot, 1.0, 0.0)
+        oh[...] = hot.astype(BF16)
+        masked = 1.0 - jnp.sum(hot, axis=0, keepdims=True)
+        mrow[...] = jnp.broadcast_to(masked, (8, rows))
+        et = et_ref[pl.ds(pl.multiple_of(j * cols, cols), cols), :]
+        e_hi = et.astype(BF16)
+        rest = et - e_hi.astype(F32)
+        e_mid = rest.astype(BF16)
+        e_lo = (rest - e_mid.astype(F32)).astype(BF16)
+        spread = jnp.where(
+            lax.broadcasted_iota(jnp.int32, (cols, rows), 1) // 8 == lax.broadcasted_iota(jnp.int32, (cols, rows), 0), 1.0, 0.0
+        ).astype(BF16)
+        e_t = mm(e_hi, spread, 0, 0) + (mm(e_mid, spread, 0, 0) + mm(e_lo, spread, 0, 0))
+        half = width // 2
+        keep = masked > 0.5
+        placed = mm(gvt_ref[...], oh[...])
+        top = (wide(vec_ref[6, :half], rows) + e_t).astype(BF16).astype(F32)
+        res[:half] = jnp.where(keep, top, placed[:half])
+        bottom = wide((vec_ref[6, half:] + ef_ref[...]).astype(BF16).astype(F32), rows)
+        res[half:] = jnp.where(keep, bottom, placed[half:])
+        k_half = (lax.broadcasted_iota(jnp.int32, (32, 128 * per), 0) % 8 + turn) % 8 // 4
+        q_half = (lax.broadcasted_iota(jnp.int32, (32, 128 * per), 1) % 8 + turn) % 8 // 4
+        hb[...] = jnp.where(k_half == q_half, 0.0, -1e30)
+
+        ln_forward(0, xh1, n1)
+
+        def qkv_part(i):
+            part = pl.ds(pl.multiple_of(i * chunk, chunk), chunk)
+            qkv[part, :] = mm(wt_ref[part, :], n1[...]).astype(BF16)
+        loop(3 * width // chunk, qkv_part)
+
+        q_group = (lax.broadcasted_iota(jnp.int32, (32, 128 * per), 1) % 128) // 32
+
+        def compact(s):
+            c = s[96:128]
+            for i in (2, 1, 0):
+                c = jnp.where(q_group == i, s[32 * i : 32 * i + 32], c)
+            return c
+
+        def attend(i):
+            sb, g = i // groups, i % groups
+            at = lane(sb)
+            f0 = pl.multiple_of(g * 128, 128)
+            q = qkv[pl.ds(f0, 128), at]
+            k = qkv[pl.ds(width + f0, 128), at]
+            v = qkv[pl.ds(2 * width + f0, 128), at]
+            s = mm(k.T, wide(q, 128 * per) * hm[...])
+            c = compact(s) * scale + hb[...]
+            e = jnp.exp(c - jnp.max(c, axis=0, keepdims=True))
+            p = e * (1.0 / jnp.sum(e, axis=0, keepdims=True))
+            probs[i] = p
+            p_low = p.astype(BF16)
+            p_all = jnp.concatenate([p_low] * 4, axis=0) * wm[...]
+            for h in range(per):
+                o = mm(v[size * h : size * h + size], p_all[:, 128 * h : 128 * h + 128])
+                att[pl.ds(f0 + size * h, size), at] = o.astype(BF16)
+        loop(rows // 128 * groups, attend, 4)
+
+        res[...] += mm(wt_ref[c_out : c_out + width], att[...])
+        ln_forward(1, xh2, n2)
+
+        def up_part(i):
+            part = pl.ds(pl.multiple_of(i * chunk, chunk), chunk)
+            u = mm(wt_ref[pl.ds(pl.multiple_of(c_up + i * chunk, chunk), chunk), :], n2[...])
+            t = jnp.tanh(GELU_C * (u + 0.044715 * (u * u * u)))
+            hp = 0.5 * (1.0 + t)
+            act[part, :] = (u * hp).astype(BF16)
+            dgel[part, :] = hp + (0.5 * GELU_C) * u * (1.0 - t * t) * (1.0 + 0.134145 * (u * u))
+        loop(hidden // chunk, up_part)
+
+        res[...] += mm(wdt_ref[...], act[...])
+        ln_forward(2, xh3, fin)
+        pred = mm(wt_ref[c_head:], fin[...])
+        pix = pix_ref[pl.ds(first, rows), :].astype(F32).T
+        centre = pix - jnp.mean(pix, axis=0, keepdims=True)
+        target = (centre * lax.rsqrt(jnp.mean(centre * centre, axis=0, keepdims=True) + 1e-06)).astype(BF16).astype(F32)
+        err = pred - target
+        loss_ref[...] += fold(mrow[...] * jnp.mean(err * err, axis=0, keepdims=True))
+        gpred = (mrow[0:1] * err * coef).astype(BF16)
+
+        gin_ref[:, c_head:] += mm(fin[...], gpred, 1, 1)
+        tmp[...] = mm(w_ref[:, c_head:], gpred)
+        ln_backward(2, xh3, False)
+
+        def mlp_back(i):
+            part = pl.ds(pl.multiple_of(i * chunk, chunk), chunk)
+            there = pl.ds(pl.multiple_of(c_up + i * chunk, chunk), chunk)
+            d = (mm(wd_ref[part, :], low[...]) * dgel[part, :]).astype(BF16)
+            dup[part, :] = d
+            gdown_ref[part, :] += mm(act[part, :], low[...], 1, 1)
+            gin_ref[:, there] += mm(n2[...], d, 1, 1)
+        loop(hidden // chunk, mlp_back)
+        tmp[...] = mm(w_ref[:, c_up:c_head], dup[...])
+        ln_backward(1, xh2, True)
+        gin_ref[:, c_out:c_up] += mm(att[...], low[...], 1, 1)
+        fin[...] = mm(w_ref[:, c_out:c_up], low[...]).astype(BF16)
+
+        def attend_back(i):
+            sb, g = i // groups, i % groups
+            at = lane(sb)
+            f0 = pl.multiple_of(g * 128, 128)
+            q = qkv[pl.ds(f0, 128), at]
+            k = qkv[pl.ds(width + f0, 128), at]
+            v = qkv[pl.ds(2 * width + f0, 128), at]
+            do = fin[pl.ds(f0, 128), at]
+            dp = compact(mm(v.T, wide(do, 128 * per) * hm[...]))
+            p = probs[i]
+            ds = p * (dp - jnp.sum(dp * p, axis=0, keepdims=True))
+            p_all = jnp.concatenate([p.astype(BF16)] * 4, axis=0) * wm[...]
+            ds_all = jnp.concatenate([(ds * scale).astype(BF16)] * 4, axis=0) * wm[...]
+            for h in range(per):
+                rows_h = slice(size * h, size * h + size)
+                ds_h = ds_all[:, 128 * h : 128 * h + 128]
+                p_h = p_all[:, 128 * h : 128 * h + 128]
+                dqkv[pl.ds(f0 + size * h, size), at] = mm(k[rows_h], ds_h).astype(BF16)
+                dqkv[pl.ds(width + f0 + size * h, size), at] = mm(q[rows_h], ds_h, 1, 1).astype(BF16)
+                dqkv[pl.ds(2 * width + f0 + size * h, size), at] = mm(do[rows_h], p_h, 1, 1).astype(BF16)
+        loop(rows // 128 * groups, attend_back, 4)
+
+        def qkv_back(i):
+            part = pl.ds(pl.multiple_of(i * chunk, chunk), chunk)
+            gin_ref[:, part] += mm(n1[...], dqkv[part, :], 1, 1)
+        loop(3 * width // chunk, qkv_back)
+        tmp[...] = mm(w_ref[:, :c_out], dqkv[...])
+        ln_backward(0, xh1, True)
+        gvec_ref[6] += fold(low[...].astype(F32) * mrow[0:1])
+        gp_ref[...] += mm(oh[...], low[...], 1, 1)
+
+    loop(nblk, block)
+
+
+def decoder_step(shift, rvis, gvt, pix, et, ef, vec, w, wt, wd, wdt, coef, heads):
+    width, total = w.shape
+    hidden = wd.shape[0]
+    rows = 512
+    vis = rvis.shape[0]
+    per = 128 // (width // heads)
+    vmem = pl.BlockSpec(memory_space=pltpu.VMEM)
+    f = lambda *s: pltpu.VMEM(s, F32)
+    b = lambda *s: pltpu.VMEM(s, BF16)
+    return pl.pallas_call(
+        functools.partial(decoder_kernel, coef, heads),
+        out_shape=(
+            jax.ShapeDtypeStruct((width, total), F32),
+            jax.ShapeDtypeStruct((hidden, width), F32),
+            jax.ShapeDtypeStruct((7, width, 128), F32),
+            jax.ShapeDtypeStruct((vis, width), F32),
+            jax.ShapeDtypeStruct((8, 128), F32),
+        ),
+        in_specs=[pl.BlockSpec(memory_space=pltpu.SMEM)] + [vmem] * 10,
+        out_specs=(vmem,) * 5,
+        scratch_shapes=[
+            f(width, rows), f(width, rows), f(width, rows), f(width, rows), f(width, rows),
+            b(width, rows), b(width, rows), b(width, rows), f(24, rows),
+            b(3 * width, rows), b(width, rows), b(hidden, rows), f(hidden, rows),
+            f(rows // 128 * (width // 128), 32, 128 * per), b(3 * width, rows), b(hidden, rows), b(width, rows),
+            b(vis, rows), f(8, rows), f(32, 128 * per), b(128, 128 * per), b(128, 128 * per),
+        ],
+        compiler_params=pltpu.CompilerParams(vmem_limit_bytes=63 * 2**20),
+        name="decoder",
+    )(shift, rvis, gvt, pix, et, ef, vec, w, wt, wd, wdt)
 
 
 def layer_norm(stream, gain, offset):
@@ -32,34 +288,16 @@
     )
 
 
-def layout(clip_lengths, clip_shifts, patch_dev):
+def clip_of(column, clip_lengths, clip_shifts):
     columns = clip_lengths // 8
-    clip_ends = jnp.cumsum(columns)
-    starts = clip_ends - columns
-    windows = columns // 8
-    offsets = jnp.cumsum(windows) - windows
-    patches = jnp.arange(patch_dev, dtype=jnp.int32)
-    column = patches // 8
-    frequency = patches % 8
-    clip_id = jnp.sum((column[:, None] >= clip_ends[None, :]).astype(jnp.int32), axis=1)
-    onehot = (
-        clip_id[:, None] == jnp.arange(clip_lengths.shape[0], dtype=jnp.int32)[None, :]
-    ).astype(jnp.int32)
+    ends = jnp.cumsum(columns)
+    clip_id = jnp.sum((column[:, None] >= ends[None, :]).astype(jnp.int32), axis=1)
+    onehot = (clip_id[:, None] == jnp.arange(clip_lengths.shape[0], dtype=jnp.int32)[None, :]).astype(jnp.int32)
 
     def select(values):
         return jnp.sum(onehot * values[None, :], axis=1)
 
-    time_pos = column - select(starts)
-    turned_time = (time_pos + select(clip_shifts[:, 0])) % select(columns)
-    turned_band = (frequency + select(clip_shifts[:, 1])) % 8
-    target_band = turned_band // 4 * 2 + turned_time // 4 % 2
-    dest_row = (
-        target_band * (patch_dev // 4)
-        + (select(offsets) + turned_time // 8) * 16
-        + turned_time % 4 * 4
-        + turned_band % 4
-    )
-    return (time_pos, frequency, clip_id, dest_row)
+    return clip_id, select(ends - columns), select(columns), select(clip_shifts[:, 0]), select(clip_shifts[:, 1])
 
 
 def product(values_in, weights_in):
@@ -231,68 +469,51 @@
         w_enc_down,
     )
     w_proj = w_enc[:, 4 * enc_width + enc_hidden :]
-    dec_weights = (
-        w_dec[:, : 3 * dec_width],
-        w_dec[:, 3 * dec_width : 4 * dec_width],
-        w_dec[:, 4 * dec_width : 4 * dec_width + dec_hidden],
-        w_dec_down,
-    )
-    w_head = w_dec[:, 4 * dec_width + dec_hidden :]
-    patch_dev = pixels.shape[0]
-    time_pos, frequency, clip_id, dest_row = layout(lengths[0], shifts[0], patch_dev)
-    source = (
-        jnp.zeros((patch_dev,), jnp.int32).at[dest_row].set(jnp.arange(patch_dev, dtype=jnp.int32))
-    )
+    patch_dev, n_visible = pixels.shape[0], visible.shape[0]
+    turned = jnp.arange(patch_dev // 8, dtype=jnp.int32)
+    _, start, size, shift_time, shift_band = clip_of(turned, lengths[0], shifts[0])
+    turned_time = (turned - start - shift_time) % size
+    decoder_pixels = pixels.reshape(patch_dev // 8, 8, -1)[start + turned_time].reshape(pixels.shape)
     seen = pixels[visible]
-    segment = clip_id[visible]
+    seen_column, seen_band = visible // 8, visible % 8
+    segment, seen_start, seen_size, seen_shift, _ = clip_of(seen_column, lengths[0], shifts[0])
+    seen_time = seen_column - seen_start
+    decoder_row = 8 * (seen_start + (seen_time + seen_shift) % seen_size) + seen_band
+    padded = -(-n_visible // 128) * 128
+    decoder_row = jnp.pad(decoder_row, (0, padded - n_visible), constant_values=-1)
+    decoder_row = jnp.broadcast_to(decoder_row[:, None], (padded, 128))
     score_bias = jnp.where(segment[:, None] == segment[None, :], 0.0, -1e30)
-    embedded = product(seen, w_embed) + sincos(time_pos[visible], frequency[visible], enc_width)
+    embedded = product(seen, w_embed) + sincos(seen_time, seen_band, enc_width)
     encoded, enc_cache = block_forward(
         embedded, enc_weights, enc_gains, HEADS_ENC, seen.shape[0], score_bias
     )
     final_enc = layer_norm(encoded, enc_gains[4], enc_gains[5]).astype(jnp.bfloat16)
     projected = product(final_enc, w_proj)
-    kept_mask = jnp.zeros((patch_dev,), jnp.float32).at[visible].set(1.0)
-    placed = jnp.zeros((patch_dev, dec_width), jnp.float32).at[visible].set(projected)
-    grid = jnp.where(kept_mask[:, None] > 0.5, placed, dec_gains[6][None, :]) + sincos(
-        time_pos, frequency, dec_width
-    )
-    pixel_float = pixels.astype(jnp.float32)
-    centre = pixel_float - jnp.mean(pixel_float, axis=1, keepdims=True)
-    target = (centre * lax.rsqrt(jnp.mean(centre * centre, axis=1, keepdims=True) + 1e-06)).astype(
-        jnp.bfloat16
-    )
-    grid_rows = grid.astype(jnp.bfloat16)[source]
-    target_rows = target[source]
-    masked_rows = (1.0 - kept_mask).astype(jnp.bfloat16)[source]
-    grid_rows, target_rows, masked_rows = (
-        lax.all_to_all(grid_rows, "band", split_axis=0, concat_axis=0, tiled=True),
-        lax.all_to_all(target_rows, "band", split_axis=0, concat_axis=0, tiled=True),
-        lax.all_to_all(masked_rows, "band", split_axis=0, concat_axis=0, tiled=True),
-    )
-    decoded, dec_cache = block_forward(
-        grid_rows.astype(jnp.float32), dec_weights, dec_gains, HEADS_DEC, 16, 0.0
-    )
-    final_dec = layer_norm(decoded, dec_gains[4], dec_gains[5]).astype(jnp.bfloat16)
-    predicted = product(final_dec, w_head)
-    error = predicted - target_rows.astype(jnp.float32)
-    row_weight = masked_rows.astype(jnp.float32)
-    local_loss = jnp.sum(row_weight * jnp.mean(error * error, axis=1))
+    grid_seen = (projected + sincos(seen_time, seen_band, dec_width)).astype(jnp.bfloat16)
+    grid_seen = jnp.pad(grid_seen, ((0, padded - n_visible), (0, 0)))
+    time_table = sincos(turned_time, turned_time, dec_width)[:, : dec_width // 2]
+    bands = jnp.arange(8, dtype=jnp.int32)
+    band_table = jnp.tile(sincos(bands, bands, dec_width)[:, dec_width // 2 :].T, (1, 16))
+    wide_vectors = jnp.broadcast_to(dec_gains[:, :, None], dec_gains.shape + (128,))
     masked_count = 13.0 * (patch_dev // 16) * lax.axis_size("clip") * lax.axis_size("band")
-    grad_pred = (row_weight[:, None] * error * (2.0 / (error.shape[1] * masked_count))).astype(
-        jnp.bfloat16
-    )
-    g_head = weight_grad(final_dec, grad_pred)
-    _, dec_final_back = jax.vjp(layer_norm, decoded, dec_gains[4], dec_gains[5])
-    grad_decoded, g_dec_gain, g_dec_offset = dec_final_back(input_grad(grad_pred, w_head))
-    grad_grid, g_dec_mats, g_dec_norms = block_backward(
-        grad_decoded, dec_cache, dec_weights, dec_gains, HEADS_DEC, 16, 0.0
-    )
-    grad_grid = grad_grid.astype(jnp.bfloat16)
-    grad_grid = lax.all_to_all(grad_grid, "band", split_axis=0, concat_axis=0, tiled=True)
-    grad_patch = grad_grid[dest_row]
-    g_token = jnp.sum((1.0 - kept_mask)[:, None] * grad_patch.astype(jnp.float32), axis=0)
-    grad_proj = grad_patch[visible]
+    g_dec_in, g_dec_down, g_dec_vectors, grad_proj, loss = decoder_step(
+        shift_band[::64],
+        decoder_row,
+        grid_seen.T,
+        decoder_pixels,
+        time_table,
+        band_table,
+        wide_vectors,
+        w_dec,
+        w_dec.T,
+        w_dec_down,
+        w_dec_down.T,
+        2.0 / (pixels.shape[1] * masked_count),
+        HEADS_DEC,
+    )
+    local_loss = jnp.sum(loss[0])
+    g_dec_vectors = jnp.sum(g_dec_vectors, axis=2)
+    grad_proj = grad_proj[:n_visible].astype(jnp.bfloat16)
     g_proj = weight_grad(final_enc, grad_proj)
     _, enc_final_back = jax.vjp(layer_norm, encoded, enc_gains[4], enc_gains[5])
     grad_encoded, g_enc_gain, g_enc_offset = enc_final_back(input_grad(grad_proj, w_proj))
@@ -301,16 +522,12 @@
     )
     g_embed = weight_grad(seen, grad_embedded.astype(jnp.bfloat16))
     g_enc_in = jnp.concatenate([g_enc_mats[0], g_enc_mats[1], g_enc_mats[2], g_proj], axis=1)
-    g_dec_in = jnp.concatenate([g_dec_mats[0], g_dec_mats[1], g_dec_mats[2], g_head], axis=1)
     g_vectors = jnp.concatenate(
         [
             g_enc_norms.reshape(-1),
             g_enc_gain,
             g_enc_offset,
-            g_dec_norms.reshape(-1),
-            g_dec_gain,
-            g_dec_offset,
-            g_token,
+            g_dec_vectors.reshape(-1),
         ]
     )
     shard_grads = (
@@ -318,7 +535,7 @@
         lax.psum_scatter(g_enc_in, "clip", scatter_dimension=0, tiled=True),
         lax.psum_scatter(g_enc_mats[3], "clip", scatter_dimension=0, tiled=True),
         lax.psum_scatter(g_dec_in, "clip", scatter_dimension=0, tiled=True),
-        lax.psum_scatter(g_dec_mats[3], "clip", scatter_dimension=0, tiled=True),
+        lax.psum_scatter(g_dec_down, "clip", scatter_dimension=0, tiled=True),
         lax.psum_scatter(g_vectors, "clip", scatter_dimension=0, tiled=True),
     )
     reduced = lax.psum(

time: 2130 us -> 1730 us (0.81)
  local copies, waits for them, and re-layouts: 360 us -> 40.9 us
  matrix products: 491 us -> 174 us
  Pallas kernels: 0 us -> 196 us
  waiting for transfers between devices: 897 us -> 1070 us
  other arithmetic: 162 us -> 54 us
    pallas_call x0 -> x1, Pallas kernels: none -> 196 us  [decoder_step(): pl.pallas_call(functools.partial(decoder_kernel, coef, heads), out_shape=...]
    all_gather x1, waiting for transfers between devices: 0.02 us -> 142 us  [shards(): lax.all_gather(encoder_in.astype(jnp.bfloat16), 'clip', axis=0, tiled=True)]
    convert_element_type x6 -> x0, local copies, waits for them, and re-layouts: 113 us -> none  [the longest x2 80.4 us: block_backward(): attend_back(grad_attended, projections, heads, group, score_bias)]
    gather x8 -> x1, local copies, waits for them, and re-layouts: 72.9 us -> 2.6 us  [shards(): pixels.reshape(patch_dev // 8, 8, -1)[start + turned_time]]
    all_to_all x4 -> x0, waiting for transfers between devices: 66.8 us -> none  [the longest x1 36.8 us: shards(): lax.all_to_all(grad_grid, 'band', split_axis=0, concat_axis=0, tiled=True)]
    dot_general x10 -> x5, matrix products: 80.7 us -> 27.3 us  [input_grad(): lax.dot_general(grad_low, weights_in, (((1,), (1,)), ((), ())), preferred...]
    reshape x2 -> x1, local copies, waits for them, and re-layouts: 51.6 us -> 0.01 us  [shards(): g_dec_vectors.reshape(-1)]
    dot_general x11 -> x6, matrix products: 76 us -> 27.9 us  [product(): return jnp.dot(values_in, weights_in, preferred_element_type=jnp.float32)]
  transfers between devices with their start and end apart: 14 -> 10, of which waited for: 8 -> 9; matrix products, arithmetic and copies ran while one was open for 22% -> 6% of each run, Pallas kernels for 0% -> 0%
where the time goes in v1:
time: 1730 us; the launch traced here: 1720 us
  waiting for transfers between devices  1070 us (62%)
  Pallas kernels  196 us (11%)
  matrix products  174 us (10%)
  blocking collectives  163 us (9%)
  other arithmetic  54 us (3%)
  local copies, waits for them, and re-layouts  40.9 us (2%)
  between operations  22 us (1%)
    reduce_scatter x1, waiting for transfers between devices, shards(): lax.psum_scatter(g_enc_in, 'clip', scatter_dimension=0, tiled=True)  339 us
    pallas_call x1, Pallas kernels, decoder_step(): pl.pallas_call(functools.partial(decoder_kernel, coef, heads), out_shape=...  196 us
    reduce_scatter x1, waiting for transfers between devices, shards(): lax.psum_scatter(g_enc_mats[3], 'clip', scatter_dimension=0, tiled=True)  166 us
    reduce_scatter x1, waiting for transfers between devices, shards(): lax.psum_scatter(g_dec_in, 'clip', scatter_dimension=0, tiled=True)  160 us
    all_gather x1, waiting for transfers between devices, shards(): lax.all_gather(encoder_in.astype(jnp.bfloat16), 'clip', axis=0, tiled=True)  142 us
    reduce_scatter x1, waiting for transfers between devices, shards(): lax.psum_scatter(g_dec_down, 'clip', scatter_dimension=0, tiled=True)  90.8 us
    psum x1, waiting for transfers between devices, shards(): lax.psum((shard_grads[0], shard_grads[1], shard_grads[2], shard_grads[3],...  62.8 us
    all_gather x1, waiting for transfers between devices, shards(): lax.all_gather(decoder_in.astype(jnp.bfloat16), 'clip', axis=0, tiled=True)  45.2 us
  transfers between devices with their start and end apart: 10, of which 9 were waited for; matrix products, arithmetic and copies ran while one was open for 6% of the time, Pallas kernels for 0%

profile of v1, /device:TPU:0, one launch (start us, length us, event | category | flops | bytes accessed | tf_op | source)
XLA Modules:
  0.0 1724.0 jit_solution(7177144954917443093)
XLA Ops:
  16.5 27.9 %all_gather.19 = bf16[8192]{0:T(1024)(128)(2,1)S(1)} all-gather(bf16[1024]{0:T(1024)(128)(2,1)S(1)} %convert_element_type.119), channel_id=1, replica_groups=mesh['clip'=8,'band'=4] {'clip'}, dimensions={0}, use_global_device_ids=true | all-gather | bytes 18432 | tf_op jit(solution)/shard_map/all_gather | solution.py:458
  53.6 32.1 %all_gather.18 = bf16[256,768]{1,0:T(8,128)(2,1)S(1)} all-gather(bf16[32,768]{1,0:T(8,128)(2,1)S(1)} %convert_element_type.116), channel_id=1, replica_groups=mesh['clip'=8,'band'=4] {'clip'}, dimensions={0}, use_global_device_ids=true | all-gather | bytes 442368 | tf_op jit(solution)/shard_map/all_gather | solution.py:453
  99.4 45.2 %all-gather.9.cloned.1.call-done.w_ref = bf16[512,4352]{1,0:T(8,128)(2,1)} async-done(((bf16[64,4352]{1,0:T(8,128)(2,1)}), bf16[512,4352]{1,0:T(8,128)(2,1)}) %all-gather.9.cloned.1.call-update) | async-done | bytes 4456464 | tf_op jit(solution)/shard_map/all_gather | solution.py:456
  151.1 142.1 %all-gather.5.cloned.1.call-done = bf16[768,6656]{1,0:T(8,128)(2,1)} async-done(((bf16[96,6656]{1,0:T(8,128)(2,1)}), bf16[768,6656]{1,0:T(8,128)(2,1)}) %all-gather.5.cloned.1.call-update) | async-done | bytes 10223632 | tf_op jit(solution)/shard_map/all_gather | solution.py:454
  303.6 10.2 fusion.108
  313.8 8.1 fusion.35
  333.7 40.2 %all-gather.7.cloned.1.call-done = bf16[3072,768]{1,0:T(8,128)(2,1)} async-done(((bf16[384,768]{1,0:T(8,128)(2,1)}), bf16[3072,768]{1,0:T(8,128)(2,1)}) %all-gather.7.cloned.1.call-update) | async-done | bytes 4718608 | tf_op jit(solution)/shard_map/all_gather | solution.py:455
  373.9 8.6 fusion.110
  390.3 196.2 %decoder.1 = (f32[512,4352]{1,0:T(8,128)}, f32[2048,512]{1,0:T(8,128)}, f32[7,512,128]{2,1,0:T(8,128)}, f32[640,512]{1,0:T(8,128)}, f32[8,128]{1,0:T(8,128)}) custom-call(s32[6]{0:T(128)} %slice.89.shift_ref, s32[640,128]{1,0:T(8,128)} %broadcast_in_dim.34.rvis_ref, bf16[512,640]{1,0:T(8,128)(2,1)} %pad_bitcast_fusion.gvt_ref, bf16[3072,256]{1,0:T(8,128)(2,1)} %bitcast.102, ...), custom_call_target="tpu_custom_call" | custom-call | tf_op jit(solution)/shard_map/decoder/pallas_call | solution.py:252
  591.1 11.3 fusion.16
  612.2 9.7 fusion.54
  621.9 9.7 fusion.63
  631.6 27.5 %fusion.51 = bf16[1,576,1,12,64]{1,4,3,2,0:T(8,128)(2,1)} fusion(f32[12,576,576]{1,2,0:T(8,128)} %fusion.63, bf16[1,576,3,12,64]{1,4,3,2,0:T(8,128)(2,1)} %bitcast.106, f32[12,576,576]{1,2,0:T(8,128)} %get-tuple-element.108, f32[12,576]{1,0:T(8,128)S(1)} %copy-done.80), kind=kOutput, calls=%fused_computation.77 | convolution fusion | flops 537926976 | bytes 72728576 | tf_op jit(solution)/shard_map/bhqk,bkhd->bqhd/dot_general | solution.py:358
  659.1 27.9 %fusion.48 = bf16[1,576,1,12,64]{1,4,3,2,0:T(8,128)(2,1)} fusion(f32[12,576,576]{1,2,0:T(8,128)} %fusion.63, bf16[1,576,3,12,64]{1,4,3,2,0:T(8,128)(2,1)} %bitcast.107, f32[12,576,576]{1,2,0:T(8,128)} %get-tuple-element.108, f32[12,576]{1,0:T(8,128)S(1)} %copy-done.80), kind=kOutput, calls=%fused_computation.76 | convolution fusion | flops 537926976 | bytes 72728576 | tf_op jit(solution)/shard_map/bhqk,bqhd->bkhd/dot_general | solution.py:359
  700.5 12.1 fusion.93
  733.1 26.9 %reduce-scatter.6.cloned.1.call-done = f32[32,768]{1,0:T(8,128)} async-done(((f32[256,768]{1,0:T(8,128)}), f32[32,768]{1,0:T(8,128)}) %reduce-scatter.6.cloned.1.call-update) | async-done | bytes 98320 | tf_op jit(solution)/shard_map/reduce_scatter | solution.py:534
  760.0 90.8 %reduce-scatter.14.cloned.1.call-done = f32[256,512]{1,0:T(8,128)} async-done(((f32[2048,512]{1,0:T(8,128)}), f32[256,512]{1,0:T(8,128)}) %reduce-scatter.14.cloned.1.call-update) | async-done | bytes 524304 | tf_op jit(solution)/shard_map/reduce_scatter | solution.py:538
  850.8 159.6 %reduce-scatter.12.cloned.1.call-done = f32[64,4352]{1,0:T(8,128)} async-done(((f32[512,4352]{1,0:T(8,128)}), f32[64,4352]{1,0:T(8,128)}) %reduce-scatter.12.cloned.1.call-update) | async-done | bytes 1114128 | tf_op jit(solution)/shard_map/reduce_scatter | solution.py:537
  1010.4 166.0 %reduce-scatter.10.cloned.1.call-done = f32[384,768]{1,0:T(8,128)} async-done(((f32[3072,768]{1,0:T(8,128)}), f32[384,768]{1,0:T(8,128)}) %reduce-scatter.10.cloned.1.call-update) | async-done | bytes 1179664 | tf_op jit(solution)/shard_map/reduce_scatter | solution.py:536
  1176.4 338.5 %reduce-scatter.8.cloned.1.call-done = f32[96,6656]{1,0:T(8,128)} async-done(((f32[768,6656]{1,0:T(8,128)}), f32[96,6656]{1,0:T(8,128)}) %reduce-scatter.8.cloned.1.call-update) | async-done | bytes 2555920 | tf_op jit(solution)/shard_map/reduce_scatter | solution.py:535
  1517.5 35.2 %all-reduce.2 = f32[8192]{0:T(1024)S(1)} all-reduce(f32[8192]{0:T(1024)S(1)} %pad_maximum_fusion.3), channel_id=7, replica_groups=mesh['clip'=8,'band'=4] {'clip'}, use_global_device_ids=true, to_apply=%region_49.50.clone | all-reduce | flops 8192 | bytes 65536
  1561.2 62.8 %all-reduce.6.cloned.1.call-done = (f32[32,768]{1,0:T(8,128)}, f32[96,6656]{1,0:T(8,128)}, f32[384,768]{1,0:T(8,128)}, f32[64,4352]{1,0:T(8,128)}, f32[256,512]{1,0:T(8,128)}) async-done(((f32[32,768]{1,0:T(8,128)}, f32[96,6656]{1,0:T(8,128)}, f32[384,768]{1,0:T(8,128)}, f32[64,4352]{1,0:T(8,128)}, f32[256,512]{1,0:T(8,128)}), (f32[32,768]{1,0:T(8,128)}, f32[96,6656]{1,0:T(8,128)}, f32[384,768]{1,0:T(8,128)}, ...) | async-done | bytes 5472272 | tf_op jit(solution)/shard_map/psum | solution.py:541
  1636.2 40.0 %psum.56 = f32[]{:T(128)} all-reduce(f32[]{:T(128)} %slice_reduce_fusion), channel_id=1, replica_groups=mesh['clip'=8,'band'=4] {'clip','band'}, use_global_device_ids=true, to_apply=%region_19.20 | all-reduce | flops 1 | bytes 8 | tf_op jit(solution)/shard_map/psum | solution.py:555
  1676.1 21.6 %psum.63 = f32[]{:T(128)} all-reduce(f32[]{:T(128)S(6)} %add.347), channel_id=1, replica_groups=mesh['clip'=8,'band'=4] {'clip'}, use_global_device_ids=true, to_apply=%region_52.53 | all-reduce | flops 1 | bytes 8 | tf_op jit(solution)/shard_map/psum | solution.py:556
  (296 shorter events, 151.8 us)
Async XLA Ops:
  7.2 88.2 %all-gather.11.cloned.1.call-start = ((), (), s32[]{:S(2)}) async-start(), calls=%async_computation.8 | async-start | bytes 2359296 | tf_op jit(solution)/shard_map/all_gather | solution.py:457
  9.3 135.3 %all-gather.9.cloned.1.call-start = ((), (), s32[]{:S(2)}) async-start(), calls=%async_computation.7 | async-start | bytes 5013504 | tf_op jit(solution)/shard_map/all_gather | solution.py:456
  11.5 281.7 %all-gather.5.cloned.1.call-start = ((), (), s32[]{:S(2)}) async-start(), calls=%async_computation.5 | async-start | bytes 11501568 | tf_op jit(solution)/shard_map/all_gather | solution.py:454
  12.8 361.1 %all-gather.7.cloned.1.call-start = ((), (), s32[]{:S(2)}) async-start(), calls=%async_computation.6 | async-start | bytes 5308416 | tf_op jit(solution)/shard_map/all_gather | solution.py:455
  14.9 745.1 %reduce-scatter.6.cloned.1.call-start = ((), (), s32[]{:S(2)}) async-start(), calls=%async_computation.9 | async-start | bytes 884736 | tf_op jit(solution)/shard_map/reduce_scatter | solution.py:534
  90.5 231.5 %copy-start.2 = (f32[576,768]{1,0:T(8,128)}, f32[576,768]{1,0:T(8,128)S(1)}, u32[]{:S(2)}) copy-start(f32[576,768]{1,0:T(8,128)S(1)} %get-tuple-element.106) | copy-start | bytes 5308420
  90.5 202.7 %copy-start.44 = (f32[576]{0:T(1024)}, f32[576]{0:T(1024)S(1)}, u32[]{:S(2)}) copy-start(f32[576]{0:T(1024)S(1)} %broadcast_multiply_fusion.2) | copy-start | bytes 6916
  90.9 202.3 %copy-start.56 = (f32[576]{0:T(1024)}, f32[576]{0:T(1024)S(1)}, u32[]{:S(2)}) copy-start(f32[576]{0:T(1024)S(1)} %fusion.79) | copy-start | bytes 6916
  91.7 201.5 %copy-start.52 = (f32[768]{0:T(1024)}, f32[768]{0:T(1024)S(1)}, u32[]{:S(2)}) copy-start(f32[768]{0:T(1024)S(1)} %get-tuple-element.81) | copy-start | bytes 9220
  91.7 201.5 %copy-start.69 = (f32[768]{0:T(1024)}, f32[768]{0:T(1024)S(1)}, u32[]{:S(2)}) copy-start(f32[768]{0:T(1024)S(1)} %get-tuple-element.82) | copy-start | bytes 9220
  382.6 207.7 %copy-start.47 = (f32[576]{0:T(1024)}, f32[576]{0:T(1024)S(1)}, u32[]{:S(2)}) copy-start(f32[576]{0:T(1024)S(1)} %broadcast_multiply_fusion) | copy-start | bytes 6916
  383.0 207.3 %copy-start.59 = (f32[576]{0:T(1024)}, f32[576]{0:T(1024)S(1)}, u32[]{:S(2)}) copy-start(f32[576]{0:T(1024)S(1)} %fusion.81) | copy-start | bytes 6916
  699.2 151.6 %reduce-scatter.14.cloned.1.call-start = ((), (), s32[]{:S(2)}) async-start(), calls=%async_computation.13 | async-start | bytes 4718592 | tf_op jit(solution)/shard_map/reduce_scatter | solution.py:538
  699.7 310.6 %reduce-scatter.12.cloned.1.call-start = ((), (), s32[]{:S(2)}) async-start(), calls=%async_computation.12 | async-start | bytes 10027008 | tf_op jit(solution)/shard_map/reduce_scatter | solution.py:537
  700.5 475.9 %reduce-scatter.10.cloned.1.call-start = ((), (), s32[]{:S(2)}) async-start(), calls=%async_computation.11 | async-start | bytes 10616832 | tf_op jit(solution)/shard_map/reduce_scatter | solution.py:536
  712.6 802.3 %reduce-scatter.8.cloned.1.call-start = ((), (), s32[]{:S(2)}) async-start(), calls=%async_computation.10 | async-start | bytes 23003136 | tf_op jit(solution)/shard_map/reduce_scatter | solution.py:535
  733.1 891.0 %all-reduce.6.cloned.1.call-start = ((), (), s32[]{:S(2)}) async-start(), calls=%async_computation.14 | async-start | bytes 10944512 | tf_op jit(solution)/shard_map/psum | solution.py:541
  1628.1 70.4 %copy-start.61 = (f32[1024]{0:T(1024)S(1)}, f32[1024]{0:T(1024)}, u32[]{:S(2)}) copy-start(f32[1024]{0:T(1024)} %param.31) | copy-start | bytes 12292
  1628.1 70.4 %copy-start.65 = (f32[1024]{0:T(1024)S(1)}, f32[1024]{0:T(1024)}, u32[]{:S(2)}) copy-start(f32[1024]{0:T(1024)} %param.37) | copy-start | bytes 12292
  1628.1 70.4 %copy-start.66 = (f32[1024]{0:T(1024)S(1)}, f32[1024]{0:T(1024)}, u32[]{:S(2)}) copy-start(f32[1024]{0:T(1024)} %param.43) | copy-start | bytes 12292
  1628.1 71.0 %copy-start.35 = (f32[32,768]{1,0:T(8,128)S(1)}, f32[32,768]{1,0:T(8,128)}, u32[]{:S(2)}) copy-start(f32[32,768]{1,0:T(8,128)} %param.26) | copy-start | bytes 294916
  1628.1 71.0 %copy-start.41 = (f32[32,768]{1,0:T(8,128)S(1)}, f32[32,768]{1,0:T(8,128)}, u32[]{:S(2)}) copy-start(f32[32,768]{1,0:T(8,128)} %param.32) | copy-start | bytes 294916
  1628.1 71.0 %copy-start.42 = (f32[32,768]{1,0:T(8,128)S(1)}, f32[32,768]{1,0:T(8,128)}, u32[]{:S(2)}) copy-start(f32[32,768]{1,0:T(8,128)} %param.38) | copy-start | bytes 294916
  1630.4 69.5 %copy-start.29 = (f32[256,512]{1,0:T(8,128)S(1)}, f32[256,512]{1,0:T(8,128)}, u32[]{:S(2)}) copy-start(f32[256,512]{1,0:T(8,128)} %param.30) | copy-start | bytes 1572868
  (70 other events, 413.3 us)
Sparse Core Ops, SparseCore 0:
  10.7 56.1 all-gather.10
  69.7 74.8 all-gather.8
  147.3 145.8 all-gather.4
  295.8 78.0 all-gather.6
  699.3 60.6 reduce-scatter.5
  763.9 86.8 reduce-scatter.13
  854.4 155.8 reduce-scatter.11
  1013.9 162.4 reduce-scatter.9
  1180.4 334.4 reduce-scatter.7
  1517.7 106.2 all-reduce.5

commit v2 on v1

--- a/solution.py
+++ b/solution.py
@@ -270,6 +270,342 @@
         compiler_params=pltpu.CompilerParams(vmem_limit_bytes=63 * 2**20),
         name="decoder",
     )(shift, rvis, gvt, pix, et, ef, vec, w, wt, wd, wdt)
+
+
+def place():
+    clip, band = lax.axis_index("clip"), lax.axis_index("band")
+    return clip // 2, clip % 2, band // 2, band % 2
+
+
+def device(z, x, y, c):
+    return (z * 2 + x, y * 2 + c)
+
+
+def greet(z, x, y, c):
+    barrier = pltpu.get_barrier_semaphore()
+    others = [device(z, x, y, 1 - c), device(z, 1 - x, y, c), device(z, x, 1 - y, c)]
+    others += [device((z + k) % 4, x, y, c) for k in (1, 2, 3)]
+    for other in others:
+        pl.semaphore_signal(barrier, inc=1, device_id=other, device_id_type=pl.DeviceIdType.MESH)
+    pl.semaphore_wait(barrier, len(others))
+
+
+def remote(src, dst, send, recv, to):
+    return pltpu.make_async_remote_copy(
+        src_ref=src, dst_ref=dst, send_sem=send, recv_sem=recv, device_id=to, device_id_type=pl.DeviceIdType.MESH
+    )
+
+
+def reduce_kernel(widths, n, *refs):
+    grads, small, outs, small_out = refs[:n], refs[n], refs[n + 1 : 2 * n + 1], refs[2 * n + 1]
+    rest = refs[2 * n + 2 :]
+    sums, r0, r1x, r1y, r2x, r2y, r3 = (rest[i * n : (i + 1) * n] for i in range(7))
+    s_buf, s_sum, send, recv, near, s_send, s_recv = rest[7 * n :]
+    z, x, y, c = place()
+    greet(z, x, y, c)
+
+    def at_z(k):
+        return (z + k) % 4
+
+    def columns(t, core):
+        half = sums[t].shape[4]
+        return pl.ds(pl.multiple_of(core * half, 128), half)
+
+    def local(t, k):
+        zk = at_z(k)
+        return pltpu.make_async_copy(grads[t].at[zk, :, :, :, columns(t, c)], sums[t].at[zk], near.at[t, k])
+
+    def copy(stage, t, k):
+        zk, w = at_z(k), widths[t]
+        total = sums[t].shape[4]
+        first, last = pl.ds(0, w), pl.ds(w, total - w)
+        s = sums[t]
+        src, dst, to = {
+            0: lambda: (grads[t].at[zk, :, :, :, columns(t, 1 - c)], r0[t].at[zk], device(z, x, y, 1 - c)),
+            1: lambda: (s.at[zk, 1 - x, :, :, first], r1x[t].at[zk], device(z, 1 - x, y, c)),
+            2: lambda: (s.at[zk, :, 1 - y, :, last], r1y[t].at[zk], device(z, x, 1 - y, c)),
+            3: lambda: (s.at[zk, x, 1 - y, :, first], r2x[t].at[zk], device(z, x, 1 - y, c)),
+            4: lambda: (s.at[zk, 1 - x, y, :, last], r2y[t].at[zk], device(z, 1 - x, y, c)),
+            5: lambda: (s.at[zk, x, y], r3[t].at[k - 1], device(zk, x, y, c)),
+            6: lambda: (s.at[z, x, y], outs[t].at[y, :, columns(t, c)], device(z, x, 1 - y, c)),
+            7: lambda: (outs[t].at[:, :, columns(t, c)], outs[t].at[:, :, columns(t, c)], device(z, x, y, 1 - c)),
+        }[stage]()
+        return remote(src, dst, send.at[t, stage, k], recv.at[t, stage, k], to)
+
+    def keep(t):
+        return pltpu.make_async_copy(sums[t].at[z, x, y], outs[t].at[y, :, columns(t, c)], near.at[t, 4])
+
+    def add(rows, parts, body):
+        per = rows // 16
+        def step(i, carry):
+            body(i // per, pl.ds(pl.multiple_of(i % per * 16, 16), 16))
+            return carry
+        lax.fori_loop(0, parts * per, step, 0)
+
+    def each(lo, hi, body):
+        def step(k, carry):
+            body(k)
+            return carry
+        lax.fori_loop(lo, hi, step, 0)
+
+    def start(k):
+        for t in range(n):
+            copy(0, t, k).start()
+            local(t, k).start()
+    each(1, 5, lambda k: start(k % 4))
+
+    s_sum[...] = small[...]
+    for stage, to in enumerate((device(z, x, y, 1 - c), device(z, 1 - x, y, c), device(z, x, 1 - y, c))):
+        hop = remote(s_sum, s_buf.at[stage], s_send.at[stage], s_recv.at[stage], to)
+        hop.start()
+        hop.wait()
+        s_sum[...] += s_buf[stage]
+    def small_hop(k):
+        return remote(s_sum, s_buf.at[3 + z], s_send.at[2 + k], s_recv.at[2 + k], device(at_z(k), x, y, c))
+    for k in (1, 2, 3):
+        small_hop(k).start()
+    s_buf[3 + z] = s_sum[...]
+
+    def first_sum(k):
+        zk = at_z(k)
+        for t in range(n):
+            copy(0, t, k).wait_recv()
+            local(t, k).wait()
+            def body(p, rows, t=t):
+                sums[t][zk, p // 2, p % 2, rows] += r0[t][zk, p // 2, p % 2, rows]
+            add(sums[t].shape[3], 4, body)
+            copy(1, t, k).start()
+            copy(2, t, k).start()
+    each(1, 5, lambda k: first_sum(k % 4))
+
+    def second_sum(k):
+        zk = at_z(k)
+        for t in range(n):
+            w = widths[t]
+            copy(1, t, k).wait_recv()
+            def body(p, rows, t=t, w=w):
+                sums[t][zk, x, p, rows, :w] += r1x[t][zk, p, rows]
+            add(sums[t].shape[3], 2, body)
+            copy(3, t, k).start()
+            copy(2, t, k).wait_recv()
+            def body(p, rows, t=t, w=w):
+                sums[t][zk, p, y, rows, w:] += r1y[t][zk, p, rows]
+            add(sums[t].shape[3], 2, body)
+            copy(4, t, k).start()
+    each(1, 5, lambda k: second_sum(k % 4))
+
+    def third_sum(k):
+        zk = at_z(k)
+        for t in range(n):
+            w = widths[t]
+            copy(3, t, k).wait_recv()
+            copy(4, t, k).wait_recv()
+            def body(p, rows, t=t, w=w):
+                sums[t][zk, x, y, rows, :w] += r2x[t][zk, rows]
+                sums[t][zk, x, y, rows, w:] += r2y[t][zk, rows]
+            add(sums[t].shape[3], 1, body)
+    def send_sum(k):
+        third_sum(k)
+        for t in range(n):
+            copy(5, t, k).start()
+    each(1, 4, send_sum)
+    third_sum(0)
+
+    for t in range(n):
+        for k in (1, 2, 3):
+            copy(5, t, k).wait_recv()
+        def body(p, rows, t=t):
+            sums[t][z, x, y, rows] += r3[t][0, rows] + r3[t][1, rows] + r3[t][2, rows]
+        add(sums[t].shape[3], 1, body)
+        copy(6, t, 0).start()
+        keep(t).start()
+    for k in (1, 2, 3):
+        small_hop(k).wait()
+    small_out[...] = (s_buf[3] + s_buf[4]) + (s_buf[5] + s_buf[6])
+    for t in range(n):
+        copy(6, t, 0).wait_recv()
+        keep(t).wait()
+        copy(7, t, 0).start()
+
+    def finish(k):
+        for t in range(n):
+            for stage in range(5):
+                copy(stage, t, k).wait_send()
+    each(0, 4, finish)
+    def finish_z(k):
+        for t in range(n):
+            copy(5, t, k).wait_send()
+    each(1, 4, finish_z)
+    for t in range(n):
+        copy(6, t, 0).wait_send()
+        copy(7, t, 0).wait()
+
+
+def reduce_grads(grads, small, ident):
+    n = len(grads)
+    views, widths = [], []
+    scratch = [[] for _ in range(7)]
+    for grad in grads:
+        rows, total = grad.shape
+        r2, half = rows // 16, total // 2
+        w = (half // 128 + 1) // 2 * 128
+        views.append(grad.reshape(4, 2, 2, r2, total))
+        widths.append(w)
+        f = lambda *s: pltpu.VMEM(s, F32)
+        for i, s in enumerate((f(4, 2, 2, r2, half), f(4, 2, 2, r2, half), f(4, 2, r2, w), f(4, 2, r2, half - w),
+                               f(4, r2, w), f(4, r2, half - w), f(3, r2, half))):
+            scratch[i].append(s)
+    anywhere, vmem = pl.BlockSpec(memory_space=pl.ANY), pl.BlockSpec(memory_space=pltpu.VMEM)
+    dma = pltpu.SemaphoreType.DMA
+    out = pl.pallas_call(
+        functools.partial(reduce_kernel, tuple(widths), n),
+        out_shape=tuple(jax.ShapeDtypeStruct((2, v.shape[3], v.shape[4]), F32) for v in views)
+        + (jax.ShapeDtypeStruct(small.shape, F32),),
+        in_specs=[anywhere] * n + [vmem],
+        out_specs=(anywhere,) * n + (vmem,),
+        scratch_shapes=sum(scratch, []) + [
+            pltpu.VMEM((7,) + small.shape, F32), pltpu.VMEM(small.shape, F32),
+            dma((n, 8, 4)), dma((n, 8, 4)), dma((n, 5)), dma((6,)), dma((6,)),
+        ],
+        compiler_params=pltpu.CompilerParams(
+            collective_id=ident, has_side_effects=True, vmem_limit_bytes=60 * 2**20
+        ),
+        name="reduce",
+    )(*views, small)
+    return [o.reshape(-1, o.shape[2]) for o in out[:n]], out[n]
+
+
+def gather_kernel(widths, n, *refs):
+    shards, vector, outs, vectors = refs[:n], refs[n], refs[n + 1 : 2 * n + 1], refs[2 * n + 1]
+    send, recv, near, v_send, v_recv = refs[2 * n + 2 :]
+    z, x, y, c = place()
+    greet(z, x, y, c)
+
+    def at_z(k):
+        return (z + k) % 4
+
+    def columns(t, lo, size):
+        half = shards[t].shape[2] // 2
+        return pl.ds(pl.multiple_of(c * half + lo, 128), size)
+
+    def own(t):
+        return pltpu.make_async_copy(shards[t], outs[t].at[z, x], near.at[t])
+
+    def copy(stage, t, k):
+        zk, w, half = at_z(k), widths[t], shards[t].shape[2] // 2
+        both, split, whole = columns(t, 0, w), columns(t, w, half - w), columns(t, 0, half)
+        first = isinstance(k, int) and k == 0
+        o = outs[t]
+        zo = (z - k) % 4
+        src, dst, to = {
+            0: lambda: (shards[t].at[:, :, both], o.at[z, x, :, :, both], device(zk, x, y, c)),
+            1: lambda: (shards[t].at[y, :, split], o.at[z, x, y, :, split], device(zk, x, y, c)),
+            2: lambda: ((shards[t].at[:, :, both] if first else o.at[zo, x, :, :, both]), o.at[zo, x, :, :, both], device(z, 1 - x, y, c)),
+            3: lambda: ((shards[t].at[y, :, split] if first else o.at[zo, x, y, :, split]), o.at[zo, x, y, :, split], device(z, 1 - x, y, c)),
+            4: lambda: ((o.at[zo, 1 - x, y, :, split],) * 2 if first else (o.at[zo, :, y, :, split],) * 2) + (device(z, x, 1 - y, c),),
+            5: lambda: ((o.at[zo, 1 - x, :, :, whole],) * 2 if first else (o.at[zo, :, :, :, whole],) * 2) + (device(z, x, y, 1 - c),),
+        }[stage]()
+        return remote(src, dst, send.at[t, stage, k], recv.at[t, stage, k], to)
+
+    def arrived(stage, t, k):
+        copy(stage, t, k).wait_recv()
+
+    def vector_copy(stage, k):
+        zo = (z - k) % 4
+        if stage == 0:
+            return remote(vector, vectors.at[z, x], v_send.at[k], v_recv.at[k], device(at_z(k), x, y, c))
+        src = vector if isinstance(k, int) and k == 0 else vectors.at[zo, x]
+        return remote(src, vectors.at[zo, x], v_send.at[4 + k], v_recv.at[4 + k], device(z, 1 - x, y, c))
+
+    def each(lo, hi, body):
+        def step(k, carry):
+            body(k)
+            return carry
+        lax.fori_loop(lo, hi, step, 0)
+
+    vectors[z, x] = vector[...]
+    for k in (1, 2, 3):
+        vector_copy(0, k).start()
+    vector_copy(1, 0).start()
+    for t in range(n):
+        copy(2, t, 0).start()
+        copy(3, t, 0).start()
+    def spread(k):
+        for t in range(n):
+            copy(0, t, k).start()
+            copy(1, t, k).start()
+    each(1, 4, spread)
+    for t in range(n):
+        own(t).start()
+    for k in (1, 2, 3):
+        vector_copy(0, k).wait_recv()
+        vector_copy(1, k).start()
+
+    def along_x(k):
+        for t in range(n):
+            copy(0, t, k).wait_recv()
+            copy(2, t, k).start()
+            copy(1, t, k).wait_recv()
+            copy(3, t, k).start()
+    each(1, 4, along_x)
+
+    for t in range(n):
+        own(t).wait()
+        copy(3, t, 0).wait_recv()
+        copy(4, t, 0).start()
+    def along_y(k):
+        for t in range(n):
+            copy(3, t, k).wait_recv()
+            copy(4, t, k).start()
+    each(1, 4, along_y)
+
+    for t in range(n):
+        copy(2, t, 0).wait_recv()
+        copy(4, t, 0).wait_recv()
+        copy(5, t, 0).start()
+    def across(k):
+        for t in range(n):
+            copy(2, t, k).wait_recv()
+            copy(4, t, k).wait_recv()
+            copy(5, t, k).start()
+    each(1, 4, across)
+
+    for t in range(n):
+        for stage in (2, 3, 4, 5):
+            copy(stage, t, 0).wait_send()
+        copy(5, t, 0).wait_recv()
+    def finish(k):
+        for t in range(n):
+            for stage in range(6):
+                copy(stage, t, k).wait_send()
+            copy(5, t, k).wait_recv()
+    each(1, 4, finish)
+    vector_copy(1, 0).wait()
+    for k in (1, 2, 3):
+        vector_copy(0, k).wait_send()
+        vector_copy(1, k).wait()
+
+
+def gather_weights(shards, vector, ident):
+    n = len(shards)
+    views, widths = [], []
+    for shard in shards:
+        rows, total = shard.shape
+        views.append(shard.reshape(2, rows // 2, total))
+        widths.append((total // 256 + 1) // 3 * 128)
+    anywhere, vmem = pl.BlockSpec(memory_space=pl.ANY), pl.BlockSpec(memory_space=pltpu.VMEM)
+    dma = pltpu.SemaphoreType.DMA
+    out = pl.pallas_call(
+        functools.partial(gather_kernel, tuple(widths), n),
+        out_shape=tuple(jax.ShapeDtypeStruct((4, 2) + v.shape, BF16) for v in views)
+        + (jax.ShapeDtypeStruct((4, 2, 8, 128), F32),),
+        in_specs=[anywhere] * n + [vmem],
+        out_specs=(anywhere,) * n + (vmem,),
+        scratch_shapes=[dma((n, 6, 4)), dma((n, 6, 4)), dma((n,)), dma((8,)), dma((8,))],
+        compiler_params=pltpu.CompilerParams(collective_id=ident, has_side_effects=True),
+        name="gather",
+    )(*views, vector.reshape(8, 128))
+    return [o.reshape(-1, o.shape[4]) for o in out[:n]], out[n].reshape(-1)
 
 
 def layer_norm(stream, gain, offset):
@@ -449,17 +785,19 @@
         second_decoder_down,
         second_vectors,
     )
-    w_embed, w_enc, w_enc_down, w_dec, w_dec_down, gathered_vectors = (
-        lax.all_gather(patch_embed.astype(jnp.bfloat16), "clip", axis=0, tiled=True),
-        lax.all_gather(encoder_in.astype(jnp.bfloat16), "clip", axis=0, tiled=True),
-        lax.all_gather(encoder_down.astype(jnp.bfloat16), "clip", axis=0, tiled=True),
-        lax.all_gather(decoder_in.astype(jnp.bfloat16), "clip", axis=0, tiled=True),
-        lax.all_gather(decoder_down.astype(jnp.bfloat16), "clip", axis=0, tiled=True),
-        lax.all_gather(norm_vectors.astype(jnp.bfloat16), "clip", axis=0, tiled=True),
-    )
+    direct = lax.axis_size("clip") == 8 and lax.axis_size("band") == 4
+    low_shards = [master.astype(jnp.bfloat16) for master in masters]
+    if direct:
+        (w_embed, w_enc, w_enc_down, w_dec, w_dec_down), vectors = gather_weights(
+            low_shards[:5], lax.reduce_precision(norm_vectors, exponent_bits=8, mantissa_bits=7), 0
+        )
+    else:
+        w_embed, w_enc, w_enc_down, w_dec, w_dec_down, gathered_vectors = (
+            lax.all_gather(shard, "clip", axis=0, tiled=True) for shard in low_shards
+        )
+        vectors = gathered_vectors.astype(jnp.float32)
     enc_width, dec_width = (w_enc.shape[0], w_dec.shape[0])
     enc_hidden, dec_hidden = (w_enc_down.shape[0], w_dec_down.shape[0])
-    vectors = gathered_vectors.astype(jnp.float32)
     enc_gains = vectors[: 6 * enc_width].reshape(6, enc_width)
     dec_gains = vectors[6 * enc_width :].reshape(7, dec_width)
     enc_weights = (
@@ -530,29 +868,26 @@
             g_dec_vectors.reshape(-1),
         ]
     )
-    shard_grads = (
-        lax.psum_scatter(g_embed, "clip", scatter_dimension=0, tiled=True),
-        lax.psum_scatter(g_enc_in, "clip", scatter_dimension=0, tiled=True),
-        lax.psum_scatter(g_enc_mats[3], "clip", scatter_dimension=0, tiled=True),
-        lax.psum_scatter(g_dec_in, "clip", scatter_dimension=0, tiled=True),
-        lax.psum_scatter(g_dec_down, "clip", scatter_dimension=0, tiled=True),
-        lax.psum_scatter(g_vectors, "clip", scatter_dimension=0, tiled=True),
-    )
-    reduced = lax.psum(
-        (
-            shard_grads[0],
-            shard_grads[1],
-            shard_grads[2],
-            shard_grads[3],
-            shard_grads[4],
-            shard_grads[5],
-        ),
-        "band",
-    )
+    if direct:
+        small = jnp.concatenate([g_vectors.reshape(-1, 128), jnp.full((8, 128), local_loss)])
+        dec_shards, _ = reduce_grads([g_dec_in, g_dec_down], small[:8], 1)
+        enc_shards, summed = reduce_grads([g_embed, g_enc_in, g_enc_mats[3]], small, 2)
+        rows = norm_vectors.shape[0]
+        own = lax.dynamic_slice(summed[:-8].reshape(-1), (lax.axis_index("clip") * rows,), (rows,))
+        reduced = (*enc_shards, *dec_shards, own)
+        loss_sum = summed[-1, 0]
+    else:
+        reduced = lax.psum(
+            tuple(
+                lax.psum_scatter(grad, "clip", scatter_dimension=0, tiled=True)
+                for grad in (g_embed, g_enc_in, g_enc_mats[3], g_dec_in, g_dec_down, g_vectors)
+            ),
+            "band",
+        )
+        loss_sum = lax.psum(local_loss, ("clip", "band"))
     squares = jnp.zeros((), jnp.float32)
     for grad in reduced:
         squares = squares + jnp.sum(grad * grad)
-    loss_sum = lax.psum(local_loss, ("clip", "band"))
     norm_squared = lax.psum(squares, "clip")
     grad_norm = jnp.sqrt(norm_squared)
     factor = jnp.minimum(1.0, CLIP_LIMIT / (grad_norm + 1e-06))

time: 1730 us -> 969 us (0.56)
  waiting for transfers between devices: 1070 us -> 0 us
  Pallas kernels: 196 us -> 647 us
  blocking collectives: 163 us -> 36.9 us
    reduce_scatter x5 -> x0, waiting for transfers between devices: 782 us -> none  [the longest x1 339 us: shards(): lax.psum_scatter(g_enc_in, 'clip', scatter_dimension=0, tiled=True)]
    pallas_call x0 -> x3, Pallas kernels: none -> 451 us  [the longest x2 297 us: reduce_grads(): pl.pallas_call(functools.partial(reduce_kernel, tuple(widths), n), out_sh...]
    all_gather x4 -> x0, waiting for transfers between devices: 228 us -> none  [the longest x1 142 us: shards(): lax.all_gather(encoder_in.astype(jnp.bfloat16), 'clip', axis=0, tiled=True)]
    psum x1 -> x0, waiting for transfers between devices: 62.8 us -> none  [shards(): lax.psum((shard_grads[0], shard_grads[1], shard_grads[2], shard_grads[3],...]
    all_gather x2 -> x0, blocking collectives: 60 us -> none  [the longest x1 32.1 us: shards(): lax.all_gather(patch_embed.astype(jnp.bfloat16), 'clip', axis=0, tiled=True)]
    psum x2 -> x0, blocking collectives: 46.5 us -> none  [the longest x1 40 us: shards(): loss_sum = lax.psum(local_loss, ('clip', 'band'))]
    unnamed x1 -> x0, blocking collectives: 35.2 us -> none
  transfers between devices with their start and end apart: 10 -> 0, of which waited for: 9 -> 0; matrix products, arithmetic and copies ran while one was open for 6% -> 0% of each run, Pallas kernels for 0% -> 0%
where the time goes in v2:
time: 969 us; the launch traced here: 959 us
  Pallas kernels  647 us (67%)
  matrix products  166 us (17%)
  other arithmetic  55.9 us (6%)
  local copies, waits for them, and re-layouts  45.1 us (5%)
  blocking collectives  36.9 us (4%)
    pallas_call x2, Pallas kernels, reduce_grads(): pl.pallas_call(functools.partial(reduce_kernel, tuple(widths), n), out_sh...  297 us
    pallas_call x1, Pallas kernels, decoder_step(): pl.pallas_call(functools.partial(decoder_kernel, coef, heads), out_shape=...  196 us
    pallas_call x1, Pallas kernels, gather_weights(): pl.pallas_call(functools.partial(gather_kernel, tuple(widths), n), out_sh...  154 us
    psum x1, blocking collectives, shards(): norm_squared = lax.psum(squares, 'clip')  36.9 us
    dot_general x1, matrix products, attend_back(): jnp.einsum('bhqk,bqhd->bkhd', scaled, query, preferred_element_type=jnp.f...  27.7 us
    dot_general x1, matrix products, attend_back(): jnp.einsum('bhqk,bkhd->bqhd', scaled, key_rows, preferred_element_type=jn...  27.5 us
    dot_general x5, matrix products, input_grad(): lax.dot_general(grad_low, weights_in, (((1,), (1,)), ((), ())), preferred...  27.4 us
    dot_general x6, matrix products, weight_grad(): lax.dot_general(values_in, grad_low, (((0,), (0,)), ((), ())), preferred_...  23.6 us

profile of v2, /device:TPU:0, one launch (start us, length us, event | category | flops | bytes accessed | tf_op | source)
XLA Modules:
  0.0 958.6 jit_solution(15708140536893745994)
XLA Ops:
  4.6 5.6 multiply_sine_fusion.1
  10.3 3.9 gather_fusion
  19.8 153.9 %gather.13 = (bf16[4,2,2,16,768]{4,3,2,1,0:T(8,128)(2,1)}, bf16[4,2,2,48,6656]{4,3,2,1,0:T(8,128)(2,1)}, bf16[4,2,2,192,768]{4,3,2,1,0:T(8,128)(2,1)}, bf16[4,2,...) custom-call(bf16[2,16,768]{2,1,0:T(8,128)(2,1)} %bitcast.189, ...), custom_call_target="tpu_custom_call" | custom-call | tf_op jit(solution)/shard_map/gather/pallas_call | solution.py:598
  176.5 5.9 convolution_convert_fusion
  182.4 4.5 copy.71
  187.1 10.2 %fusion.118 = (f32[12,576]{1,0:T(8,128)S(1)}, f32[12,576,576]{1,2,0:T(8,128)}) fusion(f32[576,576]{0,1:T(8,128)S(1)} %compare_select_fusion, bf16[1,576,3,12,64]{1,4,3,2,0:T(8,128)(2,1)} %bitcast.171), kind=kOutput, calls=%fused_computation.236 | convolution fusion | flops 525533760 | bytes 19246080 | tf_op jit(solution)/shard_map/sub | solution.py:664
  197.2 8.0 fusion.36
  208.3 6.2 fusion.29
  214.6 4.3 fusion.120
  230.9 6.7 copy.74
  243.0 196.1 %decoder.1 = (f32[512,4352]{1,0:T(8,128)}, f32[2048,512]{1,0:T(8,128)}, f32[7,512,128]{2,1,0:T(8,128)}, f32[640,512]{1,0:T(8,128)}, f32[8,128]{1,0:T(8,128)}) custom-call(s32[6]{0:T(128)} %slice.103.shift_ref, s32[640,128]{1,0:T(8,128)} %broadcast_in_dim.39.rvis_ref, bf16[512,640]{1,0:T(8,128)(2,1)} %pad_bitcast_fusion.gvt_ref, bf16[3072,256]{1,0:T(8,128)(2,1)} %bitcast.170, ...), custom_call_target="tpu_custom_call" | custom-call | tf_op jit(solution)/shard_map/decoder/pallas_call | solution.py:252
  443.7 11.3 %fusion.16 = bf16[576,3072]{1,0:T(8,128)(2,1)S(1)} fusion(f32[576,3072]{1,0:T(8,128)} %copy-done.81, bf16[3072,768]{1,0:T(8,128)(2,1)} %bitcast.206, f32[576,768]{1,0:T(8,128)S(1)} %get-tuple-element.93, f32[576]{0:T(1024)S(1)} %negate_multiply_fusion.2), kind=kOutput, calls=%fused_computation.23 | convolution fusion | flops 2754183168 | bytes 17107200 | tf_op jit(solution)/shard_map/dot_general | solution.py:644
  464.5 9.7 %fusion.66 = f32[12,576,576]{1,2,0:T(8,128)} fusion(bf16[576,12,64]{0,2,1:T(8,128)(2,1)S(1)} %bitcast.180, bf16[1,576,3,12,64]{1,4,3,2,0:T(8,128)(2,1)} %bitcast.173), kind=kOutput, calls=%fused_computation.99 | convolution fusion | flops 509607936 | bytes 17793024 | tf_op jit(solution)/shard_map/bqhd,bkhd->bhqk/dot_general | solution.py:683
  474.2 27.5 %fusion.52 = bf16[1,576,1,12,64]{1,4,3,2,0:T(8,128)(2,1)} fusion(f32[12,576,576]{1,2,0:T(8,128)} %fusion.66, bf16[1,576,3,12,64]{1,4,3,2,0:T(8,128)(2,1)} %bitcast.174, f32[12,576,576]{1,2,0:T(8,128)} %get-tuple-element.127, f32[12,576]{1,0:T(8,128)S(1)} %get-tuple-element.126), kind=kOutput, calls=%fused_computation.78 | convolution fusion | flops 537926976 | bytes 72728576 | tf_op jit(solution)/shard_map/bhqk,bkhd->bqhd/dot_general | solution.py:694
  501.7 27.7 %fusion.49 = bf16[1,576,1,12,64]{1,4,3,2,0:T(8,128)(2,1)} fusion(f32[12,576,576]{1,2,0:T(8,128)} %fusion.66, bf16[1,576,3,12,64]{1,4,3,2,0:T(8,128)(2,1)} %bitcast.175, f32[12,576,576]{1,2,0:T(8,128)} %get-tuple-element.127, f32[12,576]{1,0:T(8,128)S(1)} %get-tuple-element.126), kind=kOutput, calls=%fused_computation.77 | convolution fusion | flops 537926976 | bytes 72728576 | tf_op jit(solution)/shard_map/bhqk,bqhd->bkhd/dot_general | solution.py:695
  529.4 8.9 fusion.55
  539.8 6.8 multiply_reduce_fusion.4
  549.8 94.2 %reduce.17 = (f32[2,32,4352]{2,1,0:T(8,128)}, f32[2,128,512]{2,1,0:T(8,128)}, f32[8,128]{1,0:T(8,128)}) custom-call(f32[4,2,2,32,4352]{4,3,2,1,0:T(8,128)} %bitcast.166, f32[4,2,2,128,512]{4,3,2,1,0:T(8,128)} %bitcast.177, f32[8,128]{1,0:T(8,128)} %slice.140.refs_2_), custom_call_target="tpu_custom_call" | custom-call | tf_op jit(solution)/shard_map/reduce/pallas_call | solution.py:460
  654.8 12.2 %fusion.98 = f32[3072,768]{1,0:T(8,128)} fusion(f32[576,768]{1,0:T(8,128)} %copy-done.14, f32[576]{0:T(1024)} %copy-done.70, f32[576,3072]{1,0:T(8,128)} %copy-done.81), kind=kOutput, calls=%fused_computation.227 | convolution fusion | flops 2734718976 | bytes 18286848 | tf_op jit(solution)/shard_map/dot_general | solution.py:650
  672.4 4.4 fusion.101
  677.9 7.6 pad_maximum_fusion
  688.1 202.5 %reduce.16 = (f32[2,16,768]{2,1,0:T(8,128)}, f32[2,48,6656]{2,1,0:T(8,128)}, f32[2,192,768]{2,1,0:T(8,128)}, f32[72,128]{1,0:T(8,128)}) custom-call(f32[4,2,2,16,768]{4,3,2,1,0:T(8,128)} %bitcast.182, f32[4,2,2,48,6656]{4,3,2,1,0:T(8,128)} %bitcast.160, f32[4,2,2,192,768]{4,3,2,1,0:T(8,128)} %bitcast.165, f32[72,128]{1,0:T(8,128)} %concatenate.27.refs_3_), custom_call_target="tpu_custom_call" | custom-call | tf_op jit(solution)/shard_map/reduce/pallas_call | solution.py:460
  900.6 36.9 %psum.7 = f32[]{:T(128)} all-reduce(f32[]{:T(128)S(6)} %add.327), channel_id=1, replica_groups=mesh['clip'=8,'band'=4] {'clip'}, use_global_device_ids=true, to_apply=%region_39.40 | all-reduce | flops 1 | bytes 8 | tf_op jit(solution)/shard_map/psum | solution.py:891
  951.4 4.5 multiply_subtract_fusion
  (279 shorter events, 91.4 us)
Async XLA Ops:
  14.2 159.5 %copy-start.27 = (bf16[576,256]{1,0:T(8,128)(2,1)}, bf16[576,256]{1,0:T(8,128)(2,1)S(1)}, u32[]{:S(2)}) copy-start(bf16[576,256]{1,0:T(8,128)(2,1)S(1)} %gather_fusion) | copy-start | bytes 884740
  17.8 155.9 %copy-start.31 = (f32[576,192]{1,0:T(8,128)S(1)}, f32[576,192]{1,0:T(8,128)}, u32[]{:S(2)}) copy-start(f32[576,192]{1,0:T(8,128)} %get-tuple-element.105) | copy-start | bytes 1327108
  175.7 29.6 %copy-start.2 = (f32[576,768]{1,0:T(8,128)}, f32[576,768]{1,0:T(8,128)S(1)}, u32[]{:S(2)}) copy-start(f32[576,768]{1,0:T(8,128)S(1)} %get-tuple-element.125) | copy-start | bytes 5308420
  176.4 45.2 %copy-start.71 = (f32[768]{0:T(1024)}, f32[768]{0:T(1024)S(1)}, u32[]{:S(2)}) copy-start(f32[768]{0:T(1024)S(1)} %get-tuple-element.97) | copy-start | bytes 9220
  176.5 266.4 %copy-start.61 = (f32[768]{0:T(1024)}, f32[768]{0:T(1024)S(1)}, u32[]{:S(2)}) copy-start(f32[768]{0:T(1024)S(1)} %get-tuple-element.96) | copy-start | bytes 9220
  218.9 224.0 %copy-start.53 = (f32[576]{0:T(1024)}, f32[576]{0:T(1024)S(1)}, u32[]{:S(2)}) copy-start(f32[576]{0:T(1024)S(1)} %broadcast_multiply_fusion.5) | copy-start | bytes 6916
  219.3 223.6 %copy-start.66 = (f32[576]{0:T(1024)}, f32[576]{0:T(1024)S(1)}, u32[]{:S(2)}) copy-start(f32[576]{0:T(1024)S(1)} %fusion.86) | copy-start | bytes 6916
  442.9 12.1 %slice-start = ((s8[10223616]{0:T(1024)(128)(4,1)}), s8[4194304]{0:T(1024)(128)(4,1)S(1)}, s32[]{:S(2)}) async-start(s8[10223616]{0:T(1024)(128)(4,1)} %bitcast.196), calls=%async_computation | async-start | bytes 8388608
  443.6 15.9 %copy-start.14 = (f32[576,768]{1,0:T(8,128)}, f32[576,768]{1,0:T(8,128)S(1)}, u32[]{:S(2)}) copy-start(f32[576,768]{1,0:T(8,128)S(1)} %get-tuple-element.93) | copy-start | bytes 5308420
  443.6 15.9 %copy-start.70 = (f32[576]{0:T(1024)}, f32[576]{0:T(1024)S(1)}, u32[]{:S(2)}) copy-start(f32[576]{0:T(1024)S(1)} %negate_multiply_fusion.2) | copy-start | bytes 6916
  443.7 11.3 %copy-start.1 = (f32[576,768]{1,0:T(8,128)S(1)}, f32[576,768]{1,0:T(8,128)}, u32[]{:S(2)}) copy-start(f32[576,768]{1,0:T(8,128)} %copy-done) | copy-start | bytes 5308420
  443.7 11.3 %slice-start.1 = ((s8[10223616]{0:T(1024)(128)(4,1)}), s8[4194304]{0:T(1024)(128)(4,1)S(1)}, s32[]{:S(2)}) async-start(s8[10223616]{0:T(1024)(128)(4,1)} %bitcast.196), calls=%async_computation.1 | async-start | bytes 8388608
  443.7 11.3 %slice-start.2 = ((s8[10223616]{0:T(1024)(128)(4,1)}), s8[1835008]{0:T(1024)(128)(4,1)S(1)}, s32[]{:S(2)}) async-start(s8[10223616]{0:T(1024)(128)(4,1)} %bitcast.196), calls=%async_computation.2 | async-start | bytes 3670016
  654.7 12.2 %copy-start.26 = (bf16[1,576,3,12,64]{1,4,3,2,0:T(8,128)(2,1)S(1)}, bf16[1,576,3,12,64]{1,4,3,2,0:T(8,128)(2,1)}, u32[]{:S(2)}) copy-start(bf16[1,576,3,12,64]{1,4,3,2,0:T(8,128)(2,1)} %copy-done.25) | copy-start | bytes 7962628
  654.7 12.2 %copy-start.52 = (f32[576]{0:T(1024)S(1)}, f32[576]{0:T(1024)}, u32[]{:S(2)}) copy-start(f32[576]{0:T(1024)} %copy-done.50) | copy-start | bytes 6916
  654.7 12.2 %copy-start.60 = (f32[768]{0:T(1024)S(1)}, f32[768]{0:T(1024)}, u32[]{:S(2)}) copy-start(f32[768]{0:T(1024)} %copy-done.58) | copy-start | bytes 9220
  654.7 12.2 %copy-start.65 = (f32[576]{0:T(1024)S(1)}, f32[576]{0:T(1024)}, u32[]{:S(2)}) copy-start(f32[576]{0:T(1024)} %copy-done.63) | copy-start | bytes 6916
  654.7 12.2 %copy-start.74 = (f32[768]{0:T(1024)S(1)}, f32[768]{0:T(1024)}, u32[]{:S(2)}) copy-start(f32[768]{0:T(1024)} %copy-done.73) | copy-start | bytes 9220
  890.6 47.6 %copy-start.69 = (f32[1024]{0:T(1024)S(1)}, f32[1024]{0:T(1024)}, u32[]{:S(2)}) copy-start(f32[1024]{0:T(1024)} %param.31) | copy-start | bytes 12292
  890.6 47.6 %copy-start.78 = (f32[1024]{0:T(1024)S(1)}, f32[1024]{0:T(1024)}, u32[]{:S(2)}) copy-start(f32[1024]{0:T(1024)} %param.37) | copy-start | bytes 12292
  890.6 47.6 %copy-start.79 = (f32[1024]{0:T(1024)S(1)}, f32[1024]{0:T(1024)}, u32[]{:S(2)}) copy-start(f32[1024]{0:T(1024)} %param.43) | copy-start | bytes 12292
  893.7 45.1 %copy-start.33 = (f32[256,512]{1,0:T(8,128)S(1)}, f32[256,512]{1,0:T(8,128)}, u32[]{:S(2)}) copy-start(f32[256,512]{1,0:T(8,128)} %param.30) | copy-start | bytes 1572868
  893.7 45.2 %copy-start.42 = (f32[256,512]{1,0:T(8,128)S(1)}, f32[256,512]{1,0:T(8,128)}, u32[]{:S(2)}) copy-start(f32[256,512]{1,0:T(8,128)} %param.36) | copy-start | bytes 1572868
  893.7 45.2 %copy-start.43 = (f32[256,512]{1,0:T(8,128)S(1)}, f32[256,512]{1,0:T(8,128)}, u32[]{:S(2)}) copy-start(f32[256,512]{1,0:T(8,128)} %param.42) | copy-start | bytes 1572868
  (63 other events, 262.5 us)

commit v3 on v1

--- a/solution.py
+++ b/solution.py
@@ -270,6 +270,472 @@
         compiler_params=pltpu.CompilerParams(vmem_limit_bytes=63 * 2**20),
         name="decoder",
     )(shift, rvis, gvt, pix, et, ef, vec, w, wt, wd, wdt)
+
+
+def place():
+    clip, band = lax.axis_index("clip"), lax.axis_index("band")
+    return clip // 2, clip % 2, band // 2, band % 2
+
+
+def device(z, x, y, c):
+    return (z * 2 + x, y * 2 + c)
+
+
+def greet(z, x, y, c):
+    barrier = pltpu.get_barrier_semaphore()
+    others = [device(z, x, y, 1 - c), device(z, 1 - x, y, c), device(z, x, 1 - y, c)]
+    others += [device((z + k) % 4, x, y, c) for k in (1, 2, 3)]
+    for other in others:
+        pl.semaphore_signal(barrier, inc=1, device_id=other, device_id_type=pl.DeviceIdType.MESH)
+    pl.semaphore_wait(barrier, len(others))
+
+
+def remote(src, dst, send, recv, to):
+    return pltpu.make_async_remote_copy(
+        src_ref=src, dst_ref=dst, send_sem=send, recv_sem=recv, device_id=to, device_id_type=pl.DeviceIdType.MESH
+    )
+
+
+def reduce_kernel(widths, n, *refs):
+    grads, small, before = refs[:n], refs[n], refs[n + 1]
+    outs, small_out, squares = refs[n + 2 : 2 * n + 2], refs[2 * n + 2], refs[2 * n + 3]
+    rest = refs[2 * n + 4 :]
+    sums, r0 = rest[:n], rest[n : 2 * n]
+    coded = {1 + i: rest[(2 + i) * n : (3 + i) * n] for i in range(5)}
+    came = {1 + i: rest[(7 + i) * n : (8 + i) * n] for i in range(5)}
+    step_out = {1 + i: rest[(12 + i) * n : (13 + i) * n] for i in range(5)}
+    step_in = {1 + i: rest[(17 + i) * n : (18 + i) * n] for i in range(5)}
+    s_buf, s_sum, q_buf, q_sum, send, recv, near, t_send, t_recv, s_send, s_recv = rest[22 * n :]
+    z, x, y, c = place()
+    greet(z, x, y, c)
+
+    def at_z(k):
+        return (z + k) % 4
+
+    def columns(t, core):
+        half = sums[t].shape[4]
+        return pl.ds(pl.multiple_of(core * half, 128), half)
+
+    def local(t, k):
+        zk = at_z(k)
+        return pltpu.make_async_copy(grads[t].at[zk, :, :, :, columns(t, c)], sums[t].at[zk], near.at[t, k])
+
+    def target(stage, k):
+        return {
+            1: lambda: device(z, 1 - x, y, c),
+            2: lambda: device(z, x, 1 - y, c),
+            3: lambda: device(z, x, 1 - y, c),
+            4: lambda: device(z, 1 - x, y, c),
+            5: lambda: device(at_z(k), x, y, c),
+        }[stage]()
+
+    def copy(stage, t, k):
+        if stage == 0:
+            src, dst, to = grads[t].at[at_z(k), :, :, :, columns(t, 1 - c)], r0[t].at[at_z(k)], device(z, x, y, 1 - c)
+        elif stage == 6:
+            src, dst, to = sums[t].at[z, x, y], outs[t].at[y, :, columns(t, c)], device(z, x, 1 - y, c)
+        elif stage == 7:
+            src = outs[t].at[:, :, columns(t, c)]
+            dst, to = src, device(z, x, y, 1 - c)
+        else:
+            src, dst, to = coded[stage][t].at[k], came[stage][t].at[k], target(stage, k)
+        return remote(src, dst, send.at[t, stage, k], recv.at[t, stage, k], to)
+
+    def steps(stage, t, k):
+        src, dst = step_out[stage][t].at[k], step_in[stage][t].at[k]
+        return remote(src, dst, t_send.at[t, stage, k], t_recv.at[t, stage, k], target(stage, k))
+
+    def keep(t):
+        return pltpu.make_async_copy(sums[t].at[z, x, y], outs[t].at[y, :, columns(t, c)], near.at[t, 4])
+
+    def each(lo, hi, body):
+        def one(k, carry):
+            body(k)
+            return carry
+        lax.fori_loop(lo, hi, one, 0)
+
+    def slab(i, height):
+        return pl.ds(pl.multiple_of(i * height, height), height)
+
+    def part(stage, t):
+        w = widths[t]
+        return slice(0, w) if stage in (1, 3) else slice(w, None) if stage in (2, 4) else slice(None)
+
+    def encode(stage, t, k, parts, read):
+        rows = sums[t].shape[3]
+        zk, width = at_z(k), coded[stage][t].shape[-1]
+        block = lambda p: coded[stage][t].at[(k, p) if parts > 1 else k]
+        per = rows // 8
+        def peak(i, most):
+            return jnp.maximum(most, jnp.abs(read(zk, i // per, slab(i % per, 8))))
+        most = lax.fori_loop(0, parts * per, peak, jnp.zeros((8, width), F32))
+        most = jnp.maximum(jnp.max(most, axis=0, keepdims=True), 1e-30)
+        step_out[stage][t][k] = most * (1.0 / 32767.0)
+        steps(stage, t, k).start()
+        scale = 32767.0 / most
+        half = rows // 16
+        def one(i):
+            values = jnp.round(read(zk, i // half, slab(i % half, 16)) * scale).astype(jnp.int32).astype(jnp.int16)
+            block(i // half)[slab(i % half, 16)] = values
+        each(0, parts * half, one)
+        copy(stage, t, k).start()
+
+    def landed(stage, t, k):
+        steps(stage, t, k).wait_recv()
+        copy(stage, t, k).wait_recv()
+
+    def decoded(stage, t, k, p, rows, parts):
+        values = came[stage][t][(k, p, rows) if parts > 1 else (k, rows)]
+        return values.astype(jnp.int32).astype(F32) * step_in[stage][t][k]
+
+    order = (2, 1, 3, 0)
+    for t in range(n):
+        for k in order:
+            copy(0, t, k).start()
+            local(t, k).start()
+
+    def hop(total, buffer, first, stage, to):
+        return remote(total, buffer.at[stage], s_send.at[first + stage], s_recv.at[first + stage], to)
+
+    def advance(total, buffer, first, stage):
+        neighbours = (device(z, x, y, 1 - c), device(z, 1 - x, y, c), device(z, x, 1 - y, c))
+        if stage:
+            hop(total, buffer, first, stage - 1, neighbours[stage - 1]).wait()
+            total[...] += buffer[stage - 1]
+        if stage < 3:
+            hop(total, buffer, first, stage, neighbours[stage]).start()
+        else:
+            for k in (1, 2, 3):
+                last_hop(total, buffer, first, k).start()
+            buffer[3 + z] = total[...]
+
+    def last_hop(total, buffer, first, k):
+        return remote(total, buffer.at[3 + z], s_send.at[first + 2 + k], s_recv.at[first + 2 + k], device(at_z(k), x, y, c))
+
+    def finish_sum(total, buffer, first, out):
+        for k in (1, 2, 3):
+            last_hop(total, buffer, first, k).wait()
+        out[...] = (buffer[3] + buffer[4]) + (buffer[5] + buffer[6])
+
+    s_sum[...] = small[...]
+
+    def first_sum(t, k):
+        zk = at_z(k)
+        copy(0, t, k).wait_recv()
+        local(t, k).wait()
+        per = sums[t].shape[3] // 16
+        def one(i):
+            p, r = i // per, slab(i % per, 16)
+            sums[t][zk, p // 2, p % 2, r] += r0[t][zk, p // 2, p % 2, r]
+        each(0, 4 * per, one)
+        encode(1, t, k, 2, lambda zk, p, r: sums[t][zk, 1 - x, p, r, part(1, t)])
+        encode(2, t, k, 2, lambda zk, p, r: sums[t][zk, p, 1 - y, r, part(2, t)])
+
+    def second_sum(t, k):
+        zk = at_z(k)
+        per = sums[t].shape[3] // 16
+        landed(1, t, k)
+        def one(i):
+            p, r = i // per, slab(i % per, 16)
+            sums[t][zk, x, p, r, part(1, t)] += decoded(1, t, k, p, r, 2)
+        each(0, 2 * per, one)
+        encode(3, t, k, 1, lambda zk, p, r: sums[t][zk, x, 1 - y, r, part(3, t)])
+        landed(2, t, k)
+        def two(i):
+            p, r = i // per, slab(i % per, 16)
+            sums[t][zk, p, y, r, part(2, t)] += decoded(2, t, k, p, r, 2)
+        each(0, 2 * per, two)
+        encode(4, t, k, 1, lambda zk, p, r: sums[t][zk, 1 - x, y, r, part(4, t)])
+
+    def third_sum(t, k):
+        zk = at_z(k)
+        landed(3, t, k)
+        landed(4, t, k)
+        def one(i):
+            r = slab(i, 16)
+            sums[t][zk, x, y, r, part(3, t)] += decoded(3, t, k, 0, r, 1)
+            sums[t][zk, x, y, r, part(4, t)] += decoded(4, t, k, 0, r, 1)
+        each(0, sums[t].shape[3] // 16, one)
+        if k:
+            encode(5, t, k, 1, lambda zk, p, r: sums[t][zk, x, y, r])
+
+    def last_sum(t, total):
+        for k in (1, 2, 3):
+            landed(5, t, k)
+        half = sums[t].shape[4]
+        def one(i, acc):
+            r = slab(i, 16)
+            value = sums[t][z, x, y, r]
+            for k in (1, 2, 3):
+                value = value + decoded(5, t, k, 0, r, 1)
+            sums[t][z, x, y, r] = value
+            value = value * value
+            value = value[:8] + value[8:]
+            for j in range(half // 128):
+                acc = acc + value[:, 128 * j : 128 * j + 128]
+            return acc
+        total = lax.fori_loop(0, sums[t].shape[3] // 16, one, total)
+        copy(6, t, 0).start()
+        keep(t).start()
+        return total
+
+    def share(t):
+        copy(6, t, 0).wait_recv()
+        keep(t).wait()
+        copy(7, t, 0).start()
+
+    blocks = [(t, k) for t in range(n) for k in order]
+    total = before[...]
+    for i in range(len(blocks) + 2):
+        if i < len(blocks):
+            first_sum(*blocks[i])
+        if 0 <= i - 1 < len(blocks):
+            second_sum(*blocks[i - 1])
+        if 0 <= i - 2:
+            third_sum(*blocks[i - 2])
+        if i < 4:
+            advance(s_sum, s_buf, 0, i)
+        for t in range(n - 1):
+            if i == 4 * t + 7:
+                total = last_sum(t, total)
+            if i == 4 * t + 9:
+                share(t)
+    total = last_sum(n - 1, total)
+    finish_sum(s_sum, s_buf, 0, small_out)
+    late = [t for t in range(n) if t == n - 1 or 4 * t + 9 >= len(blocks) + 2]
+    for t in late[:-1]:
+        share(t)
+    q_sum[...] = total
+    if q_buf.shape[0] > 1:
+        for stage in range(4):
+            advance(q_sum, q_buf, 6, stage)
+        finish_sum(q_sum, q_buf, 6, squares)
+    else:
+        squares[...] = total
+    share(late[-1])
+
+    def finish(k):
+        for t in range(n):
+            copy(0, t, k).wait_send()
+            for stage in range(1, 5):
+                copy(stage, t, k).wait_send()
+                steps(stage, t, k).wait_send()
+    each(0, 4, finish)
+    def finish_z(k):
+        for t in range(n):
+            copy(5, t, k).wait_send()
+            steps(5, t, k).wait_send()
+    each(1, 4, finish_z)
+    for t in range(n):
+        copy(6, t, 0).wait_send()
+        copy(7, t, 0).wait()
+
+
+def reduce_grads(grads, small, before, last, ident):
+    n = len(grads)
+    views, widths = [], []
+    scratch = [[] for _ in range(22)]
+    f = lambda *s: pltpu.VMEM(s, F32)
+    q = lambda *s: pltpu.VMEM(s, jnp.int16)
+    for grad in grads:
+        rows, cols = grad.shape
+        r2, half = rows // 16, cols // 2
+        w = (half // 128 * 7 + 5) // 10 * 128
+        views.append(grad.reshape(4, 2, 2, r2, cols))
+        widths.append(w)
+        blocks = [(4, 2, r2, w), (4, 2, r2, half - w), (4, r2, w), (4, r2, half - w), (4, r2, half)]
+        for i, s in enumerate([f(4, 2, 2, r2, half)] * 2 + [q(*b) for b in blocks * 2] + [f(4, 1, b[-1]) for b in blocks * 2]):
+            scratch[i].append(s)
+    anywhere, vmem = pl.BlockSpec(memory_space=pl.ANY), pl.BlockSpec(memory_space=pltpu.VMEM)
+    dma = pltpu.SemaphoreType.DMA
+    square = jax.ShapeDtypeStruct((8, 128), F32)
+    out = pl.pallas_call(
+        functools.partial(reduce_kernel, tuple(widths), n),
+        out_shape=tuple(jax.ShapeDtypeStruct((2, v.shape[3], v.shape[4]), F32) for v in views)
+        + (jax.ShapeDtypeStruct(small.shape, F32), square),
+        in_specs=[anywhere] * n + [vmem] * 2,
+        out_specs=(anywhere,) * n + (vmem,) * 2,
+        scratch_shapes=sum(scratch, []) + [
+            f(7, *small.shape), f(*small.shape), f(7 if last else 1, 8, 128), f(8, 128),
+            dma((n, 8, 4)), dma((n, 8, 4)), dma((n, 5)), dma((n, 6, 4)), dma((n, 6, 4)), dma((12,)), dma((12,)),
+        ],
+        compiler_params=pltpu.CompilerParams(
+            collective_id=ident, has_side_effects=True, vmem_limit_bytes=60 * 2**20
+        ),
+        name="reduce",
+    )(*views, small, before)
+    return [o.reshape(-1, o.shape[2]) for o in out[:n]], out[n], out[n + 1]
+
+
+def gather_kernel(chunks, n, *refs):
+    shards, vector, results, vectors = refs[:n], refs[n], refs[n + 1 : 2 * n + 1], refs[2 * n + 1]
+    outs = refs[2 * n + 2 : 3 * n + 2]
+    send, recv, near, v_send, v_recv = refs[3 * n + 2 :]
+    z, x, y, c = place()
+    greet(z, x, y, c)
+
+    def at_z(k):
+        return (z + k) % 4
+
+    def own(t):
+        return pltpu.make_async_copy(shards[t], outs[t].at[z, x], near.at[t])
+
+    def copy(stage, i, k):
+        t, r0, nr, c0, both, split = chunks[i]
+        half = shards[t].shape[2] // 2
+        columns = lambda lo, size: pl.ds(pl.multiple_of(c * half + lo, 128), size)
+        wide, narrow, whole = columns(c0, both), columns(c0 + both, split), columns(c0, both + split)
+        rows = pl.ds(r0, nr)
+        mine = isinstance(k, int) and k == 0
+        o, src_z = outs[t], (z + 4 - k) % 4
+        if stage == 0:
+            src, dst, to = shards[t].at[:, rows, wide], o.at[z, x, :, rows, wide], device(at_z(k), x, y, c)
+        elif stage == 1:
+            src, dst, to = shards[t].at[y, rows, narrow], o.at[z, x, y, rows, narrow], device(at_z(k), x, y, c)
+        elif stage == 2:
+            dst, to = o.at[src_z, x, :, rows, wide], device(z, 1 - x, y, c)
+            src = shards[t].at[:, rows, wide] if mine else dst
+        elif stage == 3:
+            dst, to = o.at[src_z, x, y, rows, narrow], device(z, 1 - x, y, c)
+            src = shards[t].at[y, rows, narrow] if mine else dst
+        elif stage == 4:
+            src = o.at[src_z, 1 - x, y, rows, narrow] if mine else o.at[src_z, :, y, rows, narrow]
+            dst, to = src, device(z, x, 1 - y, c)
+        else:
+            src = o.at[src_z, 1 - x, :, rows, whole] if mine else o.at[src_z, :, :, rows, whole]
+            dst, to = src, device(z, x, y, 1 - c)
+        return remote(src, dst, send.at[i, stage, k], recv.at[i, stage, k], to)
+
+    def leave(t):
+        return pltpu.make_async_copy(outs[t], results[t], near.at[n + t])
+
+    def vector_copy(stage, k):
+        src_z = (z + 4 - k) % 4
+        if stage == 0:
+            return remote(vector, vectors.at[z, x], v_send.at[k], v_recv.at[k], device(at_z(k), x, y, c))
+        src = vector if k == 0 else vectors.at[src_z, x]
+        return remote(src, vectors.at[src_z, x], v_send.at[4 + k], v_recv.at[4 + k], device(z, 1 - x, y, c))
+
+    def each(lo, hi, body):
+        def step(k, carry):
+            body(k)
+            return carry
+        lax.fori_loop(lo, hi, step, 0)
+
+    def along_z(i):
+        def one(k):
+            copy(0, i, k).start()
+            copy(1, i, k).start()
+        each(1, 4, one)
+        copy(2, i, 0).start()
+        copy(3, i, 0).start()
+
+    def along_x(i):
+        def one(k):
+            copy(0, i, k).wait_recv()
+            copy(2, i, k).start()
+            copy(1, i, k).wait_recv()
+            copy(3, i, k).start()
+        each(1, 4, one)
+
+    def along_y(i):
+        copy(3, i, 0).wait_recv()
+        copy(4, i, 0).start()
+        def one(k):
+            copy(3, i, k).wait_recv()
+            copy(4, i, k).start()
+        each(1, 4, one)
+
+    def across(i):
+        def one(k):
+            copy(2, i, k).wait_recv()
+            copy(4, i, k).wait_recv()
+            copy(5, i, k).start()
+        one(0)
+        each(1, 4, one)
+
+    vectors[z, x] = vector[...]
+    for k in (1, 2, 3):
+        vector_copy(0, k).start()
+    vector_copy(1, 0).start()
+    along_z(0)
+    for t in range(n):
+        own(t).start()
+    count = len(chunks)
+    for i in range(count + 3):
+        if i + 1 < count:
+            along_z(i + 1)
+        if i < count:
+            along_x(i)
+        if i == 0:
+            for t in range(n):
+                own(t).wait()
+        if i == 1:
+            for k in (1, 2, 3):
+                vector_copy(0, k).wait_recv()
+                vector_copy(1, k).start()
+        if 0 <= i - 1 < count:
+            along_y(i - 1)
+        if 0 <= i - 2 < count:
+            across(i - 2)
+        if 0 <= i - 3:
+            copy(5, i - 3, 0).wait_recv()
+            each(1, 4, lambda k, i=i: copy(5, i - 3, k).wait_recv())
+            if i - 2 == count or chunks[i - 2][0] != chunks[i - 3][0]:
+                leave(chunks[i - 3][0]).start()
+
+    for i in range(count):
+        for stage in (2, 3, 4, 5):
+            copy(stage, i, 0).wait_send()
+        def finish(k, i=i):
+            for stage in range(6):
+                copy(stage, i, k).wait_send()
+        each(1, 4, finish)
+    for t in range(n):
+        leave(t).wait()
+    vector_copy(1, 0).wait()
+    for k in (1, 2, 3):
+        vector_copy(0, k).wait_send()
+        vector_copy(1, k).wait()
+
+
+def chunks_of(shards, largest):
+    chunks = []
+    for t, shard in enumerate(shards):
+        rows, tiles = shard.shape[0] // 2, shard.shape[1] // 256
+        size = rows * tiles * 128
+        parts = -(-size // largest)
+        by_rows = rows // parts % 16 == 0 and tiles < 2 * parts
+        if by_rows:
+            for p in range(parts):
+                both = max(1, tiles // 3) if tiles > 1 else 0
+                chunks.append((t, rows // parts * p, rows // parts, 0, both * 128, (tiles - both) * 128))
+        else:
+            cuts = [tiles * p // parts for p in range(parts + 1)]
+            for lo, hi in zip(cuts, cuts[1:]):
+                both = max(1, (hi - lo) // 3)
+                chunks.append((t, 0, rows, lo * 128, both * 128, (hi - lo - both) * 128))
+    return tuple(chunks)
+
+
+def gather_weights(shards, vector, ident):
+    n = len(shards)
+    views = [shard.reshape(2, shard.shape[0] // 2, shard.shape[1]) for shard in shards]
+    chunks = chunks_of(shards, 75000)
+    anywhere, vmem = pl.BlockSpec(memory_space=pl.ANY), pl.BlockSpec(memory_space=pltpu.VMEM)
+    dma = pltpu.SemaphoreType.DMA
+    out = pl.pallas_call(
+        functools.partial(gather_kernel, chunks, n),
+        out_shape=tuple(jax.ShapeDtypeStruct((4, 2) + v.shape, BF16) for v in views)
+        + (jax.ShapeDtypeStruct((4, 2, 8, 128), F32),),
+        in_specs=[vmem] * n + [vmem],
+        out_specs=(anywhere,) * n + (vmem,),
+        scratch_shapes=[pltpu.VMEM((4, 2) + v.shape, BF16) for v in views]
+        + [dma((len(chunks), 6, 4)), dma((len(chunks), 6, 4)), dma((2 * n,)), dma((8,)), dma((8,))],
+        compiler_params=pltpu.CompilerParams(collective_id=ident, has_side_effects=True, vmem_limit_bytes=60 * 2**20),
+        name="gather",
+    )(*views, vector.reshape(8, 128))
+    return [o.reshape(-1, o.shape[4]) for o in out[:n]], out[n].reshape(-1)
 
 
 def layer_norm(stream, gain, offset):
@@ -449,17 +915,19 @@
         second_decoder_down,
         second_vectors,
     )
-    w_embed, w_enc, w_enc_down, w_dec, w_dec_down, gathered_vectors = (
-        lax.all_gather(patch_embed.astype(jnp.bfloat16), "clip", axis=0, tiled=True),
-        lax.all_gather(encoder_in.astype(jnp.bfloat16), "clip", axis=0, tiled=True),
-        lax.all_gather(encoder_down.astype(jnp.bfloat16), "clip", axis=0, tiled=True),
-        lax.all_gather(decoder_in.astype(jnp.bfloat16), "clip", axis=0, tiled=True),
-        lax.all_gather(decoder_down.astype(jnp.bfloat16), "clip", axis=0, tiled=True),
-        lax.all_gather(norm_vectors.astype(jnp.bfloat16), "clip", axis=0, tiled=True),
-    )
+    direct = lax.axis_size("clip") == 8 and lax.axis_size("band") == 4
+    low_shards = [master.astype(jnp.bfloat16) for master in masters]
+    if direct:
+        (w_embed, w_enc, w_enc_down, w_dec, w_dec_down), vectors = gather_weights(
+            low_shards[:5], lax.reduce_precision(norm_vectors, exponent_bits=8, mantissa_bits=7), 0
+        )
+    else:
+        w_embed, w_enc, w_enc_down, w_dec, w_dec_down, gathered_vectors = (
+            lax.all_gather(shard, "clip", axis=0, tiled=True) for shard in low_shards
+        )
+        vectors = gathered_vectors.astype(jnp.float32)
     enc_width, dec_width = (w_enc.shape[0], w_dec.shape[0])
     enc_hidden, dec_hidden = (w_enc_down.shape[0], w_dec_down.shape[0])
-    vectors = gathered_vectors.astype(jnp.float32)
     enc_gains = vectors[: 6 * enc_width].reshape(6, enc_width)
     dec_gains = vectors[6 * enc_width :].reshape(7, dec_width)
     enc_weights = (
@@ -530,30 +998,29 @@
             g_dec_vectors.reshape(-1),
         ]
     )
-    shard_grads = (
-        lax.psum_scatter(g_embed, "clip", scatter_dimension=0, tiled=True),
-        lax.psum_scatter(g_enc_in, "clip", scatter_dimension=0, tiled=True),
-        lax.psum_scatter(g_enc_mats[3], "clip", scatter_dimension=0, tiled=True),
-        lax.psum_scatter(g_dec_in, "clip", scatter_dimension=0, tiled=True),
-        lax.psum_scatter(g_dec_down, "clip", scatter_dimension=0, tiled=True),
-        lax.psum_scatter(g_vectors, "clip", scatter_dimension=0, tiled=True),
-    )
-    reduced = lax.psum(
-        (
-            shard_grads[0],
-            shard_grads[1],
-            shard_grads[2],
-            shard_grads[3],
-            shard_grads[4],
-            shard_grads[5],
-        ),
-        "band",
-    )
-    squares = jnp.zeros((), jnp.float32)
-    for grad in reduced:
-        squares = squares + jnp.sum(grad * grad)
-    loss_sum = lax.psum(local_loss, ("clip", "band"))
-    norm_squared = lax.psum(squares, "clip")
+    if direct:
+        small = jnp.concatenate([g_vectors.reshape(-1, 128), jnp.full((8, 128), local_loss)])
+        nothing = jnp.zeros((8, 128), jnp.float32)
+        dec_shards, _, squares = reduce_grads([g_dec_in, g_dec_down], nothing, nothing, False, 1)
+        enc_shards, summed, squares = reduce_grads(
+            [g_enc_in, g_enc_mats[3], g_embed], small, squares, True, 2
+        )
+        rows = norm_vectors.shape[0]
+        vector_sums = summed[:-8].reshape(-1)
+        own = lax.dynamic_slice(vector_sums, (lax.axis_index("clip") * rows,), (rows,))
+        reduced = (enc_shards[2], enc_shards[0], enc_shards[1], *dec_shards, own)
+        loss_sum = summed[-1, 0]
+        norm_squared = jnp.sum(squares) + jnp.sum(vector_sums * vector_sums)
+    else:
+        reduced = lax.psum(
+            tuple(
+                lax.psum_scatter(grad, "clip", scatter_dimension=0, tiled=True)
+                for grad in (g_embed, g_enc_in, g_enc_mats[3], g_dec_in, g_dec_down, g_vectors)
+            ),
+            "band",
+        )
+        loss_sum = lax.psum(local_loss, ("clip", "band"))
+        norm_squared = lax.psum(sum(jnp.sum(grad * grad) for grad in reduced), "clip")
     grad_norm = jnp.sqrt(norm_squared)
     factor = jnp.minimum(1.0, CLIP_LIMIT / (grad_norm + 1e-06))
     results = []

time: 1730 us -> 786 us (0.45)
  waiting for transfers between devices: 1070 us -> 0 us
  Pallas kernels: 196 us -> 512 us
  blocking collectives: 163 us -> 0 us
    reduce_scatter x5 -> x0, waiting for transfers between devices: 782 us -> none  [the longest x1 339 us: shards(): lax.psum_scatter(g_enc_in, 'clip', scatter_dimension=0, tiled=True)]
    pallas_call x0 -> x3, Pallas kernels: none -> 307 us  [the longest x2 191 us: reduce_grads(): pl.pallas_call(functools.partial(reduce_kernel, tuple(widths), n), out_sh...]
    all_gather x4 -> x0, waiting for transfers between devices: 228 us -> none  [the longest x1 142 us: shards(): lax.all_gather(encoder_in.astype(jnp.bfloat16), 'clip', axis=0, tiled=True)]
    psum x3 -> x0, blocking collectives: 68.1 us -> none  [the longest x1 40 us: shards(): loss_sum = lax.psum(local_loss, ('clip', 'band'))]
    psum x1 -> x0, waiting for transfers between devices: 62.8 us -> none  [shards(): lax.psum((shard_grads[0], shard_grads[1], shard_grads[2], shard_grads[3],...]
    all_gather x2 -> x0, blocking collectives: 60 us -> none  [the longest x1 32.1 us: shards(): lax.all_gather(patch_embed.astype(jnp.bfloat16), 'clip', axis=0, tiled=True)]
    unnamed x1 -> x0, blocking collectives: 35.2 us -> none
  transfers between devices with their start and end apart: 10 -> 0, of which waited for: 9 -> 0; matrix products, arithmetic and copies ran while one was open for 6% -> 0% of each run, Pallas kernels for 0% -> 0%
where the time goes in v3:
time: 786 us; the launch traced here: 777 us
  Pallas kernels  512 us (65%)
  matrix products  164 us (21%)
  other arithmetic  52.7 us (7%)
  local copies, waits for them, and re-layouts  43.5 us (6%)
    pallas_call x1, Pallas kernels, decoder_step(): pl.pallas_call(functools.partial(decoder_kernel, coef, heads), out_shape=...  205 us
    pallas_call x2, Pallas kernels, reduce_grads(): pl.pallas_call(functools.partial(reduce_kernel, tuple(widths), n), out_sh...  191 us
    pallas_call x1, Pallas kernels, gather_weights(): pl.pallas_call(functools.partial(gather_kernel, chunks, n), out_shape=tup...  117 us
    dot_general x1, matrix products, attend_back(): jnp.einsum('bhqk,bqhd->bkhd', scaled, query, preferred_element_type=jnp.f...  27.5 us
    dot_general x1, matrix products, attend_back(): jnp.einsum('bhqk,bkhd->bqhd', scaled, key_rows, preferred_element_type=jn...  27.2 us
    dot_general x5, matrix products, input_grad(): lax.dot_general(grad_low, weights_in, (((1,), (1,)), ((), ())), preferred...  26.4 us
    dot_general x6, matrix products, weight_grad(): lax.dot_general(values_in, grad_low, (((0,), (0,)), ((), ())), preferred_...  23.2 us
    dot_general x6, matrix products, product(): return jnp.dot(values_in, weights_in, preferred_element_type=jnp.float32)  22.9 us

profile of v3, /device:TPU:0, one launch (start us, length us, event | category | flops | bytes accessed | tf_op | source)
XLA Modules:
  0.0 777.2 jit_solution(662927300775967578)
XLA Ops:
  4.6 5.6 multiply_sine_fusion.1
  10.3 3.9 gather_fusion
  19.8 116.8 %gather.13 = (bf16[4,2,2,16,768]{4,3,2,1,0:T(8,128)(2,1)}, bf16[4,2,2,48,6656]{4,3,2,1,0:T(8,128)(2,1)}, bf16[4,2,2,192,768]{4,3,2,1,0:T(8,128)(2,1)}, bf16[4,2,...) custom-call(bf16[2,16,768]{2,1,0:T(8,128)(2,1)} %bitcast.189, ...), custom_call_target="tpu_custom_call" | custom-call | tf_op jit(solution)/shard_map/gather/pallas_call | solution.py:727
  139.4 5.9 convolution_convert_fusion
  145.4 4.5 copy.71
  150.1 10.3 %fusion.118 = (f32[12,576]{1,0:T(8,128)S(1)}, f32[12,576,576]{1,2,0:T(8,128)}) fusion(f32[576,576]{0,1:T(8,128)S(1)} %compare_select_fusion, bf16[1,576,3,12,64]{1,4,3,2,0:T(8,128)(2,1)} %bitcast.171), kind=kOutput, calls=%fused_computation.232 | convolution fusion | flops 525533760 | bytes 19246080 | tf_op jit(solution)/shard_map/sub | solution.py:794
  160.4 8.0 %fusion.36 = bf16[12,64,576]{2,1,0:T(8,128)(2,1)S(1)} fusion(bf16[1,576,3,12,64]{1,4,3,2,0:T(8,128)(2,1)} %bitcast.172, f32[12,576,576]{1,2,0:T(8,128)} %get-tuple-element.133, f32[12,576]{1,0:T(8,128)S(1)} %get-tuple-element.132), kind=kOutput, calls=%fused_computation.68 | convolution fusion | flops 518012928 | bytes 19590144 | tf_op jit(solution)/shard_map/bhqk,bkhd->bqhd/dot_general | solution.py:800
  171.5 5.8 fusion.29
  177.4 4.3 fusion.120
  193.8 6.6 copy.74
  205.5 204.8 %decoder.1 = (f32[512,4352]{1,0:T(8,128)}, f32[2048,512]{1,0:T(8,128)}, f32[7,512,128]{2,1,0:T(8,128)}, f32[640,512]{1,0:T(8,128)}, f32[8,128]{1,0:T(8,128)}) custom-call(s32[6]{0:T(128)} %slice.93.shift_ref, s32[640,128]{1,0:T(8,128)} %broadcast_in_dim.41.rvis_ref, bf16[512,640]{1,0:T(8,128)(2,1)} %pad_bitcast_fusion.gvt_ref, bf16[3072,256]{1,0:T(8,128)(2,1)} %bitcast.170, ...), custom_call_target="tpu_custom_call" | custom-call | tf_op jit(solution)/shard_map/decoder/pallas_call | solution.py:252
  410.9 68.8 %reduce.12 = (f32[2,32,4352]{2,1,0:T(8,128)}, f32[2,128,512]{2,1,0:T(8,128)}, f32[8,128]{1,0:T(8,128)}, f32[8,128]{1,0:T(8,128)}) custom-call(f32[4,2,2,32,4352]{4,3,2,1,0:T(8,128)} %bitcast.166, f32[4,2,2,128,512]{4,3,2,1,0:T(8,128)} %bitcast.177, f32[8,128]{1,0:T(8,128)} %broadcast_in_dim.52.refs_2_.refs_3_, f32[8,128]{1,0:T(8,128)} %broadcast_in_dim.52.refs_2_.refs_3_), custom_call_target="tpu_custom_call" | custom-call | tf_op jit(solution)/shard_map/reduce/pallas_call | solution.py:552
  483.3 11.3 %fusion.16 = bf16[576,3072]{1,0:T(8,128)(2,1)S(1)} fusion(f32[576,3072]{1,0:T(8,128)} %copy-done.80, bf16[3072,768]{1,0:T(8,128)(2,1)} %bitcast.206, f32[576,768]{1,0:T(8,128)S(1)} %get-tuple-element.97, f32[576]{0:T(1024)S(1)} %negate_multiply_fusion.2), kind=kOutput, calls=%fused_computation.23 | convolution fusion | flops 2754183168 | bytes 17107200 | tf_op jit(solution)/shard_map/dot_general | solution.py:774
  494.7 3.8 multiply_reduce_fusion.2
  504.1 9.7 %fusion.66 = f32[12,576,576]{1,2,0:T(8,128)} fusion(bf16[576,12,64]{0,2,1:T(8,128)(2,1)S(1)} %bitcast.180, bf16[1,576,3,12,64]{1,4,3,2,0:T(8,128)(2,1)} %bitcast.173), kind=kOutput, calls=%fused_computation.96 | convolution fusion | flops 509607936 | bytes 17793024 | tf_op jit(solution)/shard_map/bqhd,bkhd->bhqk/dot_general | solution.py:813
  513.8 27.2 %fusion.52 = bf16[1,576,1,12,64]{1,4,3,2,0:T(8,128)(2,1)} fusion(f32[12,576,576]{1,2,0:T(8,128)} %fusion.66, bf16[1,576,3,12,64]{1,4,3,2,0:T(8,128)(2,1)} %bitcast.174, f32[12,576,576]{1,2,0:T(8,128)} %get-tuple-element.133, f32[12,576]{1,0:T(8,128)S(1)} %get-tuple-element.132), kind=kOutput, calls=%fused_computation.77 | convolution fusion | flops 537926976 | bytes 72728576 | tf_op jit(solution)/shard_map/bhqk,bkhd->bqhd/dot_general | solution.py:824
  541.0 27.5 %fusion.49 = bf16[1,576,1,12,64]{1,4,3,2,0:T(8,128)(2,1)} fusion(f32[12,576,576]{1,2,0:T(8,128)} %fusion.66, bf16[1,576,3,12,64]{1,4,3,2,0:T(8,128)(2,1)} %bitcast.175, f32[12,576,576]{1,2,0:T(8,128)} %get-tuple-element.133, f32[12,576]{1,0:T(8,128)S(1)} %get-tuple-element.132), kind=kOutput, calls=%fused_computation.76 | convolution fusion | flops 537926976 | bytes 72728576 | tf_op jit(solution)/shard_map/bhqk,bqhd->bkhd/dot_general | solution.py:825
  568.5 8.9 %fusion.55 = bf16[1,576,1,12,64]{1,4,3,2,0:T(8,128)(2,1)S(1)} fusion(bf16[576,12,64]{0,2,1:T(8,128)(2,1)S(1)} %bitcast.181, f32[12,576,576]{1,2,0:T(8,128)} %get-tuple-element.133, f32[12,576]{1,0:T(8,128)S(1)} %get-tuple-element.132), kind=kOutput, calls=%fused_computation.78 | convolution fusion | flops 518012928 | bytes 17722368 | tf_op jit(solution)/shard_map/bhqk,bqhd->bkhd/dot_general | solution.py:816
  578.9 6.8 multiply_reduce_fusion.3
  599.6 12.0 %fusion.98 = f32[3072,768]{1,0:T(8,128)} fusion(f32[576,768]{1,0:T(8,128)S(1)} %copy-done.14, f32[576]{0:T(1024)S(1)} %copy-done.69, f32[576,3072]{1,0:T(8,128)} %copy-done.80), kind=kOutput, calls=%fused_computation.223 | convolution fusion | flops 2734718976 | bytes 18286848 | tf_op jit(solution)/shard_map/dot_general | solution.py:780
  617.0 4.2 fusion.101
  622.3 7.7 pad_maximum_fusion
  630.0 121.8 %reduce.13 = (f32[2,48,6656]{2,1,0:T(8,128)}, f32[2,192,768]{2,1,0:T(8,128)}, f32[2,16,768]{2,1,0:T(8,128)}, f32[72,128]{1,0:T(8,128)}, f32[8,128]{1,0:T(8,128)}) custom-call(f32[4,2,2,48,6656]{4,3,2,1,0:T(8,128)} %bitcast.160, f32[4,2,2,192,768]{4,3,2,1,0:T(8,128)} %bitcast.165, f32[4,2,2,16,768]{4,3,2,1,0:T(8,128)} %bitcast.182, ...), custom_call_target="tpu_custom_call" | custom-call | tf_op jit(solution)/shard_map/reduce/pallas_call | solution.py:552
  769.1 4.5 multiply_subtract_fusion
  (270 shorter events, 81.6 us)
Async XLA Ops:
  14.2 122.4 %copy-start.25 = (bf16[576,256]{1,0:T(8,128)(2,1)}, bf16[576,256]{1,0:T(8,128)(2,1)S(1)}, u32[]{:S(2)}) copy-start(bf16[576,256]{1,0:T(8,128)(2,1)S(1)} %gather_fusion) | copy-start | bytes 884740
  17.8 118.8 %copy-start.30 = (f32[576,192]{1,0:T(8,128)S(1)}, f32[576,192]{1,0:T(8,128)}, u32[]{:S(2)}) copy-start(f32[576,192]{1,0:T(8,128)} %get-tuple-element.111) | copy-start | bytes 1327108
  138.6 29.8 %copy-start.2 = (f32[576,768]{1,0:T(8,128)}, f32[576,768]{1,0:T(8,128)S(1)}, u32[]{:S(2)}) copy-start(f32[576,768]{1,0:T(8,128)S(1)} %get-tuple-element.131) | copy-start | bytes 5308420
  139.4 45.1 %copy-start.70 = (f32[768]{0:T(1024)}, f32[768]{0:T(1024)S(1)}, u32[]{:S(2)}) copy-start(f32[768]{0:T(1024)S(1)} %get-tuple-element.103) | copy-start | bytes 9220
  139.4 343.1 %copy-start.56 = (f32[768]{0:T(1024)}, f32[768]{0:T(1024)S(1)}, u32[]{:S(2)}) copy-start(f32[768]{0:T(1024)S(1)} %get-tuple-element.102) | copy-start | bytes 9220
  181.8 300.8 %copy-start.53 = (f32[576]{0:T(1024)}, f32[576]{0:T(1024)S(1)}, u32[]{:S(2)}) copy-start(f32[576]{0:T(1024)S(1)} %broadcast_multiply_fusion.5) | copy-start | bytes 6916
  182.1 300.4 %copy-start.64 = (f32[576]{0:T(1024)}, f32[576]{0:T(1024)S(1)}, u32[]{:S(2)}) copy-start(f32[576]{0:T(1024)S(1)} %fusion.86) | copy-start | bytes 6916
  410.9 68.9 %copy-start.11 = (f32[576,768]{1,0:T(8,128)S(1)}, f32[576,768]{1,0:T(8,128)}, u32[]{:S(2)}) copy-start(f32[576,768]{1,0:T(8,128)} %copy-done.10) | copy-start | bytes 5308420
  410.9 68.9 %copy-start.78 = (f32[640,512]{1,0:T(8,128)S(1)}, f32[640,512]{1,0:T(8,128)}, u32[]{:S(2)}) copy-start(f32[640,512]{1,0:T(8,128)} %get-tuple-element.45) | copy-start | bytes 3932164
  482.5 12.1 %slice-start = ((s8[10223616]{0:T(1024)(128)(4,1)}), s8[4194304]{0:T(1024)(128)(4,1)S(1)}, s32[]{:S(2)}) async-start(s8[10223616]{0:T(1024)(128)(4,1)} %bitcast.196), calls=%async_computation | async-start | bytes 8388608
  483.3 15.9 %copy-start.13 = (f32[576,768]{1,0:T(8,128)}, f32[576,768]{1,0:T(8,128)S(1)}, u32[]{:S(2)}) copy-start(f32[576,768]{1,0:T(8,128)S(1)} %get-tuple-element.97) | copy-start | bytes 5308420
  483.3 15.9 %copy-start.68 = (f32[576]{0:T(1024)}, f32[576]{0:T(1024)S(1)}, u32[]{:S(2)}) copy-start(f32[576]{0:T(1024)S(1)} %negate_multiply_fusion.2) | copy-start | bytes 6916
  599.5 12.1 %copy-start.24 = (bf16[1,576,3,12,64]{1,4,3,2,0:T(8,128)(2,1)S(1)}, bf16[1,576,3,12,64]{1,4,3,2,0:T(8,128)(2,1)}, u32[]{:S(2)}) copy-start(bf16[1,576,3,12,64]{1,4,3,2,0:T(8,128)(2,1)} %copy-done.23) | copy-start | bytes 7962628
  599.5 12.1 %copy-start.52 = (f32[576]{0:T(1024)S(1)}, f32[576]{0:T(1024)}, u32[]{:S(2)}) copy-start(f32[576]{0:T(1024)} %copy-done.50) | copy-start | bytes 6916
  599.5 12.1 %copy-start.60 = (f32[768]{0:T(1024)S(1)}, f32[768]{0:T(1024)}, u32[]{:S(2)}) copy-start(f32[768]{0:T(1024)} %copy-done.58) | copy-start | bytes 9220
  599.5 12.0 %copy-start.63 = (f32[576]{0:T(1024)S(1)}, f32[576]{0:T(1024)}, u32[]{:S(2)}) copy-start(f32[576]{0:T(1024)} %copy-done.61) | copy-start | bytes 6916
  599.5 12.0 %copy-start.73 = (f32[768]{0:T(1024)S(1)}, f32[768]{0:T(1024)}, u32[]{:S(2)}) copy-start(f32[768]{0:T(1024)} %copy-done.72) | copy-start | bytes 9220
  630.0 125.9 %copy-start.67 = (f32[1024]{0:T(1024)S(1)}, f32[1024]{0:T(1024)}, u32[]{:S(2)}) copy-start(f32[1024]{0:T(1024)} %param.31) | copy-start | bytes 12292
  630.0 125.9 %copy-start.76 = (f32[1024]{0:T(1024)S(1)}, f32[1024]{0:T(1024)}, u32[]{:S(2)}) copy-start(f32[1024]{0:T(1024)} %param.37) | copy-start | bytes 12292
  630.0 125.9 %copy-start.77 = (f32[1024]{0:T(1024)S(1)}, f32[1024]{0:T(1024)}, u32[]{:S(2)}) copy-start(f32[1024]{0:T(1024)} %param.43) | copy-start | bytes 12292
  630.0 126.5 %copy-start.43 = (f32[2,128,512]{2,1,0:T(8,128)S(1)}, f32[2,128,512]{2,1,0:T(8,128)}, u32[]{:S(2)}) copy-start(f32[2,128,512]{2,1,0:T(8,128)} %get-tuple-element.57) | copy-start | bytes 1572868
  630.0 126.6 %copy-start.32 = (f32[256,512]{1,0:T(8,128)S(1)}, f32[256,512]{1,0:T(8,128)}, u32[]{:S(2)}) copy-start(f32[256,512]{1,0:T(8,128)} %param.30) | copy-start | bytes 1572868
  630.0 126.6 %copy-start.41 = (f32[256,512]{1,0:T(8,128)S(1)}, f32[256,512]{1,0:T(8,128)}, u32[]{:S(2)}) copy-start(f32[256,512]{1,0:T(8,128)} %param.36) | copy-start | bytes 1572868
  630.0 126.6 %copy-start.42 = (f32[256,512]{1,0:T(8,128)S(1)}, f32[256,512]{1,0:T(8,128)}, u32[]{:S(2)}) copy-start(f32[256,512]{1,0:T(8,128)} %param.42) | copy-start | bytes 1572868
  (62 other events, 253.7 us)

commit v4 on v3

--- a/solution.py
+++ b/solution.py
@@ -138,7 +138,7 @@
         def qkv_part(i):
             part = pl.ds(pl.multiple_of(i * chunk, chunk), chunk)
             qkv[part, :] = mm(wt_ref[part, :], n1[...]).astype(BF16)
-        loop(3 * width // chunk, qkv_part)
+        loop(3 * width // chunk, qkv_part, 3)
 
         q_group = (lax.broadcasted_iota(jnp.int32, (32, 128 * per), 1) % 128) // 32
 
@@ -165,7 +165,7 @@
             for h in range(per):
                 o = mm(v[size * h : size * h + size], p_all[:, 128 * h : 128 * h + 128])
                 att[pl.ds(f0 + size * h, size), at] = o.astype(BF16)
-        loop(rows // 128 * groups, attend, 4)
+        loop(rows // 128 * groups, attend, 16)
 
         res[...] += mm(wt_ref[c_out : c_out + width], att[...])
         ln_forward(1, xh2, n2)
@@ -173,11 +173,12 @@
         def up_part(i):
             part = pl.ds(pl.multiple_of(i * chunk, chunk), chunk)
             u = mm(wt_ref[pl.ds(pl.multiple_of(c_up + i * chunk, chunk), chunk), :], n2[...])
-            t = jnp.tanh(GELU_C * (u + 0.044715 * (u * u * u)))
-            hp = 0.5 * (1.0 + t)
-            act[part, :] = (u * hp).astype(BF16)
-            dgel[part, :] = hp + (0.5 * GELU_C) * u * (1.0 - t * t) * (1.0 + 0.134145 * (u * u))
-        loop(hidden // chunk, up_part)
+            square = u * u
+            hp = 0.5 + 0.5 * jnp.tanh(u * (GELU_C + (GELU_C * 0.044715) * square))
+            v = u * hp
+            act[part, :] = v.astype(BF16)
+            dgel[part, :] = hp + (v - v * hp) * ((2 * GELU_C) + (6 * GELU_C * 0.044715) * square)
+        loop(hidden // chunk, up_part, 4)
 
         res[...] += mm(wdt_ref[...], act[...])
         ln_forward(2, xh3, fin)
@@ -200,7 +201,7 @@
             dup[part, :] = d
             gdown_ref[part, :] += mm(act[part, :], low[...], 1, 1)
             gin_ref[:, there] += mm(n2[...], d, 1, 1)
-        loop(hidden // chunk, mlp_back)
+        loop(hidden // chunk, mlp_back, 4)
         tmp[...] = mm(w_ref[:, c_up:c_head], dup[...])
         ln_backward(1, xh2, True)
         gin_ref[:, c_out:c_up] += mm(att[...], low[...], 1, 1)
@@ -214,28 +215,26 @@
             k = qkv[pl.ds(width + f0, 128), at]
             v = qkv[pl.ds(2 * width + f0, 128), at]
             do = fin[pl.ds(f0, 128), at]
-            dp = compact(mm(v.T, wide(do, 128 * per) * hm[...]))
+            do_all = wide(do, 128 * per) * hm[...]
+            dp = compact(mm(v.T, do_all))
             p = probs[i]
             ds = p * (dp - jnp.sum(dp * p, axis=0, keepdims=True))
             p_all = jnp.concatenate([p.astype(BF16)] * 4, axis=0) * wm[...]
             ds_all = jnp.concatenate([(ds * scale).astype(BF16)] * 4, axis=0) * wm[...]
-            for h in range(per):
-                rows_h = slice(size * h, size * h + size)
-                ds_h = ds_all[:, 128 * h : 128 * h + 128]
-                p_h = p_all[:, 128 * h : 128 * h + 128]
-                dqkv[pl.ds(f0 + size * h, size), at] = mm(k[rows_h], ds_h).astype(BF16)
-                dqkv[pl.ds(width + f0 + size * h, size), at] = mm(q[rows_h], ds_h, 1, 1).astype(BF16)
-                dqkv[pl.ds(2 * width + f0 + size * h, size), at] = mm(do[rows_h], p_h, 1, 1).astype(BF16)
-        loop(rows // 128 * groups, attend_back, 4)
+            tall = jnp.concatenate([ds_all[:, 128 * h : 128 * h + 128] for h in range(per)], axis=0)
+            dqkv[pl.ds(f0, 128), at] = mm(wide(k, 128 * per) * hm[...], tall).astype(BF16)
+            dqkv[pl.ds(width + f0, 128), at] = mm(wide(q, 128 * per) * hm[...], ds_all, 1, 1).astype(BF16)
+            dqkv[pl.ds(2 * width + f0, 128), at] = mm(do_all, p_all, 1, 1).astype(BF16)
+        loop(rows // 128 * groups, attend_back, 8)
 
         def qkv_back(i):
             part = pl.ds(pl.multiple_of(i * chunk, chunk), chunk)
             gin_ref[:, part] += mm(n1[...], dqkv[part, :], 1, 1)
-        loop(3 * width // chunk, qkv_back)
+        loop(3 * width // chunk, qkv_back, 3)
         tmp[...] = mm(w_ref[:, :c_out], dqkv[...])
         ln_backward(0, xh1, True)
         gvec_ref[6] += fold(low[...].astype(F32) * mrow[0:1])
-        gp_ref[...] += mm(oh[...], low[...], 1, 1)
+        gp_ref[...] += mm(low[...], oh[...], 1, 1)
 
     loop(nblk, block)
 
@@ -255,7 +254,7 @@
             jax.ShapeDtypeStruct((width, total), F32),
             jax.ShapeDtypeStruct((hidden, width), F32),
             jax.ShapeDtypeStruct((7, width, 128), F32),
-            jax.ShapeDtypeStruct((vis, width), F32),
+            jax.ShapeDtypeStruct((width, vis), F32),
             jax.ShapeDtypeStruct((8, 128), F32),
         ),
         in_specs=[pl.BlockSpec(memory_space=pltpu.SMEM)] + [vmem] * 10,
@@ -270,6 +269,272 @@
         compiler_params=pltpu.CompilerParams(vmem_limit_bytes=63 * 2**20),
         name="decoder",
     )(shift, rvis, gvt, pix, et, ef, vec, w, wt, wd, wdt)
+
+
+CHUNK = 768
+
+
+def lane(i):
+    return pl.ds(i * 128 if isinstance(i, int) else pl.multiple_of(i * 128, 128), 128)
+
+
+def part(i, base=0):
+    return pl.ds(pl.multiple_of(base + i * CHUNK, 128), CHUNK)
+
+
+def encoder_scores(q, k, bias, scale):
+    c = mm(k, q, 0, 0) * scale + bias
+    e = jnp.exp(c - jnp.max(c, axis=0, keepdims=True))
+    return e * (1.0 / jnp.sum(e, axis=0, keepdims=True))
+
+
+def encoder_forward_kernel(
+    heads, seen_ref, pos_ref, grid_pos_ref, segc_ref, segr_ref, vec_ref, we_ref, wi_ref, wd_ref,
+    grid_ref, bias_ref, seen_t_ref, xh1_ref, n1_ref, qkv_ref, att_ref, xh2_ref, n2_ref, act_ref, dgel_ref, xh3_ref, fin_ref, rs_ref,
+    we, wi, wd, res, bias, seen_t, xh1, n1, qkv, att, xh2, n2, act, dgel, xh3, fin, rs, w_sem, o_sem,
+):
+    width, hidden = we.shape[1], wd.shape[0]
+    rows = res.shape[1]
+    size = width // heads
+    scale = size ** -0.5
+    c_out, c_up, c_proj = 3 * width, 4 * width, 4 * width + hidden
+    total = wi.shape[1]
+    loads = [pltpu.make_async_copy(we_ref, we, w_sem.at[0])]
+    for i, (lo, hi) in enumerate(((0, c_out), (c_out, c_up), (c_up, c_proj), (c_proj, total))):
+        at = pl.ds(lo, hi - lo)
+        loads.append(pltpu.make_async_copy(wi_ref.at[:, at], wi.at[:, at], w_sem.at[1 + i]))
+    loads.insert(4, pltpu.make_async_copy(wd_ref, wd, w_sem.at[5]))
+    for load in loads:
+        load.start()
+    pairs = (
+        (bias, bias_ref), (seen_t, seen_t_ref), (xh1, xh1_ref), (n1, n1_ref), (qkv, qkv_ref), (att, att_ref), (xh2, xh2_ref),
+        (n2, n2_ref), (act, act_ref), (dgel, dgel_ref), (xh3, xh3_ref), (fin, fin_ref), (rs, rs_ref),
+    )
+    saves = [pltpu.make_async_copy(a, b, o_sem.at[i]) for i, (a, b) in enumerate(pairs)]
+
+    def ln_forward(k, xh, out):
+        def body(i):
+            x = res[:, lane(i)]
+            centre = x - jnp.mean(x, axis=0, keepdims=True)
+            r = lax.rsqrt(jnp.mean(centre * centre, axis=0, keepdims=True) + 1e-06)
+            xhat = centre * r
+            xh[:, lane(i)] = xhat
+            rs[8 * k : 8 * k + 8, lane(i)] = jnp.broadcast_to(r, (8, 128))
+            out[:, lane(i)] = (xhat * vec_ref[2 * k] + vec_ref[2 * k + 1]).astype(BF16)
+        for i in range(rows // 128):
+            body(i)
+
+    seen_t[...] = seen_ref[...].T
+    saves[1].start()
+    bias[...] = jnp.where(wide(segc_ref[...], rows) == segr_ref[0:1], 0.0, -1e30)
+    saves[0].start()
+    loads[0].wait()
+    res[...] = mm(we[...], seen_t[...], 0, 0) + pos_ref[...]
+    ln_forward(0, xh1, n1)
+    saves[2].start()
+    saves[3].start()
+    loads[1].wait()
+
+    def qkv_part(i):
+        qkv[part(i), :] = mm(wi[:, part(i)], n1[...], 0, 0).astype(BF16)
+    loop(3, qkv_part)
+    saves[4].start()
+
+    def attend(h):
+        f0 = pl.multiple_of(h * size, size)
+        k = qkv[pl.ds(width + f0, size), :]
+        v = qkv[pl.ds(2 * width + f0, size), :]
+        for i in range(rows // 128):
+            p = encoder_scores(qkv[pl.ds(f0, size), lane(i)], k, bias[:, lane(i)], scale)
+            att[pl.ds(f0, size), lane(i)] = mm(v, p.astype(BF16)).astype(BF16)
+    loop(heads, attend)
+    saves[5].start()
+    loads[2].wait()
+    res[...] += mm(wi[:, c_out:c_up], att[...], 0, 0)
+    ln_forward(1, xh2, n2)
+    saves[6].start()
+    saves[7].start()
+    loads[3].wait()
+
+    def up_part(i):
+        u = mm(wi[:, part(i, c_up)], n2[...], 0, 0)
+        square = u * u
+        hp = 0.5 + 0.5 * jnp.tanh(u * (GELU_C + (GELU_C * 0.044715) * square))
+        v = u * hp
+        act[part(i), :] = v.astype(BF16)
+        dgel[part(i), :] = hp + (v - v * hp) * ((2 * GELU_C) + (6 * GELU_C * 0.044715) * square)
+    loop(hidden // CHUNK, up_part, 2)
+    saves[8].start()
+    saves[9].start()
+    loads[4].wait()
+    res[...] += mm(wd[...], act[...], 0, 0)
+    ln_forward(2, xh3, fin)
+    for i in (10, 11, 12):
+        saves[i].start()
+    loads[5].wait()
+    grid_ref[...] = (mm(wi[:, c_proj:], fin[...], 0, 0) + grid_pos_ref[...]).astype(BF16)
+    for save in saves:
+        save.wait()
+
+
+def encoder_forward(seen, pos, grid_pos, segc, segr, vec, we, wi, wd, heads):
+    rows, patch = seen.shape
+    width, total = wi.shape
+    hidden = wd.shape[0]
+    any_, vmem = pl.BlockSpec(memory_space=pl.ANY), pl.BlockSpec(memory_space=pltpu.VMEM)
+    saved = (
+        ((rows, rows), F32), ((patch, rows), BF16), ((width, rows), F32), ((width, rows), BF16), ((3 * width, rows), BF16),
+        ((width, rows), BF16), ((width, rows), F32), ((width, rows), BF16), ((hidden, rows), BF16), ((hidden, rows), F32),
+        ((width, rows), F32), ((width, rows), BF16), ((24, rows), F32),
+    )
+    return pl.pallas_call(
+        functools.partial(encoder_forward_kernel, heads),
+        out_shape=(jax.ShapeDtypeStruct((grid_pos.shape[0], rows), BF16),) + tuple(jax.ShapeDtypeStruct(*s) for s in saved),
+        in_specs=[vmem] * 6 + [any_] * 3,
+        out_specs=(vmem,) + (any_,) * len(saved),
+        scratch_shapes=[pltpu.VMEM(we.shape, BF16), pltpu.VMEM(wi.shape, BF16), pltpu.VMEM(wd.shape, BF16), pltpu.VMEM((width, rows), F32)]
+        + [pltpu.VMEM(*s) for s in saved] + [pltpu.SemaphoreType.DMA((6,)), pltpu.SemaphoreType.DMA((len(saved),))],
+        compiler_params=pltpu.CompilerParams(vmem_limit_bytes=62 * 2**20),
+        name="encode",
+    )(seen, pos, grid_pos, segc, segr, vec, we, wi, wd)
+
+
+def encoder_backward_kernel(
+    heads, gp_ref, vec_ref, wi_ref, wd_ref,
+    bias_ref, seen_t_ref, xh1_ref, n1_ref, qkv_ref, att_ref, xh2_ref, n2_ref, act_ref, dgel_ref, xh3_ref, fin_ref, rs_ref,
+    gin_ref, gdown_ref, gembed_ref, gvec_ref,
+    wi, wd, res, tmp, low, dqkv, probs, dscores, stage, bias, seen_t, xh1, n1, qkv, att, xh2, n2, act, dgel, rs, i_sem, s_sem,
+):
+    width, hidden = wi.shape[0], wd.shape[0]
+    rows = res.shape[1]
+    size = width // heads
+    scale = size ** -0.5
+    c_out, c_up, c_proj = 3 * width, 4 * width, 4 * width + hidden
+    total = wi.shape[1]
+    n_proj = total - c_proj
+
+    def load(i, src, dst):
+        return pltpu.make_async_copy(src, dst, i_sem.at[i])
+
+    def columns(i, lo, hi):
+        at = pl.ds(lo, hi - lo)
+        return load(i, wi_ref.at[:, at], wi.at[:, at])
+
+    first = [load(0, fin_ref, n1), columns(1, c_proj, total), load(2, xh3_ref, xh1), load(3, rs_ref, rs)]
+    mlp = [load(4, wd_ref, wd), load(5, dgel_ref, dgel), load(6, act_ref, act), load(7, n2_ref, n2)]
+    second = [columns(8, c_up, c_proj), load(9, xh2_ref, xh2), columns(10, c_out, c_up), load(11, att_ref, att)]
+    attention = [load(12, qkv_ref, qkv), load(13, bias_ref, bias), columns(14, 0, c_out), load(15, seen_t_ref, seen_t)]
+    again = [load(16, xh1_ref, xh1), load(17, n1_ref, n1)]
+    for group in (first, mlp, second, attention):
+        for copy in group:
+            copy.start()
+    gvec_ref[...] = jnp.zeros_like(gvec_ref)
+
+    open_copies = [None, None]
+    turn = [0]
+
+    def leave(value, dst):
+        slot = turn[0] % 2
+        if open_copies[slot] is not None:
+            open_copies[slot].wait()
+        height, length = value.shape
+        stage[slot, :height, :length] = value
+        copy = pltpu.make_async_copy(stage.at[slot, pl.ds(0, height), pl.ds(0, length)], dst, s_sem.at[slot])
+        copy.start()
+        open_copies[slot] = copy
+        turn[0] += 1
+
+    def ln_backward(k, xh, add):
+        for i in range(rows // 128):
+            d = tmp[:, lane(i)]
+            xhat = xh[:, lane(i)]
+            gvec_ref[2 * k] += d * xhat
+            gvec_ref[2 * k + 1] += d
+            dx = d * vec_ref[2 * k]
+            m1 = jnp.mean(dx, axis=0, keepdims=True)
+            m2 = jnp.mean(dx * xhat, axis=0, keepdims=True)
+            g = rs[8 * k : 8 * k + 1, lane(i)] * (dx - m1 - xhat * m2)
+            if add:
+                g = g + res[:, lane(i)]
+            res[:, lane(i)] = g
+            low[:, lane(i)] = g.astype(BF16)
+
+    for copy in first:
+        copy.wait()
+    gp = gp_ref[...].astype(BF16)
+    leave(mm(n1[...], gp, 1, 1), gin_ref.at[:, pl.ds(c_proj, n_proj)])
+    tmp[...] = mm(wi[:, c_proj:], gp)
+    ln_backward(2, xh1, False)
+    for copy in again:
+        copy.start()
+    for copy in mlp:
+        copy.wait()
+    for i in range(hidden // CHUNK):
+        at = pl.ds(i * CHUNK, CHUNK)
+        d = (mm(wd[at, :], low[...]) * dgel[at, :]).astype(BF16)
+        leave(mm(act[at, :], low[...], 1, 1), gdown_ref.at[at, :])
+        act[at, :] = d
+        leave(mm(n2[...], d, 1, 1), gin_ref.at[:, pl.ds(c_up + i * CHUNK, CHUNK)])
+    for copy in second:
+        copy.wait()
+    tmp[...] = mm(wi[:, c_up:c_proj], act[...])
+    ln_backward(1, xh2, True)
+    leave(mm(att[...], low[...], 1, 1), gin_ref.at[:, pl.ds(c_out, width)])
+    att[...] = mm(wi[:, c_out:c_up], low[...]).astype(BF16)
+    for copy in attention:
+        copy.wait()
+
+    def attend_back(h):
+        f0 = pl.multiple_of(h * size, size)
+        mine = pl.ds(f0, size)
+        q = qkv[mine, :]
+        k = qkv[pl.ds(width + f0, size), :]
+        v = qkv[pl.ds(2 * width + f0, size), :]
+        do = att[mine, :]
+        for i in range(rows // 128):
+            p = encoder_scores(q[:, 128 * i : 128 * i + 128], k, bias[:, lane(i)], scale)
+            dp = mm(v, do[:, 128 * i : 128 * i + 128], 0, 0)
+            ds = p * (dp - jnp.sum(dp * p, axis=0, keepdims=True))
+            probs[:, lane(i)] = p.astype(BF16)
+            dscores[:, lane(i)] = (ds * scale).astype(BF16)
+        dqkv[mine, :] = mm(k, dscores[...]).astype(BF16)
+        dqkv[pl.ds(width + f0, size), :] = mm(q, dscores[...], 1, 1).astype(BF16)
+        dqkv[pl.ds(2 * width + f0, size), :] = mm(do, probs[...], 1, 1).astype(BF16)
+    loop(heads, attend_back)
+    for copy in again:
+        copy.wait()
+    for i in range(3 * width // CHUNK):
+        at = pl.ds(i * CHUNK, CHUNK)
+        leave(mm(n1[...], dqkv[at, :], 1, 1), gin_ref.at[:, at])
+    tmp[...] = mm(wi[:, :c_out], dqkv[...])
+    ln_backward(0, xh1, True)
+    leave(mm(seen_t[...], low[...], 1, 1), gembed_ref)
+    for copy in open_copies:
+        copy.wait()
+
+
+def encoder_backward(gp, vec, wi, wd, saved, patch, heads):
+    rows = gp.shape[1]
+    width, total = wi.shape
+    hidden = wd.shape[0]
+    any_, vmem = pl.BlockSpec(memory_space=pl.ANY), pl.BlockSpec(memory_space=pltpu.VMEM)
+    f = lambda *s: pltpu.VMEM(s, F32)
+    b = lambda *s: pltpu.VMEM(s, BF16)
+    shape = lambda *s: jax.ShapeDtypeStruct(s, F32)
+    return pl.pallas_call(
+        functools.partial(encoder_backward_kernel, heads),
+        out_shape=(shape(width, total), shape(hidden, width), shape(patch, width), shape(6, width, 128)),
+        in_specs=[vmem] * 2 + [any_] * (2 + len(saved)),
+        out_specs=(any_,) * 3 + (vmem,),
+        scratch_shapes=[
+            b(*wi.shape), b(*wd.shape), f(width, rows), f(width, rows), b(width, rows), b(3 * width, rows), b(rows, rows), b(rows, rows),
+            f(2, CHUNK, CHUNK), f(rows, rows), b(patch, rows), f(width, rows), b(width, rows), b(3 * width, rows), b(width, rows),
+            f(width, rows), b(width, rows), b(hidden, rows), f(hidden, rows), f(24, rows),
+            pltpu.SemaphoreType.DMA((18,)), pltpu.SemaphoreType.DMA((2,)),
+        ],
+        compiler_params=pltpu.CompilerParams(vmem_limit_bytes=63 * 2**20),
+        name="encode_back",
+    )(gp, vec, wi, wd, *saved)
 
 
 def place():
@@ -738,22 +1003,6 @@
     return [o.reshape(-1, o.shape[4]) for o in out[:n]], out[n].reshape(-1)
 
 
-def layer_norm(stream, gain, offset):
-    centre = stream - jnp.mean(stream, axis=-1, keepdims=True)
-    spread = jnp.mean(centre * centre, axis=-1, keepdims=True)
-    return centre * lax.rsqrt(spread + 1e-06) * gain + offset
-
-
-def sincos(time_pos, frequency, width):
-    quarter = width // 4
-    omega = 1.0 / 10000.0 ** (jnp.arange(quarter, dtype=jnp.float32) / quarter)
-    time_angle = time_pos.astype(jnp.float32)[:, None] * omega[None, :]
-    band_angle = frequency.astype(jnp.float32)[:, None] * omega[None, :]
-    return jnp.concatenate(
-        [jnp.sin(time_angle), jnp.cos(time_angle), jnp.sin(band_angle), jnp.cos(band_angle)], axis=1
-    )
-
-
 def clip_of(column, clip_lengths, clip_shifts):
     columns = clip_lengths // 8
     ends = jnp.cumsum(columns)
@@ -766,103 +1015,11 @@
     return clip_id, select(ends - columns), select(columns), select(clip_shifts[:, 0]), select(clip_shifts[:, 1])
 
 
-def product(values_in, weights_in):
-    return jnp.dot(values_in, weights_in, preferred_element_type=jnp.float32)
-
-
-def input_grad(grad_low, weights_in):
-    return lax.dot_general(
-        grad_low, weights_in, (((1,), (1,)), ((), ())), preferred_element_type=jnp.float32
-    )
-
-
-def weight_grad(values_in, grad_low):
-    return lax.dot_general(
-        values_in, grad_low, (((0,), (0,)), ((), ())), preferred_element_type=jnp.float32
-    )
-
-
-def split_heads(projections, heads, group):
-    rows = projections.shape[0]
-    head_size = projections.shape[1] // (3 * heads)
-    split_parts = projections.reshape(rows // group, group, 3, heads, head_size)
-    return (split_parts[:, :, 0], split_parts[:, :, 1], split_parts[:, :, 2], head_size)
-
-
-def softmax_probs(query, key_rows, head_size, score_bias):
-    scores = jnp.einsum("bqhd,bkhd->bhqk", query, key_rows, preferred_element_type=jnp.float32)
-    return jax.nn.softmax(scores * head_size ** (-0.5) + score_bias, axis=-1)
-
-
-def attend(projections, heads, group, score_bias):
-    query, key_rows, value_rows, head_size = split_heads(projections, heads, group)
-    probs = softmax_probs(query, key_rows, head_size, score_bias)
-    mixed = jnp.einsum(
-        "bhqk,bkhd->bqhd",
-        probs.astype(jnp.bfloat16),
-        value_rows,
-        preferred_element_type=jnp.float32,
-    )
-    return mixed.reshape(projections.shape[0], -1)
-
-
-def attend_back(grad_mixed, projections, heads, group, score_bias):
-    query, key_rows, value_rows, head_size = split_heads(projections, heads, group)
-    probs = softmax_probs(query, key_rows, head_size, score_bias)
-    grad_heads = grad_mixed.reshape(query.shape)
-    grad_probs = jnp.einsum(
-        "bqhd,bkhd->bhqk", grad_heads, value_rows, preferred_element_type=jnp.float32
-    )
-    grad_values = jnp.einsum(
-        "bhqk,bqhd->bkhd",
-        probs.astype(jnp.bfloat16),
-        grad_heads,
-        preferred_element_type=jnp.float32,
-    )
-    grad_scores = probs * (grad_probs - jnp.sum(grad_probs * probs, axis=-1, keepdims=True))
-    scaled = (grad_scores * head_size ** (-0.5)).astype(jnp.bfloat16)
-    grad_query = jnp.einsum("bhqk,bkhd->bqhd", scaled, key_rows, preferred_element_type=jnp.float32)
-    grad_keys = jnp.einsum("bhqk,bqhd->bkhd", scaled, query, preferred_element_type=jnp.float32)
-    return jnp.stack([grad_query, grad_keys, grad_values], axis=2).reshape(projections.shape[0], -1)
-
-
-def block_forward(stream, weights, gains, heads, group, score_bias):
-    w_qkv, w_out, w_up, w_down = weights
-    normed = layer_norm(stream, gains[0], gains[1]).astype(jnp.bfloat16)
-    projections = product(normed, w_qkv).astype(jnp.bfloat16)
-    attended = attend(projections, heads, group, score_bias).astype(jnp.bfloat16)
-    middle = stream + product(attended, w_out)
-    second_normed = layer_norm(middle, gains[2], gains[3]).astype(jnp.bfloat16)
-    up_values = product(second_normed, w_up)
-    activated = jax.nn.gelu(up_values).astype(jnp.bfloat16)
-    return (
-        middle + product(activated, w_down),
-        (stream, normed, projections, attended, middle, second_normed, up_values, activated),
-    )
-
-
-def block_backward(grad_out, cache, weights, gains, heads, group, score_bias):
-    w_qkv, w_out, w_up, w_down = weights
-    stream, normed, projections, attended, middle, second_normed, up_values, activated = cache
-    grad_down = grad_out.astype(jnp.bfloat16)
-    g_down = weight_grad(activated, grad_down)
-    _, gelu_back = jax.vjp(jax.nn.gelu, up_values)
-    grad_up = gelu_back(input_grad(grad_down, w_down))[0].astype(jnp.bfloat16)
-    g_up = weight_grad(second_normed, grad_up)
-    _, norm_back = jax.vjp(layer_norm, middle, gains[2], gains[3])
-    grad_middle, g_gain_two, g_offset_two = norm_back(input_grad(grad_up, w_up))
-    grad_middle = grad_middle + grad_out
-    grad_branch = grad_middle.astype(jnp.bfloat16)
-    g_out = weight_grad(attended, grad_branch)
-    grad_attended = input_grad(grad_branch, w_out).astype(jnp.bfloat16)
-    grad_projections = attend_back(grad_attended, projections, heads, group, score_bias).astype(
-        jnp.bfloat16
-    )
-    g_qkv = weight_grad(normed, grad_projections)
-    _, first_back = jax.vjp(layer_norm, stream, gains[0], gains[1])
-    grad_stream, g_gain_one, g_offset_one = first_back(input_grad(grad_projections, w_qkv))
-    norm_grads = jnp.stack([g_gain_one, g_offset_one, g_gain_two, g_offset_two])
-    return (grad_stream + grad_middle, (g_qkv, g_out, g_up, g_down), norm_grads)
+def half_table(position, width):
+    quarter = width // 4
+    omega = 1.0 / 10000.0 ** (jnp.arange(quarter, dtype=jnp.float32) / quarter)
+    angle = omega[:, None] * position.astype(jnp.float32)[None, :]
+    return jnp.concatenate([jnp.sin(angle), jnp.cos(angle)])
 
 
 def adam_update(weight, first, second, grad, decay):
@@ -927,51 +1084,52 @@
         )
         vectors = gathered_vectors.astype(jnp.float32)
     enc_width, dec_width = (w_enc.shape[0], w_dec.shape[0])
-    enc_hidden, dec_hidden = (w_enc_down.shape[0], w_dec_down.shape[0])
-    enc_gains = vectors[: 6 * enc_width].reshape(6, enc_width)
-    dec_gains = vectors[6 * enc_width :].reshape(7, dec_width)
-    enc_weights = (
-        w_enc[:, : 3 * enc_width],
-        w_enc[:, 3 * enc_width : 4 * enc_width],
-        w_enc[:, 4 * enc_width : 4 * enc_width + enc_hidden],
-        w_enc_down,
-    )
-    w_proj = w_enc[:, 4 * enc_width + enc_hidden :]
     patch_dev, n_visible = pixels.shape[0], visible.shape[0]
+    padded = -(-n_visible // 128) * 128
+    enc_gains = vectors[: 6 * enc_width].reshape(6, enc_width, 1)
+    dec_gains = vectors[6 * enc_width :].reshape(7, dec_width, 1)
+    enc_gains = jnp.broadcast_to(enc_gains, (6, enc_width, 128))
+    dec_gains = jnp.broadcast_to(dec_gains, (7, dec_width, 128))
     turned = jnp.arange(patch_dev // 8, dtype=jnp.int32)
     _, start, size, shift_time, shift_band = clip_of(turned, lengths[0], shifts[0])
     turned_time = (turned - start - shift_time) % size
     decoder_pixels = pixels.reshape(patch_dev // 8, 8, -1)[start + turned_time].reshape(pixels.shape)
-    seen = pixels[visible]
-    seen_column, seen_band = visible // 8, visible % 8
-    segment, seen_start, seen_size, seen_shift, _ = clip_of(seen_column, lengths[0], shifts[0])
-    seen_time = seen_column - seen_start
-    decoder_row = 8 * (seen_start + (seen_time + seen_shift) % seen_size) + seen_band
-    padded = -(-n_visible // 128) * 128
-    decoder_row = jnp.pad(decoder_row, (0, padded - n_visible), constant_values=-1)
-    decoder_row = jnp.broadcast_to(decoder_row[:, None], (padded, 128))
-    score_bias = jnp.where(segment[:, None] == segment[None, :], 0.0, -1e30)
-    embedded = product(seen, w_embed) + sincos(seen_time, seen_band, enc_width)
-    encoded, enc_cache = block_forward(
-        embedded, enc_weights, enc_gains, HEADS_ENC, seen.shape[0], score_bias
+    time_table = half_table(turned_time, dec_width).T
+    band_table = jnp.tile(half_table(jnp.arange(8, dtype=jnp.int32), dec_width), (1, 16))
+    spots = jnp.pad(visible, (0, padded - n_visible))
+    real = jnp.arange(padded, dtype=jnp.int32) < n_visible
+    seen = pixels[spots]
+    column, band = spots // 8, spots % 8
+    segment, seen_start, seen_size, seen_shift, _ = clip_of(column, lengths[0], shifts[0])
+    segment = jnp.where(real, segment, -1).astype(jnp.int32)
+    seen_time = column - seen_start
+    decoder_row = jnp.where(real, 8 * (seen_start + (seen_time + seen_shift) % seen_size) + band, -1)
+    decoder_row = jnp.broadcast_to(decoder_row[:, None], (padded, 128)).astype(jnp.int32)
+
+    def positions(width):
+        return jnp.concatenate([half_table(seen_time, width), half_table(band, width)])
+
+    grid_seen, *saved = encoder_forward(
+        seen,
+        positions(enc_width),
+        positions(dec_width),
+        jnp.broadcast_to(segment[:, None], (padded, 128)),
+        jnp.broadcast_to(segment[None, :], (8, padded)),
+        enc_gains,
+        w_embed,
+        w_enc,
+        w_enc_down,
+        HEADS_ENC,
     )
-    final_enc = layer_norm(encoded, enc_gains[4], enc_gains[5]).astype(jnp.bfloat16)
-    projected = product(final_enc, w_proj)
-    grid_seen = (projected + sincos(seen_time, seen_band, dec_width)).astype(jnp.bfloat16)
-    grid_seen = jnp.pad(grid_seen, ((0, padded - n_visible), (0, 0)))
-    time_table = sincos(turned_time, turned_time, dec_width)[:, : dec_width // 2]
-    bands = jnp.arange(8, dtype=jnp.int32)
-    band_table = jnp.tile(sincos(bands, bands, dec_width)[:, dec_width // 2 :].T, (1, 16))
-    wide_vectors = jnp.broadcast_to(dec_gains[:, :, None], dec_gains.shape + (128,))
     masked_count = 13.0 * (patch_dev // 16) * lax.axis_size("clip") * lax.axis_size("band")
-    g_dec_in, g_dec_down, g_dec_vectors, grad_proj, loss = decoder_step(
+    g_dec_in, g_dec_down, g_dec_vectors, grad_grid, loss = decoder_step(
         shift_band[::64],
         decoder_row,
-        grid_seen.T,
+        grid_seen,
         decoder_pixels,
         time_table,
         band_table,
-        wide_vectors,
+        dec_gains,
         w_dec,
         w_dec.T,
         w_dec_down,
@@ -980,30 +1138,18 @@
         HEADS_DEC,
     )
     local_loss = jnp.sum(loss[0])
-    g_dec_vectors = jnp.sum(g_dec_vectors, axis=2)
-    grad_proj = grad_proj[:n_visible].astype(jnp.bfloat16)
-    g_proj = weight_grad(final_enc, grad_proj)
-    _, enc_final_back = jax.vjp(layer_norm, encoded, enc_gains[4], enc_gains[5])
-    grad_encoded, g_enc_gain, g_enc_offset = enc_final_back(input_grad(grad_proj, w_proj))
-    grad_embedded, g_enc_mats, g_enc_norms = block_backward(
-        grad_encoded, enc_cache, enc_weights, enc_gains, HEADS_ENC, seen.shape[0], score_bias
+    g_enc_in, g_enc_down, g_embed, g_enc_vectors = encoder_backward(
+        grad_grid, enc_gains, w_enc, w_enc_down, saved, pixels.shape[1], HEADS_ENC
     )
-    g_embed = weight_grad(seen, grad_embedded.astype(jnp.bfloat16))
-    g_enc_in = jnp.concatenate([g_enc_mats[0], g_enc_mats[1], g_enc_mats[2], g_proj], axis=1)
     g_vectors = jnp.concatenate(
-        [
-            g_enc_norms.reshape(-1),
-            g_enc_gain,
-            g_enc_offset,
-            g_dec_vectors.reshape(-1),
-        ]
+        [jnp.sum(g_enc_vectors, axis=2).reshape(-1), jnp.sum(g_dec_vectors, axis=2).reshape(-1)]
     )
     if direct:
         small = jnp.concatenate([g_vectors.reshape(-1, 128), jnp.full((8, 128), local_loss)])
         nothing = jnp.zeros((8, 128), jnp.float32)
         dec_shards, _, squares = reduce_grads([g_dec_in, g_dec_down], nothing, nothing, False, 1)
         enc_shards, summed, squares = reduce_grads(
-            [g_enc_in, g_enc_mats[3], g_embed], small, squares, True, 2
+            [g_enc_in, g_enc_down, g_embed], small, squares, True, 2
         )
         rows = norm_vectors.shape[0]
         vector_sums = summed[:-8].reshape(-1)
@@ -1015,7 +1161,7 @@
         reduced = lax.psum(
             tuple(
                 lax.psum_scatter(grad, "clip", scatter_dimension=0, tiled=True)
-                for grad in (g_embed, g_enc_in, g_enc_mats[3], g_dec_in, g_dec_down, g_vectors)
+                for grad in (g_embed, g_enc_in, g_enc_down, g_dec_in, g_dec_down, g_vectors)
             ),
             "band",
         )

time: 786 us -> 673 us (0.86)
  matrix products: 164 us -> 0 us
  Pallas kernels: 512 us -> 589 us
  other arithmetic: 52.7 us -> 39.8 us
  local copies, waits for them, and re-layouts: 43.5 us -> 34.3 us
    dot_general x22 -> x0, matrix products: 154 us -> none  [the longest x1 27.5 us: attend_back(): jnp.einsum('bhqk,bqhd->bkhd', scaled, query, preferred_element_type=jnp.f...]
    pallas_call x0 -> x2, Pallas kernels: none -> 121 us  [the longest x1 70.9 us: encoder_backward(): pl.pallas_call(functools.partial(encoder_backward_kernel, heads), out_sha...]
    pallas_call x1, Pallas kernels: 205 us -> 161 us  [decoder_step(): pl.pallas_call(functools.partial(decoder_kernel, coef, heads), out_shape=...]
    sub x1 -> x0, matrix products: 10.3 us -> none  [softmax_probs(): return jax.nn.softmax(scores * head_size ** (-0.5) + score_bias, axis=-1)]
where the time goes in v4:
time: 673 us; the launch traced here: 667 us
  Pallas kernels  589 us (88%)
  other arithmetic  39.8 us (6%)
  local copies, waits for them, and re-layouts  34.3 us (5%)
    pallas_call x2, Pallas kernels, reduce_grads(): pl.pallas_call(functools.partial(reduce_kernel, tuple(widths), n), out_sh...  191 us
    pallas_call x1, Pallas kernels, decoder_step(): pl.pallas_call(functools.partial(decoder_kernel, coef, heads), out_shape=...  161 us
    pallas_call x1, Pallas kernels, gather_weights(): pl.pallas_call(functools.partial(gather_kernel, chunks, n), out_shape=tup...  117 us
    pallas_call x1, Pallas kernels, encoder_backward(): pl.pallas_call(functools.partial(encoder_backward_kernel, heads), out_sha...  70.9 us
    pallas_call x1, Pallas kernels, encoder_forward(): pl.pallas_call(functools.partial(encoder_forward_kernel, heads), out_shap...  49.8 us

profile of v4, /device:TPU:0, one launch (start us, length us, event | category | flops | bytes accessed | tf_op | source)
XLA Modules:
  0.0 667.0 jit_solution(15224977580205393300)
XLA Ops:
  4.6 2.3 multiply_sine_fusion.3
  8.2 3.5 multiply_sine_fusion.1
  11.7 1.4 pad_maximum_fusion.pos_ref
  13.8 3.4 gather_fusion
  17.2 3.0 convert_element_type.52
  24.5 116.8 %gather.13 = (bf16[4,2,2,16,768]{4,3,2,1,0:T(8,128)(2,1)}, bf16[4,2,2,48,6656]{4,3,2,1,0:T(8,128)(2,1)}, bf16[4,2,2,192,768]{4,3,2,1,0:T(8,128)(2,1)}, bf16[4,2,...) custom-call(bf16[2,16,768]{2,1,0:T(8,128)(2,1)} %bitcast.113, ...), custom_call_target="tpu_custom_call" | custom-call | tf_op jit(solution)/shard_map/gather/pallas_call | solution.py:992
  142.0 1.8 broadcast_in_dim.34.vec_ref
  145.3 49.8 %encode.1 = (bf16[512,640]{1,0:T(8,128)(2,1)}, f32[640,640]{1,0:T(8,128)}, bf16[256,640]{1,0:T(8,128)(2,1)}, f32[768,640]{1,0:T(8,128)}, bf16[768,640]{1,0:T(8,1...) custom-call(bf16[640,256]{1,0:T(8,128)(2,1)} %gather_fusion, ...), custom_call_target="tpu_custom_call" | custom-call | tf_op jit(solution)/shard_map/encode/pallas_call | solution.py:390
  197.1 2.6 gather_fusion.1
  201.2 6.6 copy.50
  207.8 2.4 copy.54
  210.2 1.8 broadcast_in_dim.38.vec_ref
  212.9 161.2 %decoder.1 = (f32[512,4352]{1,0:T(8,128)}, f32[2048,512]{1,0:T(8,128)}, f32[7,512,128]{2,1,0:T(8,128)}, f32[512,640]{1,0:T(8,128)}, f32[8,128]{1,0:T(8,128)}) custom-call(s32[6]{0:T(128)} %slice.29.shift_ref, s32[640,128]{1,0:T(8,128)} %broadcast_in_dim.27.rvis_ref, bf16[512,640]{1,0:T(8,128)(2,1)} %get-tuple-element.61.gvt_ref, ...), custom_call_target="tpu_custom_call" | custom-call | tf_op jit(solution)/shard_map/decoder/pallas_call | solution.py:251
  374.6 68.8 %reduce.6 = (f32[2,32,4352]{2,1,0:T(8,128)}, f32[2,128,512]{2,1,0:T(8,128)}, f32[8,128]{1,0:T(8,128)}, f32[8,128]{1,0:T(8,128)}) custom-call(f32[4,2,2,32,4352]{4,3,2,1,0:T(8,128)} %bitcast.101, f32[4,2,2,128,512]{4,3,2,1,0:T(8,128)} %bitcast.107, f32[8,128]{1,0:T(8,128)} %broadcast_in_dim.39.refs_2_.refs_3_, f32[8,128]{1,0:T(8,128)} %broadcast_in_dim.39.refs_2_.refs_3_), custom_call_target="tpu_custom_call" | custom-call | tf_op jit(solution)/shard_map/reduce/pallas_call | solution.py:817
  443.4 70.9 %encode_back.1 = (f32[768,6656]{1,0:T(8,128)}, f32[3072,768]{1,0:T(8,128)}, f32[256,768]{1,0:T(8,128)}, f32[6,768,128]{2,1,0:T(8,128)}) custom-call(f32[512,640]{1,0:T(8,128)} %get-tuple-element.64.gp_ref, f32[6,768,128]{2,1,0:T(8,128)} %broadcast_in_dim.34.vec_ref, bf16[768,6656]{1,0:T(8,128)(2,1)} %bitcast.92, bf16[3072,768]{1,0:T(8,128)(2,1)} %bitcast.95, ...), custom_call_target="tpu_custom_call" | custom-call | tf_op jit(solution)/shard_map/encode_back/pallas_call | solution.py:524
  514.3 2.5 reduce_sum.144
  517.4 1.3 slice_reduce_fusion
  520.0 121.8 %reduce.7 = (f32[2,48,6656]{2,1,0:T(8,128)}, f32[2,192,768]{2,1,0:T(8,128)}, f32[2,16,768]{2,1,0:T(8,128)}, f32[72,128]{1,0:T(8,128)}, f32[8,128]{1,0:T(8,128)}) custom-call(f32[4,2,2,48,6656]{4,3,2,1,0:T(8,128)} %bitcast.93, f32[4,2,2,192,768]{4,3,2,1,0:T(8,128)} %bitcast.100, f32[4,2,2,16,768]{4,3,2,1,0:T(8,128)} %bitcast.111, ...), custom_call_target="tpu_custom_call" | custom-call | tf_op jit(solution)/shard_map/reduce/pallas_call | solution.py:817
  641.8 1.5 slice_bitcast_fusion
  643.2 1.3 reduce_sum.147
  646.6 1.4 multiply_subtract_fusion.3
  649.7 2.3 multiply_subtract_fusion.2
  653.7 2.4 multiply_subtract_fusion.1
  659.1 4.5 multiply_subtract_fusion
  (112 shorter events, 28.3 us)
Async XLA Ops:
  11.7 2.1 copy-start
  17.2 3.0 copy-start.3
  20.2 2.3 copy-start.10
  21.1 2.2 copy-start.22
  21.1 2.8 copy-start.27
  201.2 6.6 copy-start.2
  207.8 2.4 copy-start.26
  514.3 2.5 copy-start.12
  520.0 125.9 %copy-start.28 = (f32[1024]{0:T(1024)S(1)}, f32[1024]{0:T(1024)}, u32[]{:S(2)}) copy-start(f32[1024]{0:T(1024)} %param.37) | copy-start | bytes 12292
  520.0 125.9 %copy-start.29 = (f32[1024]{0:T(1024)S(1)}, f32[1024]{0:T(1024)}, u32[]{:S(2)}) copy-start(f32[1024]{0:T(1024)} %param.43) | copy-start | bytes 12292
  520.0 126.6 %copy-start.21 = (f32[2,128,512]{2,1,0:T(8,128)S(1)}, f32[2,128,512]{2,1,0:T(8,128)}, u32[]{:S(2)}) copy-start(f32[2,128,512]{2,1,0:T(8,128)} %get-tuple-element.93) | copy-start | bytes 1572868
  520.0 126.6 %copy-start.20 = (f32[256,512]{1,0:T(8,128)S(1)}, f32[256,512]{1,0:T(8,128)}, u32[]{:S(2)}) copy-start(f32[256,512]{1,0:T(8,128)} %param.42) | copy-start | bytes 1572868
  641.7 4.8 copy-start.11
  641.7 4.8 copy-start.19
  646.6 2.1 copy-start.18
  649.7 2.3 copy-start.13
  649.7 2.5 copy-start.15
  653.7 2.7 copy-start.9
  653.7 3.8 copy-start.8
  656.4 2.0 copy-start.1
  656.4 2.8 copy-start.7
  659.1 4.5 copy-start.23
  659.1 4.5 copy-start.24
  659.1 4.5 copy-start.25
  (6 other events, 9.0 us)

commit v5 on v4

--- a/solution.py
+++ b/solution.py
@@ -48,9 +48,9 @@
 
 
 def decoder_kernel(
-    coef, heads, shift_ref, rvis_ref, gvt_ref, pix_ref, et_ref, ef_ref, vec_ref, w_ref, wt_ref, wd_ref, wdt_ref,
+    coef, heads, shift_ref, rvis_ref, gvt_ref, pix_ref, et_ref, ef_ref, vec_ref, w_ref, wd_ref,
     gin_ref, gdown_ref, gvec_ref, gp_ref, loss_ref,
-    res, xh1, xh2, xh3, tmp, n1, n2, fin, rs, qkv, att, act, dgel, probs, dqkv, dup, low, oh, mrow, hb, hm, wm,
+    wt_ref, wdt_ref, res, xh1, xh2, xh3, tmp, n1, n2, fin, rs, qkv, att, act, dgel, probs, dqkv, dup, low, oh, mrow, hb, hm, wm,
 ):
     width = w_ref.shape[0]
     hidden = wd_ref.shape[0]
@@ -65,6 +65,15 @@
     nblk = pix_ref.shape[0] // rows
     chunk = 512
 
+    def turn_in(i):
+        at = pl.ds(pl.multiple_of(i * 256, 256), 256)
+        wt_ref[at, :] = w_ref[:, at].T
+    loop(w_ref.shape[1] // 256, turn_in)
+
+    def turn_down(i):
+        at = pl.ds(pl.multiple_of(i * 256, 256), 256)
+        wdt_ref[:, at] = wd_ref[at, :].T
+    loop(hidden // 256, turn_down)
     gin_ref[...] = jnp.zeros_like(gin_ref)
     gdown_ref[...] = jnp.zeros_like(gdown_ref)
     gvec_ref[...] = jnp.zeros_like(gvec_ref)
@@ -155,7 +164,7 @@
             q = qkv[pl.ds(f0, 128), at]
             k = qkv[pl.ds(width + f0, 128), at]
             v = qkv[pl.ds(2 * width + f0, 128), at]
-            s = mm(k.T, wide(q, 128 * per) * hm[...])
+            s = jnp.concatenate([mm(k[size * h : size * h + size], q[size * h : size * h + size], 0, 0) for h in range(per)], axis=1)
             c = compact(s) * scale + hb[...]
             e = jnp.exp(c - jnp.max(c, axis=0, keepdims=True))
             p = e * (1.0 / jnp.sum(e, axis=0, keepdims=True))
@@ -216,7 +225,7 @@
             v = qkv[pl.ds(2 * width + f0, 128), at]
             do = fin[pl.ds(f0, 128), at]
             do_all = wide(do, 128 * per) * hm[...]
-            dp = compact(mm(v.T, do_all))
+            dp = compact(jnp.concatenate([mm(v[size * h : size * h + size], do[size * h : size * h + size], 0, 0) for h in range(per)], axis=1))
             p = probs[i]
             ds = p * (dp - jnp.sum(dp * p, axis=0, keepdims=True))
             p_all = jnp.concatenate([p.astype(BF16)] * 4, axis=0) * wm[...]
@@ -239,7 +248,7 @@
     loop(nblk, block)
 
 
-def decoder_step(shift, rvis, gvt, pix, et, ef, vec, w, wt, wd, wdt, coef, heads):
+def decoder_step(shift, rvis, gvt, pix, et, ef, vec, w, wd, coef, heads):
     width, total = w.shape
     hidden = wd.shape[0]
     rows = 512
@@ -257,10 +266,10 @@
             jax.ShapeDtypeStruct((width, vis), F32),
             jax.ShapeDtypeStruct((8, 128), F32),
         ),
-        in_specs=[pl.BlockSpec(memory_space=pltpu.SMEM)] + [vmem] * 10,
+        in_specs=[pl.BlockSpec(memory_space=pltpu.SMEM)] + [vmem] * 8,
         out_specs=(vmem,) * 5,
         scratch_shapes=[
-            f(width, rows), f(width, rows), f(width, rows), f(width, rows), f(width, rows),
+            b(total, width), b(width, hidden), f(width, rows), f(width, rows), f(width, rows), f(width, rows), f(width, rows),
             b(width, rows), b(width, rows), b(width, rows), f(24, rows),
             b(3 * width, rows), b(width, rows), b(hidden, rows), f(hidden, rows),
             f(rows // 128 * (width // 128), 32, 128 * per), b(3 * width, rows), b(hidden, rows), b(width, rows),
@@ -268,7 +277,7 @@
         ],
         compiler_params=pltpu.CompilerParams(vmem_limit_bytes=63 * 2**20),
         name="decoder",
-    )(shift, rvis, gvt, pix, et, ef, vec, w, wt, wd, wdt)
+    )(shift, rvis, gvt, pix, et, ef, vec, w, wd)
 
 
 CHUNK = 768
@@ -282,16 +291,22 @@
     return pl.ds(pl.multiple_of(base + i * CHUNK, 128), CHUNK)
 
 
-def encoder_scores(q, k, bias, scale):
-    c = mm(k, q, 0, 0) * scale + bias
-    e = jnp.exp(c - jnp.max(c, axis=0, keepdims=True))
+def encoder_clips(seg_ref, own, others):
+    clip = lax.broadcasted_iota(jnp.int32, own.shape, 0) == seg_ref[0:1]
+    own[...] = jnp.where(clip, 1.0, 0.0).astype(BF16)
+    others[...] = jnp.where(clip, 0.0, -1e31).astype(BF16)
+
+
+def encoder_scores(q, k, scale):
+    c = mm(k, q)
+    e = jnp.exp2((c - jnp.max(c, axis=0, keepdims=True)) * (scale * 1.4426950408889634))
     return e * (1.0 / jnp.sum(e, axis=0, keepdims=True))
 
 
 def encoder_forward_kernel(
-    heads, seen_ref, pos_ref, grid_pos_ref, segc_ref, segr_ref, vec_ref, we_ref, wi_ref, wd_ref,
-    grid_ref, bias_ref, seen_t_ref, xh1_ref, n1_ref, qkv_ref, att_ref, xh2_ref, n2_ref, act_ref, dgel_ref, xh3_ref, fin_ref, rs_ref,
-    we, wi, wd, res, bias, seen_t, xh1, n1, qkv, att, xh2, n2, act, dgel, xh3, fin, rs, w_sem, o_sem,
+    heads, seen_ref, pos_ref, grid_pos_ref, seg_ref, vec_ref, we_ref, wi_ref, wd_ref,
+    grid_ref, seen_t_ref, xh1_ref, n1_ref, qkv_ref, att_ref, xh2_ref, n2_ref, act_ref, dgel_ref, xh3_ref, fin_ref, rs_ref,
+    we, wi, wd, res, own, others, seen_t, xh1, n1, qkv, att, xh2, n2, act, dgel, xh3, fin, rs, w_sem, o_sem,
 ):
     width, hidden = we.shape[1], wd.shape[0]
     rows = res.shape[1]
@@ -307,7 +322,7 @@
     for load in loads:
         load.start()
     pairs = (
-        (bias, bias_ref), (seen_t, seen_t_ref), (xh1, xh1_ref), (n1, n1_ref), (qkv, qkv_ref), (att, att_ref), (xh2, xh2_ref),
+        (seen_t, seen_t_ref), (xh1, xh1_ref), (n1, n1_ref), (qkv, qkv_ref), (att, att_ref), (xh2, xh2_ref),
         (n2, n2_ref), (act, act_ref), (dgel, dgel_ref), (xh3, xh3_ref), (fin, fin_ref), (rs, rs_ref),
     )
     saves = [pltpu.make_async_copy(a, b, o_sem.at[i]) for i, (a, b) in enumerate(pairs)]
@@ -325,35 +340,35 @@
             body(i)
 
     seen_t[...] = seen_ref[...].T
-    saves[1].start()
-    bias[...] = jnp.where(wide(segc_ref[...], rows) == segr_ref[0:1], 0.0, -1e30)
     saves[0].start()
+    encoder_clips(seg_ref, own, others)
     loads[0].wait()
     res[...] = mm(we[...], seen_t[...], 0, 0) + pos_ref[...]
     ln_forward(0, xh1, n1)
+    saves[1].start()
     saves[2].start()
-    saves[3].start()
     loads[1].wait()
 
     def qkv_part(i):
         qkv[part(i), :] = mm(wi[:, part(i)], n1[...], 0, 0).astype(BF16)
-    loop(3, qkv_part)
-    saves[4].start()
+    loop(3, qkv_part, 3)
+    saves[3].start()
 
     def attend(h):
         f0 = pl.multiple_of(h * size, size)
-        k = qkv[pl.ds(width + f0, size), :]
+        k = jnp.concatenate([qkv[pl.ds(width + f0, size), :], others[...]], axis=0).T
         v = qkv[pl.ds(2 * width + f0, size), :]
         for i in range(rows // 128):
-            p = encoder_scores(qkv[pl.ds(f0, size), lane(i)], k, bias[:, lane(i)], scale)
+            q = jnp.concatenate([qkv[pl.ds(f0, size), lane(i)], own[:, lane(i)]], axis=0)
+            p = encoder_scores(q, k, scale)
             att[pl.ds(f0, size), lane(i)] = mm(v, p.astype(BF16)).astype(BF16)
-    loop(heads, attend)
-    saves[5].start()
+    loop(heads, attend, 4)
+    saves[4].start()
     loads[2].wait()
     res[...] += mm(wi[:, c_out:c_up], att[...], 0, 0)
     ln_forward(1, xh2, n2)
+    saves[5].start()
     saves[6].start()
-    saves[7].start()
     loads[3].wait()
 
     def up_part(i):
@@ -363,13 +378,13 @@
         v = u * hp
         act[part(i), :] = v.astype(BF16)
         dgel[part(i), :] = hp + (v - v * hp) * ((2 * GELU_C) + (6 * GELU_C * 0.044715) * square)
-    loop(hidden // CHUNK, up_part, 2)
+    loop(hidden // CHUNK, up_part, 4)
+    saves[7].start()
     saves[8].start()
-    saves[9].start()
     loads[4].wait()
     res[...] += mm(wd[...], act[...], 0, 0)
     ln_forward(2, xh3, fin)
-    for i in (10, 11, 12):
+    for i in (9, 10, 11):
         saves[i].start()
     loads[5].wait()
     grid_ref[...] = (mm(wi[:, c_proj:], fin[...], 0, 0) + grid_pos_ref[...]).astype(BF16)
@@ -377,33 +392,33 @@
         save.wait()
 
 
-def encoder_forward(seen, pos, grid_pos, segc, segr, vec, we, wi, wd, heads):
+def encoder_forward(seen, pos, grid_pos, seg, vec, we, wi, wd, heads):
     rows, patch = seen.shape
     width, total = wi.shape
     hidden = wd.shape[0]
     any_, vmem = pl.BlockSpec(memory_space=pl.ANY), pl.BlockSpec(memory_space=pltpu.VMEM)
     saved = (
-        ((rows, rows), F32), ((patch, rows), BF16), ((width, rows), F32), ((width, rows), BF16), ((3 * width, rows), BF16),
+        ((patch, rows), BF16), ((width, rows), F32), ((width, rows), BF16), ((3 * width, rows), BF16),
         ((width, rows), BF16), ((width, rows), F32), ((width, rows), BF16), ((hidden, rows), BF16), ((hidden, rows), F32),
         ((width, rows), F32), ((width, rows), BF16), ((24, rows), F32),
     )
     return pl.pallas_call(
         functools.partial(encoder_forward_kernel, heads),
         out_shape=(jax.ShapeDtypeStruct((grid_pos.shape[0], rows), BF16),) + tuple(jax.ShapeDtypeStruct(*s) for s in saved),
-        in_specs=[vmem] * 6 + [any_] * 3,
+        in_specs=[vmem] * 5 + [any_] * 3,
         out_specs=(vmem,) + (any_,) * len(saved),
         scratch_shapes=[pltpu.VMEM(we.shape, BF16), pltpu.VMEM(wi.shape, BF16), pltpu.VMEM(wd.shape, BF16), pltpu.VMEM((width, rows), F32)]
-        + [pltpu.VMEM(*s) for s in saved] + [pltpu.SemaphoreType.DMA((6,)), pltpu.SemaphoreType.DMA((len(saved),))],
+        + [pltpu.VMEM((16, rows), BF16)] * 2 + [pltpu.VMEM(*s) for s in saved] + [pltpu.SemaphoreType.DMA((6,)), pltpu.SemaphoreType.DMA((len(saved),))],
         compiler_params=pltpu.CompilerParams(vmem_limit_bytes=62 * 2**20),
         name="encode",
-    )(seen, pos, grid_pos, segc, segr, vec, we, wi, wd)
+    )(seen, pos, grid_pos, seg, vec, we, wi, wd)
 
 
 def encoder_backward_kernel(
-    heads, gp_ref, vec_ref, wi_ref, wd_ref,
-    bias_ref, seen_t_ref, xh1_ref, n1_ref, qkv_ref, att_ref, xh2_ref, n2_ref, act_ref, dgel_ref, xh3_ref, fin_ref, rs_ref,
+    heads, gp_ref, vec_ref, seg_ref, wi_ref, wd_ref,
+    seen_t_ref, xh1_ref, n1_ref, qkv_ref, att_ref, xh2_ref, n2_ref, act_ref, dgel_ref, xh3_ref, fin_ref, rs_ref,
     gin_ref, gdown_ref, gembed_ref, gvec_ref,
-    wi, wd, res, tmp, low, dqkv, probs, dscores, stage, bias, seen_t, xh1, n1, qkv, att, xh2, n2, act, dgel, rs, i_sem, s_sem,
+    wi, wd, res, tmp, low, dqkv, probs, dscores, stage, own, others, seen_t, xh1, n1, qkv, att, xh2, n2, act, dgel, rs, i_sem, s_sem,
 ):
     width, hidden = wi.shape[0], wd.shape[0]
     rows = res.shape[1]
@@ -423,12 +438,13 @@
     first = [load(0, fin_ref, n1), columns(1, c_proj, total), load(2, xh3_ref, xh1), load(3, rs_ref, rs)]
     mlp = [load(4, wd_ref, wd), load(5, dgel_ref, dgel), load(6, act_ref, act), load(7, n2_ref, n2)]
     second = [columns(8, c_up, c_proj), load(9, xh2_ref, xh2), columns(10, c_out, c_up), load(11, att_ref, att)]
-    attention = [load(12, qkv_ref, qkv), load(13, bias_ref, bias), columns(14, 0, c_out), load(15, seen_t_ref, seen_t)]
+    attention = [load(12, qkv_ref, qkv), columns(14, 0, c_out), load(15, seen_t_ref, seen_t)]
     again = [load(16, xh1_ref, xh1), load(17, n1_ref, n1)]
     for group in (first, mlp, second, attention):
         for copy in group:
             copy.start()
     gvec_ref[...] = jnp.zeros_like(gvec_ref)
+    encoder_clips(seg_ref, own, others)
 
     open_copies = [None, None]
     turn = [0]
@@ -491,16 +507,19 @@
         k = qkv[pl.ds(width + f0, size), :]
         v = qkv[pl.ds(2 * width + f0, size), :]
         do = att[mine, :]
+        keys = jnp.concatenate([k, others[...]], axis=0).T
+        values = v.T
         for i in range(rows // 128):
-            p = encoder_scores(q[:, 128 * i : 128 * i + 128], k, bias[:, lane(i)], scale)
-            dp = mm(v, do[:, 128 * i : 128 * i + 128], 0, 0)
+            part_q = jnp.concatenate([q[:, 128 * i : 128 * i + 128], own[:, lane(i)]], axis=0)
+            p = encoder_scores(part_q, keys, scale)
+            dp = mm(values, do[:, 128 * i : 128 * i + 128])
             ds = p * (dp - jnp.sum(dp * p, axis=0, keepdims=True))
             probs[:, lane(i)] = p.astype(BF16)
             dscores[:, lane(i)] = (ds * scale).astype(BF16)
         dqkv[mine, :] = mm(k, dscores[...]).astype(BF16)
         dqkv[pl.ds(width + f0, size), :] = mm(q, dscores[...], 1, 1).astype(BF16)
         dqkv[pl.ds(2 * width + f0, size), :] = mm(do, probs[...], 1, 1).astype(BF16)
-    loop(heads, attend_back)
+    loop(heads, attend_back, 3)
     for copy in again:
         copy.wait()
     for i in range(3 * width // CHUNK):
@@ -513,7 +532,7 @@
         copy.wait()
 
 
-def encoder_backward(gp, vec, wi, wd, saved, patch, heads):
+def encoder_backward(gp, vec, seg, wi, wd, saved, patch, heads):
     rows = gp.shape[1]
     width, total = wi.shape
     hidden = wd.shape[0]
@@ -524,17 +543,17 @@
     return pl.pallas_call(
         functools.partial(encoder_backward_kernel, heads),
         out_shape=(shape(width, total), shape(hidden, width), shape(patch, width), shape(6, width, 128)),
-        in_specs=[vmem] * 2 + [any_] * (2 + len(saved)),
+        in_specs=[vmem] * 3 + [any_] * (2 + len(saved)),
         out_specs=(any_,) * 3 + (vmem,),
         scratch_shapes=[
             b(*wi.shape), b(*wd.shape), f(width, rows), f(width, rows), b(width, rows), b(3 * width, rows), b(rows, rows), b(rows, rows),
-            f(2, CHUNK, CHUNK), f(rows, rows), b(patch, rows), f(width, rows), b(width, rows), b(3 * width, rows), b(width, rows),
+            f(2, CHUNK, CHUNK), b(16, rows), b(16, rows), b(patch, rows), f(width, rows), b(width, rows), b(3 * width, rows), b(width, rows),
             f(width, rows), b(width, rows), b(hidden, rows), f(hidden, rows), f(24, rows),
             pltpu.SemaphoreType.DMA((18,)), pltpu.SemaphoreType.DMA((2,)),
         ],
         compiler_params=pltpu.CompilerParams(vmem_limit_bytes=63 * 2**20),
         name="encode_back",
-    )(gp, vec, wi, wd, *saved)
+    )(gp, vec, seg, wi, wd, *saved)
 
 
 def place():
@@ -1101,7 +1120,8 @@
     seen = pixels[spots]
     column, band = spots // 8, spots % 8
     segment, seen_start, seen_size, seen_shift, _ = clip_of(column, lengths[0], shifts[0])
-    segment = jnp.where(real, segment, -1).astype(jnp.int32)
+    segment = jnp.where(real, segment, 15).astype(jnp.int32)
+    segment = jnp.broadcast_to(segment[None, :], (8, padded))
     seen_time = column - seen_start
     decoder_row = jnp.where(real, 8 * (seen_start + (seen_time + seen_shift) % seen_size) + band, -1)
     decoder_row = jnp.broadcast_to(decoder_row[:, None], (padded, 128)).astype(jnp.int32)
@@ -1113,8 +1133,7 @@
         seen,
         positions(enc_width),
         positions(dec_width),
-        jnp.broadcast_to(segment[:, None], (padded, 128)),
-        jnp.broadcast_to(segment[None, :], (8, padded)),
+        segment,
         enc_gains,
         w_embed,
         w_enc,
@@ -1131,15 +1150,13 @@
         band_table,
         dec_gains,
         w_dec,
-        w_dec.T,
         w_dec_down,
-        w_dec_down.T,
         2.0 / (pixels.shape[1] * masked_count),
         HEADS_DEC,
     )
     local_loss = jnp.sum(loss[0])
     g_enc_in, g_enc_down, g_embed, g_enc_vectors = encoder_backward(
-        grad_grid, enc_gains, w_enc, w_enc_down, saved, pixels.shape[1], HEADS_ENC
+        grad_grid, enc_gains, segment, w_enc, w_enc_down, saved, pixels.shape[1], HEADS_ENC
     )
     g_vectors = jnp.concatenate(
         [jnp.sum(g_enc_vectors, axis=2).reshape(-1), jnp.sum(g_dec_vectors, axis=2).reshape(-1)]

time: 673 us -> 655 us (0.973)
  local copies, waits for them, and re-layouts: 34.3 us -> 24.4 us
  Pallas kernels: 589 us -> 581 us
    reshape x2 -> x0, local copies, waits for them, and re-layouts: 9 us -> none  [gather_weights(): return ([o.reshape(-1, o.shape[4]) for o in out[:n]], out[n].reshape(-1))]
where the time goes in v5:
time: 655 us; the launch traced here: 649 us
  Pallas kernels  581 us (89%)
  other arithmetic  39.8 us (6%)
  local copies, waits for them, and re-layouts  24.4 us (4%)
    pallas_call x2, Pallas kernels, reduce_grads(): pl.pallas_call(functools.partial(reduce_kernel, tuple(widths), n), out_sh...  190 us
    pallas_call x1, Pallas kernels, decoder_step(): pl.pallas_call(functools.partial(decoder_kernel, coef, heads), out_shape=...  157 us
    pallas_call x1, Pallas kernels, gather_weights(): pl.pallas_call(functools.partial(gather_kernel, chunks, n), out_shape=tup...  117 us
    pallas_call x1, Pallas kernels, encoder_backward(): pl.pallas_call(functools.partial(encoder_backward_kernel, heads), out_sha...  69.8 us
    pallas_call x1, Pallas kernels, encoder_forward(): pl.pallas_call(functools.partial(encoder_forward_kernel, heads), out_shap...  47.4 us

profile of v5, /device:TPU:0, one launch (start us, length us, event | category | flops | bytes accessed | tf_op | source)
XLA Modules:
  0.0 649.4 jit_solution(15460888497771284322)
XLA Ops:
  4.6 2.3 multiply_sine_fusion.3
  8.1 3.5 multiply_sine_fusion.1
  11.6 1.4 pad_maximum_fusion.pos_ref
  13.7 3.4 gather_fusion
  17.1 3.0 convert_element_type.52
  24.4 116.8 %gather.13 = (bf16[4,2,2,16,768]{4,3,2,1,0:T(8,128)(2,1)}, bf16[4,2,2,48,6656]{4,3,2,1,0:T(8,128)(2,1)}, bf16[4,2,2,192,768]{4,3,2,1,0:T(8,128)(2,1)}, bf16[4,2,...) custom-call(bf16[2,16,768]{2,1,0:T(8,128)(2,1)} %bitcast.107, ...), custom_call_target="tpu_custom_call" | custom-call | tf_op jit(solution)/shard_map/gather/pallas_call | solution.py:1011
  142.0 1.8 broadcast_in_dim.33.vec_ref
  144.4 47.4 %encode.1 = (bf16[512,640]{1,0:T(8,128)(2,1)}, bf16[256,640]{1,0:T(8,128)(2,1)}, f32[768,640]{1,0:T(8,128)}, bf16[768,640]{1,0:T(8,128)(2,1)}, bf16[2304,640]{1,...) custom-call(bf16[640,256]{1,0:T(8,128)(2,1)} %gather_fusion, ...), custom_call_target="tpu_custom_call" | custom-call | tf_op jit(solution)/shard_map/encode/pallas_call | solution.py:405
  193.8 2.6 gather_fusion.1
  197.9 1.8 broadcast_in_dim.38.vec_ref
  200.5 156.9 %decoder.1 = (f32[512,4352]{1,0:T(8,128)}, f32[2048,512]{1,0:T(8,128)}, f32[7,512,128]{2,1,0:T(8,128)}, f32[512,640]{1,0:T(8,128)}, f32[8,128]{1,0:T(8,128)}) custom-call(s32[6]{0:T(128)} %slice.29.shift_ref, s32[640,128]{1,0:T(8,128)} %broadcast_in_dim.27.rvis_ref, bf16[512,640]{1,0:T(8,128)(2,1)} %get-tuple-element.60.gvt_ref, bf16[3072,256]{1,0:T(8,128)(2,1)} %bitcast.97, ...), custom_call_target="tpu_custom_call" | custom-call | tf_op jit(solution)/shard_map/decoder/pallas_call | solution.py:260
  358.1 68.7 %reduce.6 = (f32[2,32,4352]{2,1,0:T(8,128)}, f32[2,128,512]{2,1,0:T(8,128)}, f32[8,128]{1,0:T(8,128)}, f32[8,128]{1,0:T(8,128)}) custom-call(f32[4,2,2,32,4352]{4,3,2,1,0:T(8,128)} %bitcast.96, f32[4,2,2,128,512]{4,3,2,1,0:T(8,128)} %bitcast.100, f32[8,128]{1,0:T(8,128)} %broadcast_in_dim.39.refs_2_.refs_3_, f32[8,128]{1,0:T(8,128)} %broadcast_in_dim.39.refs_2_.refs_3_), custom_call_target="tpu_custom_call" | custom-call | tf_op jit(solution)/shard_map/reduce/pallas_call | solution.py:836
  426.8 69.8 %encode_back.1 = (f32[768,6656]{1,0:T(8,128)}, f32[3072,768]{1,0:T(8,128)}, f32[256,768]{1,0:T(8,128)}, f32[6,768,128]{2,1,0:T(8,128)}) custom-call(f32[512,640]{1,0:T(8,128)} %get-tuple-element.63.gp_ref, f32[6,768,128]{2,1,0:T(8,128)} %broadcast_in_dim.33.vec_ref, s32[8,640]{1,0:T(8,128)} %broadcast_in_dim.31.seg_ref, bf16[768,6656]{1,0:T(8,128)(2,1)} %bitcast.90, ...), custom_call_target="tpu_custom_call" | custom-call | tf_op jit(solution)/shard_map/encode_back/pallas_call | solution.py:543
  496.7 2.5 reduce_sum.144
  499.8 1.3 slice_reduce_fusion
  501.0 1.3 concatenate.23.refs_3_
  502.3 121.7 %reduce.7 = (f32[2,48,6656]{2,1,0:T(8,128)}, f32[2,192,768]{2,1,0:T(8,128)}, f32[2,16,768]{2,1,0:T(8,128)}, f32[72,128]{1,0:T(8,128)}, f32[8,128]{1,0:T(8,128)}) custom-call(f32[4,2,2,48,6656]{4,3,2,1,0:T(8,128)} %bitcast.91, f32[4,2,2,192,768]{4,3,2,1,0:T(8,128)} %bitcast.95, f32[4,2,2,16,768]{4,3,2,1,0:T(8,128)} %bitcast.105, ...), custom_call_target="tpu_custom_call" | custom-call | tf_op jit(solution)/shard_map/reduce/pallas_call | solution.py:836
  624.1 1.5 slice_bitcast_fusion
  625.5 1.3 reduce_sum.147
  629.0 1.4 multiply_subtract_fusion.3
  632.1 2.3 multiply_subtract_fusion.2
  636.0 2.4 multiply_subtract_fusion.1
  641.5 4.5 multiply_subtract_fusion
  646.8 1.2 slice.35
  (107 shorter events, 24.9 us)
Async XLA Ops:
  11.6 2.1 copy-start
  17.1 3.0 copy-start.2
  20.1 2.3 copy-start.9
  21.0 2.2 copy-start.21
  21.0 2.8 copy-start.26
  193.8 4.0 copy-start.25
  496.7 2.5 copy-start.11
  502.3 125.9 %copy-start.27 = (f32[1024]{0:T(1024)S(1)}, f32[1024]{0:T(1024)}, u32[]{:S(2)}) copy-start(f32[1024]{0:T(1024)} %param.37) | copy-start | bytes 12292
  502.3 125.9 %copy-start.28 = (f32[1024]{0:T(1024)S(1)}, f32[1024]{0:T(1024)}, u32[]{:S(2)}) copy-start(f32[1024]{0:T(1024)} %param.43) | copy-start | bytes 12292
  502.3 126.6 %copy-start.20 = (f32[2,128,512]{2,1,0:T(8,128)S(1)}, f32[2,128,512]{2,1,0:T(8,128)}, u32[]{:S(2)}) copy-start(f32[2,128,512]{2,1,0:T(8,128)} %get-tuple-element.91) | copy-start | bytes 1572868
  502.3 126.6 %copy-start.19 = (f32[256,512]{1,0:T(8,128)S(1)}, f32[256,512]{1,0:T(8,128)}, u32[]{:S(2)}) copy-start(f32[256,512]{1,0:T(8,128)} %param.42) | copy-start | bytes 1572868
  624.1 4.9 copy-start.10
  624.1 4.9 copy-start.18
  629.0 2.1 copy-start.17
  630.4 1.7 copy-start.16
  632.1 2.3 copy-start.12
  632.1 2.5 copy-start.14
  636.0 2.7 copy-start.8
  636.0 3.8 copy-start.7
  638.7 2.0 copy-start.1
  638.7 2.8 copy-start.6
  641.5 4.5 copy-start.22
  641.5 4.5 copy-start.23
  641.5 4.5 copy-start.24
  (5 other events, 7.3 us)

commit v6 on v5

--- a/solution.py
+++ b/solution.py
@@ -581,9 +581,9 @@
 
 
 def reduce_kernel(widths, n, *refs):
-    grads, small, before = refs[:n], refs[n], refs[n + 1]
-    outs, small_out, squares = refs[n + 2 : 2 * n + 2], refs[2 * n + 2], refs[2 * n + 3]
-    rest = refs[2 * n + 4 :]
+    grads, small = refs[:n], refs[n]
+    outs, small_out, squares = refs[n + 1 : 2 * n + 1], refs[2 * n + 1], refs[2 * n + 2]
+    rest = refs[2 * n + 3 :]
     sums, r0 = rest[:n], rest[n : 2 * n]
     coded = {1 + i: rest[(2 + i) * n : (3 + i) * n] for i in range(5)}
     came = {1 + i: rest[(7 + i) * n : (8 + i) * n] for i in range(5)}
@@ -612,6 +612,9 @@
             4: lambda: device(z, 1 - x, y, c),
             5: lambda: device(at_z(k), x, y, c),
         }[stage]()
+
+    def slot(stage, k):
+        return k - 1 if stage == 5 else k
 
     def copy(stage, t, k):
         if stage == 0:
@@ -622,7 +625,7 @@
             src = outs[t].at[:, :, columns(t, c)]
             dst, to = src, device(z, x, y, 1 - c)
         else:
-            src, dst, to = coded[stage][t].at[k], came[stage][t].at[k], target(stage, k)
+            src, dst, to = coded[stage][t].at[slot(stage, k)], came[stage][t].at[slot(stage, k)], target(stage, k)
         return remote(src, dst, send.at[t, stage, k], recv.at[t, stage, k], to)
 
     def steps(stage, t, k):
@@ -648,7 +651,7 @@
     def encode(stage, t, k, parts, read):
         rows = sums[t].shape[3]
         zk, width = at_z(k), coded[stage][t].shape[-1]
-        block = lambda p: coded[stage][t].at[(k, p) if parts > 1 else k]
+        block = lambda p: coded[stage][t].at[(k, p) if parts > 1 else slot(stage, k)]
         per = rows // 8
         def peak(i, most):
             return jnp.maximum(most, jnp.abs(read(zk, i // per, slab(i % per, 8))))
@@ -669,7 +672,7 @@
         copy(stage, t, k).wait_recv()
 
     def decoded(stage, t, k, p, rows, parts):
-        values = came[stage][t][(k, p, rows) if parts > 1 else (k, rows)]
+        values = came[stage][t][(k, p, rows) if parts > 1 else (slot(stage, k), rows)]
         return values.astype(jnp.int32).astype(F32) * step_in[stage][t][k]
 
     order = (2, 1, 3, 0)
@@ -769,7 +772,7 @@
         copy(7, t, 0).start()
 
     blocks = [(t, k) for t in range(n) for k in order]
-    total = before[...]
+    total = jnp.zeros((8, 128), F32)
     for i in range(len(blocks) + 2):
         if i < len(blocks):
             first_sum(*blocks[i])
@@ -790,12 +793,9 @@
     for t in late[:-1]:
         share(t)
     q_sum[...] = total
-    if q_buf.shape[0] > 1:
-        for stage in range(4):
-            advance(q_sum, q_buf, 6, stage)
-        finish_sum(q_sum, q_buf, 6, squares)
-    else:
-        squares[...] = total
+    for stage in range(4):
+        advance(q_sum, q_buf, 6, stage)
+    finish_sum(q_sum, q_buf, 6, squares)
     share(late[-1])
 
     def finish(k):
@@ -815,7 +815,7 @@
         copy(7, t, 0).wait()
 
 
-def reduce_grads(grads, small, before, last, ident):
+def reduce_grads(grads, small, ident):
     n = len(grads)
     views, widths = [], []
     scratch = [[] for _ in range(22)]
@@ -824,10 +824,10 @@
     for grad in grads:
         rows, cols = grad.shape
         r2, half = rows // 16, cols // 2
-        w = (half // 128 * 7 + 5) // 10 * 128
+        w = (half // 128 * 60 + 50) // 100 * 128
         views.append(grad.reshape(4, 2, 2, r2, cols))
         widths.append(w)
-        blocks = [(4, 2, r2, w), (4, 2, r2, half - w), (4, r2, w), (4, r2, half - w), (4, r2, half)]
+        blocks = [(4, 2, r2, w), (4, 2, r2, half - w), (4, r2, w), (4, r2, half - w), (3, r2, half)]
         for i, s in enumerate([f(4, 2, 2, r2, half)] * 2 + [q(*b) for b in blocks * 2] + [f(4, 1, b[-1]) for b in blocks * 2]):
             scratch[i].append(s)
     anywhere, vmem = pl.BlockSpec(memory_space=pl.ANY), pl.BlockSpec(memory_space=pltpu.VMEM)
@@ -837,17 +837,17 @@
         functools.partial(reduce_kernel, tuple(widths), n),
         out_shape=tuple(jax.ShapeDtypeStruct((2, v.shape[3], v.shape[4]), F32) for v in views)
         + (jax.ShapeDtypeStruct(small.shape, F32), square),
-        in_specs=[anywhere] * n + [vmem] * 2,
+        in_specs=[anywhere] * n + [vmem],
         out_specs=(anywhere,) * n + (vmem,) * 2,
         scratch_shapes=sum(scratch, []) + [
-            f(7, *small.shape), f(*small.shape), f(7 if last else 1, 8, 128), f(8, 128),
+            f(7, *small.shape), f(*small.shape), f(7, 8, 128), f(8, 128),
             dma((n, 8, 4)), dma((n, 8, 4)), dma((n, 5)), dma((n, 6, 4)), dma((n, 6, 4)), dma((12,)), dma((12,)),
         ],
         compiler_params=pltpu.CompilerParams(
-            collective_id=ident, has_side_effects=True, vmem_limit_bytes=60 * 2**20
+            collective_id=ident, has_side_effects=True, vmem_limit_bytes=63 * 2**20
         ),
         name="reduce",
-    )(*views, small, before)
+    )(*views, small)
     return [o.reshape(-1, o.shape[2]) for o in out[:n]], out[n], out[n + 1]
 
 
@@ -1163,15 +1163,13 @@
     )
     if direct:
         small = jnp.concatenate([g_vectors.reshape(-1, 128), jnp.full((8, 128), local_loss)])
-        nothing = jnp.zeros((8, 128), jnp.float32)
-        dec_shards, _, squares = reduce_grads([g_dec_in, g_dec_down], nothing, nothing, False, 1)
-        enc_shards, summed, squares = reduce_grads(
-            [g_enc_in, g_enc_down, g_embed], small, squares, True, 2
+        shard_sums, summed, squares = reduce_grads(
+            [g_enc_in, g_dec_in, g_enc_down, g_dec_down, g_embed], small, 1
         )
         rows = norm_vectors.shape[0]
         vector_sums = summed[:-8].reshape(-1)
         own = lax.dynamic_slice(vector_sums, (lax.axis_index("clip") * rows,), (rows,))
-        reduced = (enc_shards[2], enc_shards[0], enc_shards[1], *dec_shards, own)
+        reduced = (shard_sums[4], shard_sums[0], shard_sums[2], shard_sums[1], shard_sums[3], own)
         loss_sum = summed[-1, 0]
         norm_squared = jnp.sum(squares) + jnp.sum(vector_sums * vector_sums)
     else:

time: 655 us -> 643 us (0.982)
  Pallas kernels: 581 us -> 562 us
    pallas_call x2 -> x1, Pallas kernels: 190 us -> 171 us  [reduce_grads(): pl.pallas_call(functools.partial(reduce_kernel, tuple(widths), n), out_sh...]
where the time goes in v6:
time: 643 us; the launch traced here: 633 us
  Pallas kernels  562 us (87%)
  other arithmetic  43.1 us (7%)
  local copies, waits for them, and re-layouts  24.1 us (4%)
    pallas_call x1, Pallas kernels, reduce_grads(): pl.pallas_call(functools.partial(reduce_kernel, tuple(widths), n), out_sh...  171 us
    pallas_call x1, Pallas kernels, decoder_step(): pl.pallas_call(functools.partial(decoder_kernel, coef, heads), out_shape=...  157 us
    pallas_call x1, Pallas kernels, gather_weights(): pl.pallas_call(functools.partial(gather_kernel, chunks, n), out_shape=tup...  117 us
    pallas_call x1, Pallas kernels, encoder_backward(): pl.pallas_call(functools.partial(encoder_backward_kernel, heads), out_sha...  69.8 us
    pallas_call x1, Pallas kernels, encoder_forward(): pl.pallas_call(functools.partial(encoder_forward_kernel, heads), out_shap...  47.5 us

profile of v6, /device:TPU:0, one launch (start us, length us, event | category | flops | bytes accessed | tf_op | source)
XLA Modules:
  0.0 633.5 jit_solution(16536635946943927897)
XLA Ops:
  4.0 1.3 reduce-precision_bitcast_fusion.refs_5_
  7.9 1.5 convert_element_type.51
  10.2 1.8 convert_element_type.55
  12.0 3.2 gather_fusion
  20.9 2.3 multiply_sine_fusion.3
  24.4 2.6 gather_fusion.1
  26.9 3.5 multiply_sine_fusion.1
  30.4 1.4 pad_maximum_fusion.pos_ref
  31.8 116.8 %gather.13 = (bf16[4,2,2,16,768]{4,3,2,1,0:T(8,128)(2,1)}, bf16[4,2,2,48,6656]{4,3,2,1,0:T(8,128)(2,1)}, bf16[4,2,2,192,768]{4,3,2,1,0:T(8,128)(2,1)}, bf16[4,2,...) custom-call(bf16[2,16,768]{2,1,0:T(8,128)(2,1)} %bitcast.107, ...), custom_call_target="tpu_custom_call" | custom-call | tf_op jit(solution)/shard_map/gather/pallas_call | solution.py:1011
  150.1 1.8 broadcast_in_dim.36.vec_ref
  151.9 2.0 broadcast_in_dim.31.vec_ref
  153.8 47.5 %encode.1 = (bf16[512,640]{1,0:T(8,128)(2,1)}, bf16[256,640]{1,0:T(8,128)(2,1)}, f32[768,640]{1,0:T(8,128)}, bf16[768,640]{1,0:T(8,128)(2,1)}, bf16[2304,640]{1,...) custom-call(bf16[640,256]{1,0:T(8,128)(2,1)} %gather_fusion, ...), custom_call_target="tpu_custom_call" | custom-call | tf_op jit(solution)/shard_map/encode/pallas_call | solution.py:405
  201.4 157.0 %decoder.1 = (f32[512,4352]{1,0:T(8,128)}, f32[2048,512]{1,0:T(8,128)}, f32[7,512,128]{2,1,0:T(8,128)}, f32[512,640]{1,0:T(8,128)}, f32[8,128]{1,0:T(8,128)}) custom-call(s32[6]{0:T(128)} %slice.29.shift_ref, s32[640,128]{1,0:T(8,128)} %broadcast_in_dim.25.rvis_ref, bf16[512,640]{1,0:T(8,128)(2,1)} %get-tuple-element.59.gvt_ref, bf16[3072,256]{1,0:T(8,128)(2,1)} %bitcast.97, ...), custom_call_target="tpu_custom_call" | custom-call | tf_op jit(solution)/shard_map/decoder/pallas_call | solution.py:260
  358.3 1.3 slice_reduce_fusion
  359.6 69.8 %encode_back.1 = (f32[768,6656]{1,0:T(8,128)}, f32[3072,768]{1,0:T(8,128)}, f32[256,768]{1,0:T(8,128)}, f32[6,768,128]{2,1,0:T(8,128)}) custom-call(f32[512,640]{1,0:T(8,128)} %get-tuple-element.62.gp_ref, f32[6,768,128]{2,1,0:T(8,128)} %broadcast_in_dim.31.vec_ref, s32[8,640]{1,0:T(8,128)} %broadcast_in_dim.29.seg_ref, bf16[768,6656]{1,0:T(8,128)(2,1)} %bitcast.90, ...), custom_call_target="tpu_custom_call" | custom-call | tf_op jit(solution)/shard_map/encode_back/pallas_call | solution.py:543
  429.4 2.0 reduce_sum.145
  431.5 2.3 reduce_sum.144
  435.2 171.3 %reduce.5 = (f32[2,48,6656]{2,1,0:T(8,128)}, f32[2,32,4352]{2,1,0:T(8,128)}, f32[2,192,768]{2,1,0:T(8,128)}, f32[2,128,512]{2,1,0:T(8,128)}, f32[2,16,768]{2,1,0...) custom-call(f32[4,2,2,48,6656]{4,3,2,1,0:T(8,128)} %bitcast.91, f32[4,2,2,32,4352]{4,3,2,1,0:T(8,128)} %bitcast.96, ...), custom_call_target="tpu_custom_call" | custom-call | tf_op jit(solution)/shard_map/reduce/pallas_call | solution.py:836
  609.0 1.4 slice_bitcast_fusion
  613.9 1.5 copy-done.9
  617.2 1.4 multiply_subtract_fusion.3
  619.7 2.3 multiply_subtract_fusion.2
  622.9 2.4 multiply_subtract_fusion.1
  627.4 4.5 multiply_subtract_fusion
  (99 shorter events, 26.8 us)
Async XLA Ops:
  0.7 11.3 %copy-start = (bf16[3072,256]{1,0:T(8,128)(2,1)S(1)}, bf16[3072,256]{1,0:T(8,128)(2,1)}, u32[]{:S(2)}) copy-start(bf16[3072,256]{1,0:T(8,128)(2,1)} %param.22) | copy-start | bytes 4718596
  15.2 2.4 copy-start.5
  16.9 1.7 copy-start.3
  17.6 2.1 copy-start.1
  435.1 176.6 %copy-start.23 = (f32[1024]{0:T(1024)S(1)}, f32[1024]{0:T(1024)}, u32[]{:S(2)}) copy-start(f32[1024]{0:T(1024)} %param.31) | copy-start | bytes 12292
  435.2 176.6 %copy-start.24 = (f32[1024]{0:T(1024)S(1)}, f32[1024]{0:T(1024)}, u32[]{:S(2)}) copy-start(f32[1024]{0:T(1024)} %param.37) | copy-start | bytes 12292
  435.2 176.6 %copy-start.25 = (f32[1024]{0:T(1024)S(1)}, f32[1024]{0:T(1024)}, u32[]{:S(2)}) copy-start(f32[1024]{0:T(1024)} %param.43) | copy-start | bytes 12292
  606.4 7.2 %copy-start.14 = (f32[2,32,4352]{2,1,0:T(8,128)S(1)}, f32[2,32,4352]{2,1,0:T(8,128)}, u32[]{:S(2)}) copy-start(f32[2,32,4352]{2,1,0:T(8,128)} %get-tuple-element.88) | copy-start | bytes 3342340
  612.4 1.4 copy-start.11
  613.6 1.8 copy-start.9
  615.4 1.0 copy-start.21
  615.4 1.0 copy-start.22
  615.4 1.8 copy-start.10
  615.4 1.8 copy-start.17
  615.4 1.8 copy-start.18
  617.2 1.5 copy-start.6
  617.2 2.1 copy-start.15
  617.2 2.5 copy-start.16
  619.7 2.3 copy-start.4
  619.7 2.5 copy-start.12
  619.7 3.2 copy-start.13
  622.9 2.7 copy-start.2
  622.9 3.8 copy-start.7
  622.9 4.5 copy-start.8
  (2 other events, 1.8 us)

commit v7 on v6

--- a/solution.py
+++ b/solution.py
@@ -358,11 +358,12 @@
         f0 = pl.multiple_of(h * size, size)
         k = jnp.concatenate([qkv[pl.ds(width + f0, size), :], others[...]], axis=0).T
         v = qkv[pl.ds(2 * width + f0, size), :]
-        for i in range(rows // 128):
-            q = jnp.concatenate([qkv[pl.ds(f0, size), lane(i)], own[:, lane(i)]], axis=0)
+        for lo in range(0, rows, 640):
+            at = pl.ds(lo, min(640, rows - lo))
+            q = jnp.concatenate([qkv[pl.ds(f0, size), at], own[:, at]], axis=0)
             p = encoder_scores(q, k, scale)
-            att[pl.ds(f0, size), lane(i)] = mm(v, p.astype(BF16)).astype(BF16)
-    loop(heads, attend, 4)
+            att[pl.ds(f0, size), at] = mm(v, p.astype(BF16)).astype(BF16)
+    loop(heads, attend, 2)
     saves[4].start()
     loads[2].wait()
     res[...] += mm(wi[:, c_out:c_up], att[...], 0, 0)
@@ -509,17 +510,19 @@
         do = att[mine, :]
         keys = jnp.concatenate([k, others[...]], axis=0).T
         values = v.T
-        for i in range(rows // 128):
-            part_q = jnp.concatenate([q[:, 128 * i : 128 * i + 128], own[:, lane(i)]], axis=0)
+        for lo in range(0, rows, 640):
+            at = pl.ds(lo, min(640, rows - lo))
+            hi = min(lo + 640, rows)
+            part_q = jnp.concatenate([q[:, lo:hi], own[:, at]], axis=0)
             p = encoder_scores(part_q, keys, scale)
-            dp = mm(values, do[:, 128 * i : 128 * i + 128])
+            dp = mm(values, do[:, lo:hi])
             ds = p * (dp - jnp.sum(dp * p, axis=0, keepdims=True))
-            probs[:, lane(i)] = p.astype(BF16)
-            dscores[:, lane(i)] = (ds * scale).astype(BF16)
+            probs[:, at] = p.astype(BF16)
+            dscores[:, at] = (ds * scale).astype(BF16)
         dqkv[mine, :] = mm(k, dscores[...]).astype(BF16)
         dqkv[pl.ds(width + f0, size), :] = mm(q, dscores[...], 1, 1).astype(BF16)
         dqkv[pl.ds(2 * width + f0, size), :] = mm(do, probs[...], 1, 1).astype(BF16)
-    loop(heads, attend_back, 3)
+    loop(heads, attend_back, 2)
     for copy in again:
         copy.wait()
     for i in range(3 * width // CHUNK):

time: 643 us -> 639 us (level)
    pallas_call x1, Pallas kernels: 47.5 us -> 33.5 us  [encoder_forward(): pl.pallas_call(functools.partial(encoder_forward_kernel, heads), out_shap...]
    pallas_call x1, Pallas kernels: 157 us -> 169 us  [decoder_step(): pl.pallas_call(functools.partial(decoder_kernel, coef, heads), out_shape=...]
where the time goes in v7:
time: 639 us; the launch traced here: 630 us
  Pallas kernels  559 us (87%)
  other arithmetic  43.1 us (7%)
  local copies, waits for them, and re-layouts  24.2 us (4%)
    pallas_call x1, Pallas kernels, reduce_grads(): pl.pallas_call(functools.partial(reduce_kernel, tuple(widths), n), out_sh...  171 us
    pallas_call x1, Pallas kernels, decoder_step(): pl.pallas_call(functools.partial(decoder_kernel, coef, heads), out_shape=...  169 us
    pallas_call x1, Pallas kernels, gather_weights(): pl.pallas_call(functools.partial(gather_kernel, chunks, n), out_shape=tup...  117 us
    pallas_call x1, Pallas kernels, encoder_backward(): pl.pallas_call(functools.partial(encoder_backward_kernel, heads), out_sha...  68.2 us
    pallas_call x1, Pallas kernels, encoder_forward(): pl.pallas_call(functools.partial(encoder_forward_kernel, heads), out_shap...  33.5 us

profile of v7, /device:TPU:0, one launch (start us, length us, event | category | flops | bytes accessed | tf_op | source)
XLA Modules:
  0.0 630.0 jit_solution(13049687057153364106)
XLA Ops:
  4.0 1.3 reduce-precision_bitcast_fusion.refs_5_
  7.9 1.5 convert_element_type.51
  10.2 1.8 convert_element_type.55
  12.0 3.2 gather_fusion
  20.9 2.3 multiply_sine_fusion.3
  24.4 2.6 gather_fusion.1
  26.9 3.5 multiply_sine_fusion.1
  30.4 1.4 pad_maximum_fusion.pos_ref
  31.8 116.8 %gather.13 = (bf16[4,2,2,16,768]{4,3,2,1,0:T(8,128)(2,1)}, bf16[4,2,2,48,6656]{4,3,2,1,0:T(8,128)(2,1)}, bf16[4,2,2,192,768]{4,3,2,1,0:T(8,128)(2,1)}, bf16[4,2,...) custom-call(bf16[2,16,768]{2,1,0:T(8,128)(2,1)} %bitcast.107, ...), custom_call_target="tpu_custom_call" | custom-call | tf_op jit(solution)/shard_map/gather/pallas_call | solution.py:1014
  150.1 1.8 broadcast_in_dim.36.vec_ref
  151.9 2.0 broadcast_in_dim.31.vec_ref
  153.9 33.5 %encode.1 = (bf16[512,640]{1,0:T(8,128)(2,1)}, bf16[256,640]{1,0:T(8,128)(2,1)}, f32[768,640]{1,0:T(8,128)}, bf16[768,640]{1,0:T(8,128)(2,1)}, bf16[2304,640]{1,...) custom-call(bf16[640,256]{1,0:T(8,128)(2,1)} %gather_fusion, ...), custom_call_target="tpu_custom_call" | custom-call | tf_op jit(solution)/shard_map/encode/pallas_call | solution.py:406
  187.4 169.0 %decoder.1 = (f32[512,4352]{1,0:T(8,128)}, f32[2048,512]{1,0:T(8,128)}, f32[7,512,128]{2,1,0:T(8,128)}, f32[512,640]{1,0:T(8,128)}, f32[8,128]{1,0:T(8,128)}) custom-call(s32[6]{0:T(128)} %slice.29.shift_ref, s32[640,128]{1,0:T(8,128)} %broadcast_in_dim.25.rvis_ref, bf16[512,640]{1,0:T(8,128)(2,1)} %get-tuple-element.59.gvt_ref, bf16[3072,256]{1,0:T(8,128)(2,1)} %bitcast.97, ...), custom_call_target="tpu_custom_call" | custom-call | tf_op jit(solution)/shard_map/decoder/pallas_call | solution.py:260
  356.5 1.3 slice_reduce_fusion
  357.8 68.2 %encode_back.1 = (f32[768,6656]{1,0:T(8,128)}, f32[3072,768]{1,0:T(8,128)}, f32[256,768]{1,0:T(8,128)}, f32[6,768,128]{2,1,0:T(8,128)}) custom-call(f32[512,640]{1,0:T(8,128)} %get-tuple-element.62.gp_ref, f32[6,768,128]{2,1,0:T(8,128)} %broadcast_in_dim.31.vec_ref, s32[8,640]{1,0:T(8,128)} %broadcast_in_dim.29.seg_ref, bf16[768,6656]{1,0:T(8,128)(2,1)} %bitcast.90, ...), custom_call_target="tpu_custom_call" | custom-call | tf_op jit(solution)/shard_map/encode_back/pallas_call | solution.py:546
  426.0 2.0 reduce_sum.145
  428.0 2.3 reduce_sum.144
  431.7 171.3 %reduce.5 = (f32[2,48,6656]{2,1,0:T(8,128)}, f32[2,32,4352]{2,1,0:T(8,128)}, f32[2,192,768]{2,1,0:T(8,128)}, f32[2,128,512]{2,1,0:T(8,128)}, f32[2,16,768]{2,1,0...) custom-call(f32[4,2,2,48,6656]{4,3,2,1,0:T(8,128)} %bitcast.91, f32[4,2,2,32,4352]{4,3,2,1,0:T(8,128)} %bitcast.96, ...), custom_call_target="tpu_custom_call" | custom-call | tf_op jit(solution)/shard_map/reduce/pallas_call | solution.py:839
  605.5 1.4 slice_bitcast_fusion
  610.4 1.5 copy-done.9
  613.7 1.4 multiply_subtract_fusion.3
  616.2 2.3 multiply_subtract_fusion.2
  619.4 2.4 multiply_subtract_fusion.1
  623.9 4.5 multiply_subtract_fusion
  (99 shorter events, 26.8 us)
Async XLA Ops:
  0.7 11.3 %copy-start = (bf16[3072,256]{1,0:T(8,128)(2,1)S(1)}, bf16[3072,256]{1,0:T(8,128)(2,1)}, u32[]{:S(2)}) copy-start(bf16[3072,256]{1,0:T(8,128)(2,1)} %param.22) | copy-start | bytes 4718596
  15.2 2.4 copy-start.5
  16.9 1.7 copy-start.3
  17.6 2.1 copy-start.1
  431.7 176.6 %copy-start.23 = (f32[1024]{0:T(1024)S(1)}, f32[1024]{0:T(1024)}, u32[]{:S(2)}) copy-start(f32[1024]{0:T(1024)} %param.31) | copy-start | bytes 12292
  431.7 176.6 %copy-start.24 = (f32[1024]{0:T(1024)S(1)}, f32[1024]{0:T(1024)}, u32[]{:S(2)}) copy-start(f32[1024]{0:T(1024)} %param.37) | copy-start | bytes 12292
  431.7 176.6 %copy-start.25 = (f32[1024]{0:T(1024)S(1)}, f32[1024]{0:T(1024)}, u32[]{:S(2)}) copy-start(f32[1024]{0:T(1024)} %param.43) | copy-start | bytes 12292
  602.9 7.2 %copy-start.14 = (f32[2,32,4352]{2,1,0:T(8,128)S(1)}, f32[2,32,4352]{2,1,0:T(8,128)}, u32[]{:S(2)}) copy-start(f32[2,32,4352]{2,1,0:T(8,128)} %get-tuple-element.88) | copy-start | bytes 3342340
  608.9 1.4 copy-start.11
  610.1 1.8 copy-start.9
  611.9 1.0 copy-start.21
  611.9 1.0 copy-start.22
  611.9 1.8 copy-start.10
  611.9 1.8 copy-start.17
  611.9 1.8 copy-start.18
  613.7 1.5 copy-start.6
  613.7 2.1 copy-start.15
  613.7 2.5 copy-start.16
  616.2 2.3 copy-start.4
  616.2 2.5 copy-start.12
  616.2 3.2 copy-start.13
  619.4 2.7 copy-start.2
  619.4 3.8 copy-start.7
  619.4 4.5 copy-start.8
  (2 other events, 1.8 us)

commit v8 on v7

--- a/solution.py
+++ b/solution.py
@@ -234,7 +234,7 @@
             dqkv[pl.ds(f0, 128), at] = mm(wide(k, 128 * per) * hm[...], tall).astype(BF16)
             dqkv[pl.ds(width + f0, 128), at] = mm(wide(q, 128 * per) * hm[...], ds_all, 1, 1).astype(BF16)
             dqkv[pl.ds(2 * width + f0, 128), at] = mm(do_all, p_all, 1, 1).astype(BF16)
-        loop(rows // 128 * groups, attend_back, 8)
+        loop(rows // 128 * groups, attend_back, 16)
 
         def qkv_back(i):
             part = pl.ds(pl.multiple_of(i * chunk, chunk), chunk)
@@ -363,7 +363,7 @@
             q = jnp.concatenate([qkv[pl.ds(f0, size), at], own[:, at]], axis=0)
             p = encoder_scores(q, k, scale)
             att[pl.ds(f0, size), at] = mm(v, p.astype(BF16)).astype(BF16)
-    loop(heads, attend, 2)
+    loop(heads, attend, 3)
     saves[4].start()
     loads[2].wait()
     res[...] += mm(wi[:, c_out:c_up], att[...], 0, 0)

time: 639 us -> 626 us (0.980)
  Pallas kernels: 559 us -> 545 us
    pallas_call x1, Pallas kernels: 169 us -> 156 us  [decoder_step(): pl.pallas_call(functools.partial(decoder_kernel, coef, heads), out_shape=...]
where the time goes in v8:
time: 626 us; the launch traced here: 617 us
  Pallas kernels  545 us (87%)
  other arithmetic  43.1 us (7%)
  local copies, waits for them, and re-layouts  24.1 us (4%)
    pallas_call x1, Pallas kernels, reduce_grads(): pl.pallas_call(functools.partial(reduce_kernel, tuple(widths), n), out_sh...  171 us
    pallas_call x1, Pallas kernels, decoder_step(): pl.pallas_call(functools.partial(decoder_kernel, coef, heads), out_shape=...  156 us
    pallas_call x1, Pallas kernels, gather_weights(): pl.pallas_call(functools.partial(gather_kernel, chunks, n), out_shape=tup...  117 us
    pallas_call x1, Pallas kernels, encoder_backward(): pl.pallas_call(functools.partial(encoder_backward_kernel, heads), out_sha...  68.2 us
    pallas_call x1, Pallas kernels, encoder_forward(): pl.pallas_call(functools.partial(encoder_forward_kernel, heads), out_shap...  33.6 us

profile of v8, /device:TPU:0, one launch (start us, length us, event | category | flops | bytes accessed | tf_op | source)
XLA Modules:
  0.0 616.5 jit_solution(11333773730018089733)
XLA Ops:
  4.0 1.3 reduce-precision_bitcast_fusion.refs_5_
  7.9 1.5 convert_element_type.51
  10.2 1.8 convert_element_type.55
  12.0 3.2 gather_fusion
  20.9 2.3 multiply_sine_fusion.3
  24.4 2.6 gather_fusion.1
  26.9 3.5 multiply_sine_fusion.1
  30.4 1.4 pad_maximum_fusion.pos_ref
  31.8 116.8 %gather.13 = (bf16[4,2,2,16,768]{4,3,2,1,0:T(8,128)(2,1)}, bf16[4,2,2,48,6656]{4,3,2,1,0:T(8,128)(2,1)}, bf16[4,2,2,192,768]{4,3,2,1,0:T(8,128)(2,1)}, bf16[4,2,...) custom-call(bf16[2,16,768]{2,1,0:T(8,128)(2,1)} %bitcast.107, ...), custom_call_target="tpu_custom_call" | custom-call | tf_op jit(solution)/shard_map/gather/pallas_call | solution.py:1014
  150.1 1.8 broadcast_in_dim.36.vec_ref
  151.9 2.0 broadcast_in_dim.31.vec_ref
  153.8 33.6 %encode.1 = (bf16[512,640]{1,0:T(8,128)(2,1)}, bf16[256,640]{1,0:T(8,128)(2,1)}, f32[768,640]{1,0:T(8,128)}, bf16[768,640]{1,0:T(8,128)(2,1)}, bf16[2304,640]{1,...) custom-call(bf16[640,256]{1,0:T(8,128)(2,1)} %gather_fusion, ...), custom_call_target="tpu_custom_call" | custom-call | tf_op jit(solution)/shard_map/encode/pallas_call | solution.py:406
  187.4 155.6 %decoder.1 = (f32[512,4352]{1,0:T(8,128)}, f32[2048,512]{1,0:T(8,128)}, f32[7,512,128]{2,1,0:T(8,128)}, f32[512,640]{1,0:T(8,128)}, f32[8,128]{1,0:T(8,128)}) custom-call(s32[6]{0:T(128)} %slice.29.shift_ref, s32[640,128]{1,0:T(8,128)} %broadcast_in_dim.25.rvis_ref, bf16[512,640]{1,0:T(8,128)(2,1)} %get-tuple-element.59.gvt_ref, bf16[3072,256]{1,0:T(8,128)(2,1)} %bitcast.97, ...), custom_call_target="tpu_custom_call" | custom-call | tf_op jit(solution)/shard_map/decoder/pallas_call | solution.py:260
  343.0 1.3 slice_reduce_fusion
  344.3 68.2 %encode_back.1 = (f32[768,6656]{1,0:T(8,128)}, f32[3072,768]{1,0:T(8,128)}, f32[256,768]{1,0:T(8,128)}, f32[6,768,128]{2,1,0:T(8,128)}) custom-call(f32[512,640]{1,0:T(8,128)} %get-tuple-element.62.gp_ref, f32[6,768,128]{2,1,0:T(8,128)} %broadcast_in_dim.31.vec_ref, s32[8,640]{1,0:T(8,128)} %broadcast_in_dim.29.seg_ref, bf16[768,6656]{1,0:T(8,128)(2,1)} %bitcast.90, ...), custom_call_target="tpu_custom_call" | custom-call | tf_op jit(solution)/shard_map/encode_back/pallas_call | solution.py:546
  412.5 2.0 reduce_sum.145
  414.6 2.3 reduce_sum.144
  418.2 171.2 %reduce.5 = (f32[2,48,6656]{2,1,0:T(8,128)}, f32[2,32,4352]{2,1,0:T(8,128)}, f32[2,192,768]{2,1,0:T(8,128)}, f32[2,128,512]{2,1,0:T(8,128)}, f32[2,16,768]{2,1,0...) custom-call(f32[4,2,2,48,6656]{4,3,2,1,0:T(8,128)} %bitcast.91, f32[4,2,2,32,4352]{4,3,2,1,0:T(8,128)} %bitcast.96, ...), custom_call_target="tpu_custom_call" | custom-call | tf_op jit(solution)/shard_map/reduce/pallas_call | solution.py:839
  592.1 1.4 slice_bitcast_fusion
  597.0 1.5 copy-done.9
  600.3 1.4 multiply_subtract_fusion.3
  602.7 2.3 multiply_subtract_fusion.2
  605.9 2.4 multiply_subtract_fusion.1
  610.5 4.5 multiply_subtract_fusion
  (99 shorter events, 26.8 us)
Async XLA Ops:
  0.7 11.3 %copy-start = (bf16[3072,256]{1,0:T(8,128)(2,1)S(1)}, bf16[3072,256]{1,0:T(8,128)(2,1)}, u32[]{:S(2)}) copy-start(bf16[3072,256]{1,0:T(8,128)(2,1)} %param.22) | copy-start | bytes 4718596
  15.2 2.4 copy-start.5
  16.9 1.7 copy-start.3
  17.6 2.1 copy-start.1
  418.2 176.6 %copy-start.23 = (f32[1024]{0:T(1024)S(1)}, f32[1024]{0:T(1024)}, u32[]{:S(2)}) copy-start(f32[1024]{0:T(1024)} %param.31) | copy-start | bytes 12292
  418.2 176.6 %copy-start.24 = (f32[1024]{0:T(1024)S(1)}, f32[1024]{0:T(1024)}, u32[]{:S(2)}) copy-start(f32[1024]{0:T(1024)} %param.37) | copy-start | bytes 12292
  418.2 176.6 %copy-start.25 = (f32[1024]{0:T(1024)S(1)}, f32[1024]{0:T(1024)}, u32[]{:S(2)}) copy-start(f32[1024]{0:T(1024)} %param.43) | copy-start | bytes 12292
  589.5 7.2 %copy-start.14 = (f32[2,32,4352]{2,1,0:T(8,128)S(1)}, f32[2,32,4352]{2,1,0:T(8,128)}, u32[]{:S(2)}) copy-start(f32[2,32,4352]{2,1,0:T(8,128)} %get-tuple-element.88) | copy-start | bytes 3342340
  595.5 1.4 copy-start.11
  596.7 1.8 copy-start.9
  598.5 1.0 copy-start.21
  598.5 1.0 copy-start.22
  598.5 1.8 copy-start.10
  598.5 1.8 copy-start.17
  598.5 1.8 copy-start.18
  600.2 1.5 copy-start.6
  600.3 2.1 copy-start.15
  600.3 2.5 copy-start.16
  602.7 2.3 copy-start.4
  602.7 2.5 copy-start.12
  602.7 3.2 copy-start.13
  605.9 2.7 copy-start.2
  605.9 3.8 copy-start.7
  605.9 4.5 copy-start.8
  (2 other events, 1.8 us)
